TPU v7x, 32 devices: a whole 2x2x4 slice. The times are simulated.
32 devices in a mesh: grid: 8 (over z, y), bundle: 4 (over x, core).
Axes of the slice: x: 2, y: 2, z: 4, core: 2. Of those that a mesh axis runs over, the one named last changes fastest.
Arguments:
- cell_state: float32 [24, 32768], P(None, 'grid'), may hold values from -6 to 6
- pore_volume: float32 [32768], P('grid'), may hold values from 0.5 to 5
- request_cell: int32 [4, 8, 8, 32], P(None, 'grid'), may hold values from 0 to 4095, as said below
- node_slot: int32 [4, 16, 2048], P('bundle', 'grid'), may hold values from 0 to 255, as said below
- line_length: int32 [4, 16], P('bundle', 'grid'), may hold values from 128 to 2048, as said below
- courant: float32 [4, 16, 2048], P('bundle', 'grid'), may hold values from 0.3 to 3
- flux_weight: float32 [4, 16, 2048], P('bundle', 'grid'), may hold values from 0.3 to 3
- inflow: float32 [4, 24], P('bundle'), may hold values from -4 to 4
- interaction: float32 [24, 24], replicated, may hold values from -0.18 to 0.18
Outputs:
- new_state: float32 [24, 32768], P(None, 'grid')
Inputs may be any that keep to these rules, and one draw needn't show every extreme that they name: `request_cell`: a cell owner's local cell index; one entry is the last cell. `node_slot`: an index into the 256 slots of the device that holds the streamline, slot o * 32 + c belonging to owner o; the last slot is used. `line_length`: live nodes come first on each streamline; some streamline has 2048 and some has 128.
All inputs are finite; a program needn't handle non-finite values.
Results may differ from a plain program's by a relative error of at most 0.0001.
Values sent between devices are 32-bit elements; how exact they have to be, the bound alone decides.
No kernel may reach another device: no remote copies, remote signals or barrier semaphores. Data moves between devices by JAX's collectives and lax.ppermute only.
A program may use at most 64 MiB of HBM per device.

v0:
```python
import jax
import jax.numpy as jnp
from jax import lax
from jax.sharding import PartitionSpec as P

SUB = 2
NEWTON = 3


def combine(earlier, later):
    return (earlier[0] * later[0], later[0] * earlier[1] + later[1])


def transport(state, rate, entry):
    decay = rate / (1.0 + rate)
    source = state / (1.0 + rate)
    source = source.at[:, :, 0].add(decay[None, :, 0] * entry[:, None])
    decay_full = jnp.broadcast_to(decay[None, :, :], source.shape)
    scanned = lax.associative_scan(combine, (decay_full, source), axis=2)
    return scanned[1]


def speciate(base, interaction):
    iterate = base
    for step in range(NEWTON):
        iterate = base - jnp.dot(interaction, jnp.tanh(iterate), precision=lax.Precision.HIGHEST)
    return iterate


def shards(
    cell_state,
    pore_volume,
    request_cell,
    node_slot,
    line_length,
    courant,
    flux_weight,
    inflow,
    interaction,
):
    species = cell_state.shape[0]
    local_cells = cell_state.shape[1]
    all_requests = request_cell[:, 0]
    request = lax.dynamic_index_in_dim(all_requests, lax.axis_index("bundle"), 0, keepdims=False)
    owners = request.shape[0]
    capacity = request.shape[1]
    flat_request = request.reshape(-1)
    picked = jnp.take(cell_state, flat_request, axis=1)
    outgoing = picked.T.reshape(owners, capacity * species)
    received = lax.all_to_all(outgoing, "grid", split_axis=0, concat_axis=0, tiled=True)
    slot_table = received.reshape(owners * capacity, species)
    slot_ids = node_slot[0]
    lines_here = slot_ids.shape[0]
    node_count = slot_ids.shape[1]
    state_now = jnp.transpose(jnp.take(slot_table, slot_ids, axis=0), (2, 0, 1))
    for substep in range(SUB):
        state_now = transport(state_now, courant[0], inflow[0])
    result = speciate(state_now.reshape(species, lines_here * node_count), interaction)
    positions = lax.broadcasted_iota(jnp.int32, slot_ids.shape, 1)
    live_mask = positions < line_length[0][:, None]
    weight = jnp.where(live_mask, flux_weight[0], 0.0).reshape(-1)
    flat_slots = slot_ids.reshape(-1)
    slot_sum = (
        jnp.zeros((species, owners * capacity), jnp.float32)
        .at[:, flat_slots]
        .add(result * weight[None, :])
    )
    slot_flux = jnp.zeros((owners * capacity,), jnp.float32).at[flat_slots].add(weight)
    back_sum, back_flux = (
        lax.all_to_all(
            slot_sum.T.reshape(owners, capacity * species),
            "grid",
            split_axis=0,
            concat_axis=0,
            tiled=True,
        ),
        lax.all_to_all(
            slot_flux.reshape(owners, capacity), "grid", split_axis=0, concat_axis=0, tiled=True
        ),
    )
    pore_row = pore_volume[None, :]
    every_sum, every_flux = (
        lax.all_gather(back_sum, "bundle", axis=0, tiled=True),
        lax.all_gather(back_flux, "bundle", axis=0, tiled=True),
    )
    every_request = all_requests.reshape(-1)
    total_sum = (
        jnp.zeros((local_cells, species), jnp.float32)
        .at[every_request]
        .add(every_sum.reshape(-1, species))
        .T
    )
    total_flux = (
        jnp.zeros((local_cells,), jnp.float32)
        .at[every_request]
        .add(every_flux.reshape(-1))[None, :]
    )
    return (pore_row * cell_state + total_sum) / (pore_row + total_flux)


def solution(mesh):
    placed = (
        P(None, "grid"),
        P("grid"),
        P(None, "grid", None, None),
        P("bundle", "grid", None),
        P("bundle", "grid"),
        P("bundle", "grid", None),
        P("bundle", "grid", None),
        P("bundle", None),
        P(),
    )
    return jax.shard_map(
        shards, mesh=mesh, in_specs=placed, out_specs=P(None, "grid"), check_vma=False
    )
```

profile of v0, /device:TPU:0, one launch (start us, length us, event | category | flops | bytes accessed | tf_op | source)
XLA Modules:
  0.0 187.7 jit_solution(15135792047870095880)
XLA Ops:
  0.0 0.7 constant_dynamic-slice_fusion
  0.9 1.6 copy.69
  2.6 0.7 gather_fusion
  3.4 0.7 all_to_all.30
  4.2 7.3 %all-to-all-start = ((f32[8,1,768]{2,1,0:T(1,128)}), f32[8,1,768]{2,1,0:T(1,128)S(1)}, u32[]{:S(2)}, u32[]{:S(2)}) async-start(f32[8,1,768]{2,1,0:T(1,128)} %all_to_all.30), calls=%async_computation | async-start | bytes 49152 | tf_op jit(solution)/shard_map/all_to_all | solution.py:50
  11.5 0.4 slice.531
  11.9 0.4 slice.535
  12.3 0.2 slice.537
  12.5 0.2 slice.541
  13.0 0.2 slice.547
  13.2 0.2 slice.549
  13.4 0.2 slice.553
  16.5 0.2 slice.548
  16.7 0.2 slice.542
  16.9 0.2 slice.536
  17.2 0.4 slice.530
  17.5 28.8 %scatter_custom_fusion.2 = f32[256]{0:T(256)S(1)} fusion(s32[4096]{0:T(1024)S(1)} %bitcast.76, f32[4096]{0:T(1024)S(1)} %broadcast_select_fusion.1, f32[]{:T(128)} %constant.88.clone.1), kind=kCustom, calls=%fused_computation.136 | custom fusion | flops 4096 | bytes 1028 | tf_op jit(solution)/shard_map/scatter-add | solution.py:68
  46.3 0.7 all_to_all.27
  47.0 6.0 %all-to-all-start.2 = ((f32[8,1,32]{2,1,0:T(1,128)}), f32[8,1,32]{2,1,0:T(1,128)S(1)}, u32[]{:S(2)}, u32[]{:S(2)}) async-start(f32[8,1,32]{2,1,0:T(1,128)} %all_to_all.27), calls=%async_computation.2 | async-start | bytes 8192 | tf_op jit(solution)/shard_map/all_to_all | solution.py:77
  53.2 14.1 %gather_fusion.1 = f32[4096,24]{1,0:T(8,128)} fusion(f32[256,24]{1,0:T(8,128)S(1)} %reshape.296, s32[4096]{0:T(1024)S(1)} %broadcast_clamp_fusion), kind=kCustom, calls=%fused_computation.1 | custom fusion | bytes 802816 | tf_op jit(solution)/shard_map/jit(_take)/gather | solution.py:55
  67.2 3.2 %divide_bitcast_fusion = f32[24,2,2048]{0,2,1:T(8,128)S(1)} fusion(f32[2,2048,24]{2,1,0:T(8,128)} %bitcast.66, f32[2,2048]{1,0:T(2,128)S(1)} %get-tuple-element.30, pred[2,2048]{1,0:T(4,128)(4,1)S(1)} %compare_and_fusion), kind=kLoop, calls=%fused_computation.17 | loop fusion | flops 196608 | bytes 806912 | tf_op jit(solution)/shard_map/div | solution.py:16
  70.6 3.6 %slice.613 = f32[24,2,1023]{0,2,1:T(8,128)} slice(f32[24,2,2048]{0,2,1:T(8,128)S(1)} %scatter-add.38), slice={[0:24:1], [0:2:1], [2:2048:2]} | slice | bytes 392832 | tf_op jit(solution)/shard_map/slice | solution.py:19
  74.2 1.3 slice.533
  75.6 3.6 %slice.532 = f32[24,2,1024]{0,2,1:T(8,128)} slice(f32[24,2,2048]{0,2,1:T(8,128)S(1)} %scatter-add.38), slice={[0:24:1], [0:2:1], [0:2047:2]} | slice | bytes 393216 | tf_op jit(solution)/shard_map/slice | solution.py:19
  79.2 1.6 multiply_add_fusion.1
  80.8 0.8 slice.539
  81.5 0.8 slice.538
  84.2 0.8 slice.611
  87.6 1.1 copy-done.2
  88.7 0.4 fusion.8
  89.2 3.4 %pad.158 = f32[24,2,2048]{0,2,1:T(8,128)} pad(f32[24,2,1024]{0,2,1:T(8,128)S(1)} %pad_maximum_fusion, f32[]{:T(128)} %constant.88.clone.1), padding=0_0_0x0_0_0x0_1_1 | pad | bytes 589828 | tf_op jit(solution)/shard_map/pad | solution.py:19
  92.6 3.4 %pad.159 = f32[24,2,2048]{0,2,1:T(8,128)} pad(f32[24,2,1024]{0,2,1:T(8,128)S(1)} %add.429, f32[]{:T(128)} %constant.88.clone.1), padding=0_0_0x0_0_0x1_0_1 | pad | bytes 589828 | tf_op jit(solution)/shard_map/pad | solution.py:19
  96.0 2.5 %add_divide_fusion = f32[24,2,2048]{0,2,1:T(8,128)S(1)} fusion(f32[24,2,2048]{0,2,1:T(8,128)} %pad.158, f32[24,2,2048]{0,2,1:T(8,128)} %pad.159, f32[2,2048]{1,0:T(2,128)S(1)} %get-tuple-element.30), kind=kLoop, calls=%fused_computation.16 | loop fusion | flops 196608 | bytes 1196032 | tf_op jit(solution)/shard_map/div | solution.py:16
  98.8 3.7 %slice.665 = f32[24,2,1023]{0,2,1:T(8,128)} slice(f32[24,2,2048]{0,2,1:T(8,128)S(1)} %scatter-add.39), slice={[0:24:1], [0:2:1], [2:2048:2]} | slice | bytes 392832 | tf_op jit(solution)/shard_map/slice | solution.py:19
  102.5 1.3 slice.616
  103.8 3.6 %slice.615 = f32[24,2,1024]{0,2,1:T(8,128)} slice(f32[24,2,2048]{0,2,1:T(8,128)S(1)} %scatter-add.39), slice={[0:24:1], [0:2:1], [0:2047:2]} | slice | bytes 393216 | tf_op jit(solution)/shard_map/slice | solution.py:19
  107.5 1.6 multiply_add_fusion
  109.0 0.8 slice.619
  109.8 0.8 slice.618
  112.6 0.8 slice.663
  115.8 1.1 copy-done.1
  116.9 0.4 fusion.7
  117.3 1.1 pad_maximum_fusion.1
  118.4 2.3 %pad.180 = f32[24,2,2048]{0,2,1:T(8,128)S(1)} pad(f32[24,2,1024]{0,2,1:T(8,128)} %pad_maximum_fusion.1, f32[]{:T(128)} %constant.88.clone.1), padding=0_0_0x0_0_0x0_1_1 | pad | bytes 589828 | tf_op jit(solution)/shard_map/pad | solution.py:19
  120.7 3.4 %pad.181 = f32[24,2,2048]{0,2,1:T(8,128)} pad(f32[24,2,1024]{0,2,1:T(8,128)S(1)} %add.462, f32[]{:T(128)} %constant.88.clone.1), padding=0_0_0x0_0_0x1_0_1 | pad | bytes 589828 | tf_op jit(solution)/shard_map/pad | solution.py:19
  124.1 3.3 %add.464 = f32[24,2,2048]{0,2,1:T(8,128)} add(f32[24,2,2048]{0,2,1:T(8,128)S(1)} %pad.180, f32[24,2,2048]{0,2,1:T(8,128)} %pad.181) | non-fusion elementwise | flops 98304 | bytes 1179648 | tf_op jit(solution)/shard_map/add | solution.py:19
  127.5 2.2 %copy.75 = f32[24,4096]{1,0:T(8,128)S(1)} copy(f32[24,4096]{0,1:T(8,128)} %bitcast.65) | data formatting | bytes 786432 | tf_op jit(solution)/shard_map/reshape | solution.py:58
  129.7 0.5 fusion.6
  130.2 0.5 fusion.4
  130.7 0.5 fusion.2
  131.1 0.6 copy.72
  131.7 22.4 %scatter_custom_fusion = f32[24,256]{0,1:T(8,128)S(1)} fusion(s32[4096]{0:T(1024)S(1)} %bitcast.77, f32[4096,24]{1,0:T(8,128)S(1)} %copy.72, f32[]{:T(128)} %constant.88.clone.1), kind=kCustom, calls=%fused_computation.65 | custom fusion | flops 98304 | bytes 24580 | tf_op jit(solution)/shard_map/scatter-add | solution.py:66
  154.1 0.7 all_to_all.31
  154.9 6.0 %all-to-all-start.1 = ((f32[8,1,768]{2,1,0:T(1,128)}), f32[8,1,768]{2,1,0:T(1,128)S(1)}, u32[]{:S(2)}, u32[]{:S(2)}) async-start(f32[8,1,768]{2,1,0:T(1,128)} %all_to_all.31), calls=%async_computation.1 | async-start | bytes 49152 | tf_op jit(solution)/shard_map/all_to_all | solution.py:70
  160.9 5.2 %all-gather.1 = f32[32,1,32]{2,1,0:T(1,128)S(1)} all-gather(f32[8,1,32]{2,1,0:T(1,128)S(1)} %all-to-all-done.2), channel_id=3, replica_groups=mesh['grid'=8,'bundle'=4] {'bundle'}, dimensions={0}, use_global_device_ids=true | all-gather | bytes 5120 | tf_op jit(solution)/shard_map/all_gather | solution.py:84
  166.1 0.6 broadcast.361
  166.7 0.7 reduce.15
  167.5 6.0 %scatter_fusion = f32[4096]{0:T(1024)S(1)} fusion(f32[4096]{0:T(1024)S(1)} %copy.81, s32[1024]{0:T(1024)S(1)} %bitcast.72, f32[1024]{0:T(1024)S(1)} %reshape.344), kind=kCustom, calls=%fused_computation.5 | custom fusion | flops 1024 | bytes 16384 | tf_op jit(solution)/shard_map/scatter-add | solution.py:96
  173.6 5.6 %all-gather = f32[32,1,768]{2,1,0:T(1,128)S(1)} all-gather(f32[8,1,768]{2,1,0:T(1,128)S(1)} %all-to-all-done.1), channel_id=2, replica_groups=mesh['grid'=8,'bundle'=4] {'bundle'}, dimensions={0}, use_global_device_ids=true | all-gather | bytes 122880 | tf_op jit(solution)/shard_map/all_gather | solution.py:83
  179.1 0.2 reduce.8
  179.4 0.4 reshape.328
  179.8 6.5 %scatter_custom_fusion.1 = f32[4096,24]{1,0:T(8,128)S(1)} fusion(s32[1024]{0:T(1024)S(1)} %bitcast.73, f32[1024,24]{1,0:T(8,128)S(1)} %reshape.328, f32[]{:T(128)} %constant.88.clone.1), kind=kCustom, calls=%fused_computation.26 | custom fusion | flops 24576 | bytes 393220 | tf_op jit(solution)/shard_map/scatter-add | solution.py:90
  186.3 0.6 copy.74
  186.9 0.8 fusion.13
  (256 shorter events, 12.3 us)
Async XLA Ops:
  0.0 129.7 %copy-start = (f32[24,24]{1,0:T(8,128)S(1)}, f32[24,24]{1,0:T(8,128)}, u32[]{:S(2)}) copy-start(f32[24,24]{1,0:T(8,128)} %param.21) | copy-start | bytes 6916
  0.0 15.8 %copy-start.6 = (s32[4,1,8,32]{3,2,1,0:T(8,128)S(1)}, s32[4,1,8,32]{3,2,1,0:T(8,128)}, u32[]{:S(2)}) copy-start(s32[4,1,8,32]{3,2,1,0:T(8,128)} %param.15) | copy-start | bytes 12292
  0.0 11.4 %copy-start.4 = (s32[1,2,2048]{2,1,0:T(2,128)S(1)}, s32[1,2,2048]{2,1,0:T(2,128)}, u32[]{:S(2)}) copy-start(s32[1,2,2048]{2,1,0:T(2,128)} %param.16) | copy-start | bytes 49156
  0.0 11.5 %copy-start.7 = (f32[1,2,2048]{2,1,0:T(2,128)S(1)}, f32[1,2,2048]{2,1,0:T(2,128)}, u32[]{:S(2)}) copy-start(f32[1,2,2048]{2,1,0:T(2,128)} %param.18) | copy-start | bytes 49156
  0.0 15.5 %copy-start.10 = (s32[1,2]{1,0:T(1,128)S(1)}, s32[1,2]{1,0:T(1,128)}, u32[]{:S(2)}) copy-start(s32[1,2]{1,0:T(1,128)} %param.17) | copy-start | bytes 28
  0.0 15.6 %copy-start.8 = (f32[1,2,2048]{2,1,0:T(2,128)S(1)}, f32[1,2,2048]{2,1,0:T(2,128)}, u32[]{:S(2)}) copy-start(f32[1,2,2048]{2,1,0:T(2,128)} %param.19) | copy-start | bytes 49156
  4.2 42.8 %all-to-all-start = ((f32[8,1,768]{2,1,0:T(1,128)}), f32[8,1,768]{2,1,0:T(1,128)S(1)}, u32[]{:S(2)}, u32[]{:S(2)}) async-start(f32[8,1,768]{2,1,0:T(1,128)} %all_to_all.30), calls=%async_computation | async-start | bytes 49152 | tf_op jit(solution)/shard_map/all_to_all | solution.py:50
  47.0 107.9 %all-to-all-start.2 = ((f32[8,1,32]{2,1,0:T(1,128)}), f32[8,1,32]{2,1,0:T(1,128)S(1)}, u32[]{:S(2)}, u32[]{:S(2)}) async-start(f32[8,1,32]{2,1,0:T(1,128)} %all_to_all.27), calls=%async_computation.2 | async-start | bytes 8192 | tf_op jit(solution)/shard_map/all_to_all | solution.py:77
  67.2 3.2 %copy-start.9 = (f32[1,24]{1,0:T(1,128)S(1)}, f32[1,24]{1,0:T(1,128)}, u32[]{:S(2)}) copy-start(f32[1,24]{1,0:T(1,128)} %param.20) | copy-start | bytes 292
  87.5 1.2 copy-start.2
  115.7 1.2 copy-start.1
  130.6 30.2 %copy-start.5 = (f32[4096]{0:T(1024)S(1)}, f32[4096]{0:T(1024)}, u32[]{:S(2)}) copy-start(f32[4096]{0:T(1024)} %param.14) | copy-start | bytes 49156
  154.9 18.7 %all-to-all-start.1 = ((f32[8,1,768]{2,1,0:T(1,128)}), f32[8,1,768]{2,1,0:T(1,128)S(1)}, u32[]{:S(2)}, u32[]{:S(2)}) async-start(f32[8,1,768]{2,1,0:T(1,128)} %all_to_all.31), calls=%async_computation.1 | async-start | bytes 49152 | tf_op jit(solution)/shard_map/all_to_all | solution.py:70
  179.7 7.1 %copy-start.3 = (f32[24,4096]{1,0:T(8,128)S(1)}, f32[24,4096]{1,0:T(8,128)}, u32[]{:S(2)}) copy-start(f32[24,4096]{1,0:T(8,128)} %param.13) | copy-start | bytes 1179652
where the time goes:
time: 188 us
  other arithmetic  84.9 us (45%)
  local copies, waits for them, and re-layouts  70 us (37%)
  starting transfers between devices  19.3 us (10%)
  blocking collectives  10.7 us (6%)
    slice x105, local copies, waits for them, and re-layouts, transport(): scanned = lax.associative_scan(combine, (decay_full, source), axis=2)  29.1 us
    scatter-add x1, other arithmetic, shards(): jnp.zeros((owners * capacity,), jnp.float32).at[flat_slots].add(weight)  28.8 us
    scatter-add x1, other arithmetic, shards(): slot_sum = jnp.zeros((species, owners * capacity), jnp.float32).at[:, fla...  22.4 us
    pad x40, local copies, waits for them, and re-layouts, transport(): scanned = lax.associative_scan(combine, (decay_full, source), axis=2)  14.4 us
    gather x1, local copies, waits for them, and re-layouts, shards(): state_now = jnp.transpose(jnp.take(slot_table, slot_ids, axis=0), (2, 0, 1))  14.1 us
    add x40, other arithmetic, combine(): return (earlier[0] * later[0], later[0] * earlier[1] + later[1])  7.41 us
    all_to_all x1, starting transfers between devices, shards(): lax.all_to_all(outgoing, 'grid', split_axis=0, concat_axis=0, tiled=True)  7.28 us
    scatter-add x1, other arithmetic, shards(): total_sum = jnp.zeros((local_cells, species), jnp.float32).at[every_reque...  6.53 us
  transfers between devices with their start and end apart: 3, of which 0 were waited for; matrix products, arithmetic and copies ran while one was open for 75% of the time, Pallas kernels for 0%

commit v1 on v0

v1 whole, which is shorter than its diff:
```python
import functools

import jax
import jax.numpy as jnp
from jax import lax
from jax.experimental import pallas as pl
from jax.experimental.pallas import tpu as pltpu
from jax.sharding import PartitionSpec as P

SUB = 2
NEWTON = 3
LANES = 128
ROWS = 8
F32 = jnp.float32
BF16 = jnp.bfloat16
VMEM_BYTES = 32 * 1024 * 1024


def repeat_steps(count, body, carry):
    if count == 1:
        return body(0, carry)
    return lax.fori_loop(0, count, body, carry)


def split(value):
    high = value.astype(BF16)
    low = (value - high.astype(F32)).astype(BF16)
    return high, low


def exchange_groups(tiles, cap):
    tiles = list(tiles)
    lane_group = lax.broadcasted_iota(jnp.int32, tiles[0].shape, 1) // cap
    step = 1
    while step < len(tiles):
        keep = (lane_group & step) == 0
        for i in range(len(tiles)):
            if i & step == 0:
                first, second = tiles[i], tiles[i | step]
                tiles[i] = jnp.where(keep, first, pltpu.roll(second, step * cap, 1))
                tiles[i | step] = jnp.where(keep, pltpu.roll(first, LANES - step * cap, 1), second)
        step *= 2
    return tiles


def spread_rows(block, cap):
    groups = block.shape[0]
    wide = jnp.concatenate([block] * groups, axis=1)
    rows = lax.broadcasted_iota(jnp.int32, wide.shape, 0)
    lanes = lax.broadcasted_iota(jnp.int32, wide.shape, 1) // cap
    return jnp.sum(jnp.where(rows == lanes, wide, 0), axis=0, keepdims=True)


def pick_kernel(cell_ref, request_ref, out_ref):
    species, cells = cell_ref.shape
    owners, cap = request_ref.shape[2:]
    groups = LANES // cap
    chunks = owners // (2 * groups)
    highs = cells // LANES
    bundle = lax.axis_index("bundle")
    cell = cell_ref[...]
    stacked = jnp.concatenate(
        [cell[:, LANES * h : LANES * (h + 1)] for h in range(highs)], axis=0
    )
    left = jnp.concatenate(split(stacked), axis=1)

    def chunk(k, carry):
        first = k * 2 * groups
        block = request_ref[bundle, 0, pl.ds(first, 2 * groups), :]
        index = jnp.concatenate(
            [spread_rows(block[:groups], cap), spread_rows(block[groups:], cap)], axis=1
        )
        low = index % LANES
        high = index // LANES
        hot = (lax.broadcasted_iota(jnp.int32, (LANES, 2 * LANES), 0) == low).astype(F32).astype(BF16)
        right = jnp.concatenate([hot, hot], axis=0)
        product = jnp.dot(left, right, preferred_element_type=F32)
        picked = jnp.zeros((species, 2 * LANES), F32)
        for h in range(highs):
            picked = picked + jnp.where(high == h, product[species * h : species * (h + 1)], 0.0)
        blank = jnp.zeros((groups * ROWS - species, 2 * LANES), F32)
        picked = jnp.concatenate([picked, blank], axis=0)
        for half in range(2):
            tiles = exchange_groups(
                [
                    picked[ROWS * g : ROWS * (g + 1), LANES * half : LANES * (half + 1)]
                    for g in range(groups)
                ],
                cap,
            )
            for j in range(groups):
                out_ref[first + half * groups + j] = tiles[j]
        return carry

    repeat_steps(chunks, chunk, 0)


def lines_kernel(
    copies,
    cap,
    table_ref,
    slot_ref,
    length_ref,
    courant_ref,
    flux_ref,
    inflow_ref,
    interaction_ref,
    out_ref,
):
    owners = table_ref.shape[0]
    species = inflow_ref.shape[1]
    lines, nodes = slot_ref.shape[1:]
    groups = species // ROWS
    all_groups = LANES // cap
    blocks = nodes // LANES
    chunk_owners = 2 * all_groups
    chunks = owners // chunk_owners
    total = lines * blocks

    def row(ref, line, block):
        return jnp.broadcast_to(
            ref[0, line : line + 1, LANES * block : LANES * (block + 1)], (ROWS, LANES)
        )

    slots = [row(slot_ref, line, block) for line in range(lines) for block in range(blocks)]

    def gather(k, state):
        columns = []
        for half in range(2):
            columns.append(
                exchange_groups(
                    [table_ref[k * chunk_owners + half * all_groups + j] for j in range(all_groups)],
                    cap,
                )[:groups]
            )
        pieces = []
        for i in range(total):
            local = slots[i] - k * 2 * LANES
            inside = local % LANES
            lower = local < LANES
            for g in range(groups):
                value = jnp.where(
                    lower,
                    jnp.take_along_axis(columns[0][g], inside, axis=1),
                    jnp.take_along_axis(columns[1][g], inside, axis=1),
                )
                if chunks > 1:
                    value = jnp.where((local >= 0) & (local < 2 * LANES), value, state[i * groups + g])
                pieces.append(value)
        return pieces

    start = repeat_steps(
        chunks, gather, [jnp.zeros((ROWS, LANES), F32)] * (total * groups if chunks > 1 else 0)
    )

    lane = lax.broadcasted_iota(jnp.int32, (ROWS, LANES), 1)
    factors, inverse, ends = [], [], []
    for line in range(lines):
        for block in range(blocks):
            rate = row(courant_ref, line, block)
            scale = 1.0 / (1.0 + rate)
            decay = rate * scale
            steps = []
            step = 1
            while step < LANES:
                masked = jnp.where(lane >= step, decay, 0.0)
                steps.append(masked)
                decay = jnp.where(lane >= step, decay * pltpu.roll(decay, step, 1), decay)
                step *= 2
            steps.append(decay)
            factors.append(steps)
            inverse.append(scale)
            ends.append(jnp.broadcast_to(decay[:, LANES - 1 :], (ROWS, LANES)))

    eye = lax.broadcasted_iota(jnp.int32, (species, LANES), 0) == lax.broadcasted_iota(
        jnp.int32, (species, LANES), 1
    )
    padded = jnp.concatenate(
        [inflow_ref[...], jnp.zeros((1, LANES - species), F32)], axis=1
    )
    column = jnp.sum(jnp.where(eye, padded, 0.0), axis=1, keepdims=True)
    entry = jnp.broadcast_to(column, (species, LANES))

    state = list(start)
    for substep in range(SUB):
        for i in range(total):
            for g in range(groups):
                value = state[i * groups + g] * inverse[i]
                step = 1
                for factor in factors[i][:-1]:
                    value = value + factor * pltpu.roll(value, step, 1)
                    step *= 2
                state[i * groups + g] = value
        for line in range(lines):
            for g in range(groups):
                carry = entry[ROWS * g : ROWS * (g + 1)]
                for block in range(blocks):
                    i = line * blocks + block
                    value = state[i * groups + g]
                    last = jnp.broadcast_to(value[:, LANES - 1 :], (ROWS, LANES))
                    state[i * groups + g] = value + factors[i][-1] * carry
                    carry = last + ends[i] * carry

    base = jnp.concatenate(
        [jnp.concatenate(state[i * groups : (i + 1) * groups], axis=0) for i in range(total)],
        axis=1,
    )

    rows = all_groups * ROWS
    blank = jnp.zeros((rows - species, lines * nodes), F32)
    matrix = interaction_ref[...]
    matrix = jnp.concatenate([matrix, jnp.zeros((species, rows - species), F32)], axis=1)
    matrix = jnp.concatenate([matrix, jnp.zeros((rows - species, rows), F32)], axis=0)
    matrix_high, matrix_low = split(matrix)
    left = jnp.concatenate([matrix_high, matrix_low, matrix_high], axis=1)
    iterate = base
    for step in range(NEWTON):
        high, low = split(jnp.concatenate([jnp.tanh(iterate), blank], axis=0))
        right = jnp.concatenate([high, high, low], axis=0)
        iterate = base - jnp.dot(left, right, preferred_element_type=F32)[:species]

    weights = []
    for line in range(lines):
        for block in range(blocks):
            live = lane + LANES * block < length_ref[0, line]
            weights.append(jnp.where(live, row(flux_ref, line, block), 0.0))
    weight = jnp.concatenate(weights, axis=1)
    first_row = lax.broadcasted_iota(jnp.int32, weight.shape, 0) == 0
    scaled = [iterate[ROWS * g : ROWS * (g + 1)] * weight for g in range(groups)]
    scaled.append(jnp.where(first_row, weight, 0.0))
    high, low = split(jnp.concatenate(scaled, axis=0))
    left = jnp.concatenate([high, low], axis=0)
    slot_row = jnp.concatenate([s[:1] for s in slots], axis=1)

    def scatter(k, carry):
        hot = (
            (
                lax.broadcasted_iota(jnp.int32, (2 * LANES, lines * nodes), 0)
                == slot_row - k * 2 * LANES
            )
            .astype(F32)
            .astype(BF16)
        )
        sums = lax.dot_general(
            left, hot, (((1,), (1,)), ((), ())), preferred_element_type=F32
        )
        sums = sums[:rows] + sums[rows:]
        for half in range(2):
            tiles = exchange_groups(
                [
                    sums[ROWS * g : ROWS * (g + 1), LANES * half : LANES * (half + 1)]
                    for g in range(all_groups)
                ],
                cap,
            )
            for j in range(all_groups):
                for copy in range(copies):
                    out_ref[k * chunk_owners + half * all_groups + j, copy] = tiles[j]
        return carry

    repeat_steps(chunks, scatter, 0)


def blend_kernel(sums_ref, request_ref, cell_ref, pore_ref, out_ref):
    owners, bundles = sums_ref.shape[:2]
    species, cells = cell_ref.shape
    cap = request_ref.shape[3]
    groups = LANES // cap
    rows = groups * ROWS
    width = 2 * LANES
    highs = cells // width
    chunks = owners // ROWS
    tiles_each = bundles // groups

    def chunk(k, total):
        values, indices = [], []
        requests = request_ref[:, 0, pl.ds(k * ROWS, ROWS), :]
        for t in range(tiles_each):
            block = jnp.concatenate([requests[t * groups + j] for j in range(groups)], axis=1)
            for d in range(ROWS):
                tiles = exchange_groups(
                    [sums_ref[k * ROWS + d, t * groups + j] for j in range(groups)], cap
                )
                values.append(jnp.concatenate(tiles, axis=0))
                indices.append(block[d : d + 1])
        value = jnp.concatenate(values, axis=1)
        index = jnp.concatenate(indices, axis=1)
        entries = index.shape[1]
        low = index % width
        high = jnp.broadcast_to(index // width, (2 * ROWS, entries)).astype(F32).astype(BF16)
        hot = (
            (lax.broadcasted_iota(jnp.int32, (width, entries), 0) == low).astype(F32).astype(BF16)
        )
        parts = jnp.concatenate(split(value), axis=0)
        pieces = []
        for h in range(highs):
            mask = high == jnp.array(h, BF16)
            for r in range(2 * rows // (2 * ROWS)):
                piece = parts[2 * ROWS * r : 2 * ROWS * (r + 1)]
                pieces.append(jnp.where(mask, piece, jnp.zeros_like(piece)))
        left = jnp.concatenate(pieces, axis=0)
        product = lax.dot_general(
            left, hot, (((1,), (1,)), ((), ())), preferred_element_type=F32
        )
        return product if chunks == 1 else total + product

    total = repeat_steps(
        chunks, chunk, jnp.zeros((highs * 2 * rows, width), F32) if chunks > 1 else 0
    )
    for h in range(highs):
        part = total[2 * rows * h : 2 * rows * (h + 1)]
        part = part[:rows] + part[rows:]
        pore = pore_ref[:, width * h : width * (h + 1)]
        scale = pore + part[species : species + 1]
        columns = slice(width * h, width * (h + 1))
        out_ref[:, columns] = (pore * cell_ref[:, columns] + part[:species]) / scale


def call(kernel, shape, operands, smem=()):
    vmem = pl.BlockSpec(memory_space=pltpu.VMEM)
    scalar = pl.BlockSpec(memory_space=pltpu.SMEM)
    return pl.pallas_call(
        kernel,
        out_shape=jax.ShapeDtypeStruct(shape, F32),
        in_specs=[scalar if i in smem else vmem for i in range(len(operands))],
        out_specs=vmem,
        compiler_params=pltpu.CompilerParams(vmem_limit_bytes=VMEM_BYTES),
    )(*operands)


def shards(
    bundles,
    cell_state,
    pore_volume,
    request_cell,
    node_slot,
    line_length,
    courant,
    flux_weight,
    inflow,
    interaction,
):
    owners = request_cell.shape[2]
    outgoing = call(pick_kernel, (owners, ROWS, LANES), (cell_state, request_cell))
    table = lax.all_to_all(outgoing, "grid", split_axis=0, concat_axis=0, tiled=True)
    sums = call(
        functools.partial(lines_kernel, bundles, request_cell.shape[3]),
        (owners, bundles, ROWS, LANES),
        (table, node_slot, line_length, courant, flux_weight, inflow, interaction),
        smem=(2,),
    )
    sums = sums.reshape(owners * bundles, ROWS, LANES)
    back = lax.all_to_all(sums, ("grid", "bundle"), split_axis=0, concat_axis=0, tiled=True)
    back = back.reshape(owners, bundles, ROWS, LANES)
    return call(
        blend_kernel,
        cell_state.shape,
        (back, request_cell, cell_state, pore_volume[None, :]),
    )


def solution(mesh):
    placed = (
        P(None, "grid"),
        P("grid"),
        P(None, "grid", None, None),
        P("bundle", "grid", None),
        P("bundle", "grid"),
        P("bundle", "grid", None),
        P("bundle", "grid", None),
        P("bundle", None),
        P(),
    )
    return jax.shard_map(
        functools.partial(shards, mesh.shape["bundle"]),
        mesh=mesh,
        in_specs=placed,
        out_specs=P(None, "grid"),
        check_vma=False,
    )
```

time: 188 us -> 48.1 us (0.26)
  other arithmetic: 84.9 us -> 0 us
  local copies, waits for them, and re-layouts: 70 us -> 1.76 us
  Pallas kernels: 0 us -> 22 us
  starting transfers between devices: 19.3 us -> 0 us
  blocking collectives: 10.7 us -> 23.9 us
    scatter-add x4 -> x0, other arithmetic: 63.7 us -> none  [the longest x1 28.8 us: shards(): jnp.zeros((owners * capacity,), jnp.float32).at[flat_slots].add(weight)]
    slice x105 -> x0, local copies, waits for them, and re-layouts: 29.1 us -> none  [transport(): scanned = lax.associative_scan(combine, (decay_full, source), axis=2)]
    all_to_all x0 -> x2, blocking collectives: none -> 23.9 us  [the longest x1 13.9 us: shards(): lax.all_to_all(outgoing, 'grid', split_axis=0, concat_axis=0, tiled=True)]
    pallas_call x0 -> x3, Pallas kernels: none -> 22 us  [call(): pl.pallas_call(kernel, out_shape=jax.ShapeDtypeStruct(shape, F32), in_spe...]
    all_to_all x3 -> x0, starting transfers between devices: 19.3 us -> none  [the longest x1 7.28 us: shards(): lax.all_to_all(outgoing, 'grid', split_axis=0, concat_axis=0, tiled=True)]
    gather x2 -> x0, local copies, waits for them, and re-layouts: 14.8 us -> none  [the longest x1 14.1 us: shards(): state_now = jnp.transpose(jnp.take(slot_table, slot_ids, axis=0), (2, 0, 1))]
    pad x40 -> x0, local copies, waits for them, and re-layouts: 14.4 us -> none  [transport(): scanned = lax.associative_scan(combine, (decay_full, source), axis=2)]
    add x63 -> x0, other arithmetic: 11.4 us -> none  [the longest x40 7.41 us: combine(): return (earlier[0] * later[0], later[0] * earlier[1] + later[1])]
  transfers between devices with their start and end apart: 3 -> 0, of which waited for: 0 -> 0; matrix products, arithmetic and copies ran while one was open for 75% -> 0% of each run, Pallas kernels for 0% -> 0%
where the time goes in v1:
time: 48.1 us; the launch traced here: 47.8 us
  blocking collectives  23.9 us (50%)
  Pallas kernels  22 us (46%)
  local copies, waits for them, and re-layouts  1.76 us (4%)
    pallas_call x3, Pallas kernels, call(): pl.pallas_call(kernel, out_shape=jax.ShapeDtypeStruct(shape, F32), in_spe...  22 us
    all_to_all x1, blocking collectives, shards(): lax.all_to_all(outgoing, 'grid', split_axis=0, concat_axis=0, tiled=True)  13.9 us
    all_to_all x1, blocking collectives, shards(): lax.all_to_all(sums, ('grid', 'bundle'), split_axis=0, concat_axis=0, til...  10 us
    unnamed x20, local copies, waits for them, and re-layouts  1.76 us

profile of v1, /device:TPU:0, one launch (start us, length us, event | category | flops | bytes accessed | tf_op | source)
XLA Modules:
  0.0 47.8 jit_solution(2289641404999785544)
XLA Ops:
  0.0 0.0 copy-start
  0.0 1.0 %copy-done = f32[24,4096]{1,0:T(8,128)S(1)} copy-done((f32[24,4096]{1,0:T(8,128)S(1)}, f32[24,4096]{1,0:T(8,128)}, u32[]{:S(2)}) %copy-start) | copy-done | bytes 393240
  1.0 0.0 copy-start.2
  1.0 0.7 %copy-done.2 = s32[4,1,8,32]{3,2,1,0:T(8,128)S(1)} copy-done((s32[4,1,8,32]{3,2,1,0:T(8,128)S(1)}, s32[4,1,8,32]{3,2,1,0:T(8,128)}, u32[]{:S(2)}) %copy-start.2) | copy-done | bytes 4120
  1.7 0.0 copy-start.1
  1.7 0.5 %shard_map.91 = f32[8,8,128]{2,1,0:T(8,128)S(1)} custom-call(f32[24,4096]{1,0:T(8,128)S(1)} %copy-done, s32[4,1,8,32]{3,2,1,0:T(8,128)S(1)} %copy-done.2), custom_call_target="tpu_custom_call" | custom-call | tf_op jit(solution)/shard_map/pallas_call | solution.py:322
  2.3 0.0 copy-start.3
  2.3 0.0 copy-start.4
  2.3 0.0 copy-start.5
  2.3 0.0 copy-start.7
  2.3 0.0 copy-start.8
  2.3 0.0 copy-start.9
  2.3 13.9 %all_to_all.10.table_ref = f32[8,8,128]{2,1,0:T(8,128)S(1)} all-to-all(f32[8,8,128]{2,1,0:T(8,128)S(1)} %shard_map.91), channel_id=1, replica_groups=mesh['grid'=8,'bundle'=4] {'grid'}, dimensions={0} | all-to-all | bytes 65536 | tf_op jit(solution)/shard_map/all_to_all | solution.py:345
  16.2 0.0 copy-done.3
  16.2 0.0 copy-done.4
  16.2 0.0 copy-done.5
  16.2 0.0 copy-done.7
  16.2 0.0 copy-done.8
  16.2 0.0 copy-done.9
  16.2 19.8 %shard_map.92 = f32[8,4,8,128]{3,2,1,0:T(8,128)S(1)} custom-call(f32[8,8,128]{2,1,0:T(8,128)S(1)} %all_to_all.10.table_ref, s32[1,2,2048]{2,1,0:T(2,128)S(1)} %copy-done.3, s32[1,2]{1,0:T(1,128)S(1)} %copy-done.8, f32[1,2,2048]{2,1,0:T(2,128)S(1)} %copy-done.4, f32[1,2,2048]{2,1,0:T(2,128)S(1)} %copy-done.5, f32[1,24]{1,0:T(1,128)S(1)} %copy-done.9, ...), custom_call_target="tpu_custom_call" | custom-call | tf_op jit(solution)/shard_map/pallas_call | solution.py:322
  36.1 0.0 copy-start.6
  36.1 10.0 %all_to_all.11 = f32[32,8,128]{2,1,0:T(8,128)S(1)} all-to-all(f32[32,8,128]{2,1,0:T(8,128)S(1)} %bitcast.3), channel_id=1, replica_groups=mesh['grid'=8,'bundle'=4] {'grid','bundle'}, dimensions={0} | all-to-all | bytes 262144 | tf_op jit(solution)/shard_map/all_to_all | solution.py:353
  46.1 0.0 copy-done.1
  46.1 0.0 copy-done.6
  46.1 1.7 %shard_map.93 = f32[24,4096]{1,0:T(8,128)} custom-call(f32[8,4,8,128]{3,2,1,0:T(8,128)S(1)} %bitcast.4, s32[4,1,8,32]{3,2,1,0:T(8,128)S(1)} %copy-done.2, f32[24,4096]{1,0:T(8,128)S(1)} %copy-done.1, f32[1,4096]{1,0:T(1,128)S(1)} %bitcast.5), custom_call_target="tpu_custom_call" | custom-call | tf_op jit(solution)/shard_map/pallas_call | solution.py:322
Async XLA Ops:
  0.0 1.0 %copy-start = (f32[24,4096]{1,0:T(8,128)S(1)}, f32[24,4096]{1,0:T(8,128)}, u32[]{:S(2)}) copy-start(f32[24,4096]{1,0:T(8,128)} %cell_ref.3) | copy-start | bytes 1179652
  1.0 0.7 %copy-start.2 = (s32[4,1,8,32]{3,2,1,0:T(8,128)S(1)}, s32[4,1,8,32]{3,2,1,0:T(8,128)}, u32[]{:S(2)}) copy-start(s32[4,1,8,32]{3,2,1,0:T(8,128)} %request_ref.3) | copy-start | bytes 12292
  1.7 44.4 %copy-start.1 = (f32[24,4096]{1,0:T(8,128)S(1)}, f32[24,4096]{1,0:T(8,128)}, u32[]{:S(2)}) copy-start(f32[24,4096]{1,0:T(8,128)} %cell_ref.3) | copy-start | bytes 1179652
  2.3 14.0 %copy-start.3 = (s32[1,2,2048]{2,1,0:T(2,128)S(1)}, s32[1,2,2048]{2,1,0:T(2,128)}, u32[]{:S(2)}) copy-start(s32[1,2,2048]{2,1,0:T(2,128)} %slot_ref.1) | copy-start | bytes 49156
  2.3 14.0 %copy-start.4 = (f32[1,2,2048]{2,1,0:T(2,128)S(1)}, f32[1,2,2048]{2,1,0:T(2,128)}, u32[]{:S(2)}) copy-start(f32[1,2,2048]{2,1,0:T(2,128)} %courant_ref.1) | copy-start | bytes 49156
  2.3 14.0 %copy-start.5 = (f32[1,2,2048]{2,1,0:T(2,128)S(1)}, f32[1,2,2048]{2,1,0:T(2,128)}, u32[]{:S(2)}) copy-start(f32[1,2,2048]{2,1,0:T(2,128)} %flux_ref.1) | copy-start | bytes 49156
  2.3 13.9 %copy-start.7 = (f32[24,24]{1,0:T(8,128)S(1)}, f32[24,24]{1,0:T(8,128)}, u32[]{:S(2)}) copy-start(f32[24,24]{1,0:T(8,128)} %interaction_ref.1) | copy-start | bytes 6916
  2.3 13.9 %copy-start.8 = (s32[1,2]{1,0:T(1,128)S(1)}, s32[1,2]{1,0:T(1,128)}, u32[]{:S(2)}) copy-start(s32[1,2]{1,0:T(1,128)} %length_ref.1) | copy-start | bytes 28
  2.3 13.9 %copy-start.9 = (f32[1,24]{1,0:T(1,128)S(1)}, f32[1,24]{1,0:T(1,128)}, u32[]{:S(2)}) copy-start(f32[1,24]{1,0:T(1,128)} %inflow_ref.1) | copy-start | bytes 292
  36.1 10.0 %copy-start.6 = (f32[4096]{0:T(1024)S(1)}, f32[4096]{0:T(1024)}, u32[]{:S(2)}) copy-start(f32[4096]{0:T(1024)} %param.10) | copy-start | bytes 49156

commit v2 on v1

--- a/solution.py
+++ b/solution.py
@@ -95,6 +95,21 @@
     repeat_steps(chunks, chunk, 0)
 
 
+def to_segments(refs):
+    lines, nodes = refs[0].shape[1:]
+    blocks = nodes // LANES
+    width = lines * blocks
+    groups = LANES // width
+    stacked = []
+    for ref in refs:
+        value = ref[0].astype(F32)
+        stacked += [value[:, LANES * block : LANES * (block + 1)] for block in range(blocks)]
+    stacked.append(jnp.zeros((LANES - width * len(refs), LANES), F32))
+    turned = jnp.transpose(jnp.concatenate(stacked, axis=0))
+    times = LANES // groups
+    return exchange_groups([turned[times * g : times * (g + 1)] for g in range(groups)], width)
+
+
 def lines_kernel(
     copies,
     cap,
@@ -112,101 +127,123 @@
     lines, nodes = slot_ref.shape[1:]
     groups = species // ROWS
     all_groups = LANES // cap
+    rows = all_groups * ROWS
     blocks = nodes // LANES
+    width = lines * blocks
+    segments = LANES // width
+    times = LANES // segments
     chunk_owners = 2 * all_groups
     chunks = owners // chunk_owners
-    total = lines * blocks
-
-    def row(ref, line, block):
-        return jnp.broadcast_to(
-            ref[0, line : line + 1, LANES * block : LANES * (block + 1)], (ROWS, LANES)
-        )
-
-    slots = [row(slot_ref, line, block) for line in range(lines) for block in range(blocks)]
+    slot, courant, flux = to_segments([slot_ref, courant_ref, flux_ref])[:3]
+
+    def hot(k):
+        local = (slot - (k * 2 * LANES)).astype(BF16) if chunks == 1 else (
+            slot - lax.convert_element_type(k * 2 * LANES, F32)
+        ).astype(BF16)
+        index = lax.broadcasted_iota(jnp.int32, (2 * LANES, LANES), 0).astype(F32).astype(BF16)
+        one, zero = jnp.ones_like(index), jnp.zeros_like(index)
+        return jnp.concatenate(
+            [
+                jnp.where(jnp.broadcast_to(local[t : t + 1], index.shape) == index, one, zero)
+                for t in range(times)
+            ],
+            axis=1,
+        )
+
+    kept = hot(0) if chunks == 1 else None
 
     def gather(k, state):
-        columns = []
+        halves = []
         for half in range(2):
-            columns.append(
-                exchange_groups(
-                    [table_ref[k * chunk_owners + half * all_groups + j] for j in range(all_groups)],
-                    cap,
-                )[:groups]
+            first = k * chunk_owners + half * all_groups
+            halves.append(
+                jnp.concatenate(
+                    exchange_groups([table_ref[first + j] for j in range(all_groups)], cap), axis=0
+                )
             )
-        pieces = []
-        for i in range(total):
-            local = slots[i] - k * 2 * LANES
-            inside = local % LANES
-            lower = local < LANES
-            for g in range(groups):
-                value = jnp.where(
-                    lower,
-                    jnp.take_along_axis(columns[0][g], inside, axis=1),
-                    jnp.take_along_axis(columns[1][g], inside, axis=1),
-                )
-                if chunks > 1:
-                    value = jnp.where((local >= 0) & (local < 2 * LANES), value, state[i * groups + g])
-                pieces.append(value)
-        return pieces
+        left = jnp.concatenate(split(jnp.concatenate(halves, axis=1)), axis=0)
+        found = jnp.dot(left, hot(k) if kept is None else kept, preferred_element_type=F32)
+        found = found[:species] + found[rows : rows + species]
+        return found if chunks == 1 else state + found
 
     start = repeat_steps(
-        chunks, gather, [jnp.zeros((ROWS, LANES), F32)] * (total * groups if chunks > 1 else 0)
+        chunks, gather, jnp.zeros((species, lines * nodes), F32) if chunks > 1 else 0
     )
 
     lane = lax.broadcasted_iota(jnp.int32, (ROWS, LANES), 1)
-    factors, inverse, ends = [], [], []
-    for line in range(lines):
-        for block in range(blocks):
-            rate = row(courant_ref, line, block)
-            scale = 1.0 / (1.0 + rate)
-            decay = rate * scale
-            steps = []
-            step = 1
-            while step < LANES:
-                masked = jnp.where(lane >= step, decay, 0.0)
-                steps.append(masked)
-                decay = jnp.where(lane >= step, decay * pltpu.roll(decay, step, 1), decay)
-                step *= 2
-            steps.append(decay)
-            factors.append(steps)
-            inverse.append(scale)
-            ends.append(jnp.broadcast_to(decay[:, LANES - 1 :], (ROWS, LANES)))
+    part = lane // width
+    block = (lane % width) // lines
+    segment = block * segments + part
+    line = lane % lines
+
+    def earlier(value, distance):
+        major, minor = distance // segments, distance % segments
+        near = pltpu.roll(value, minor * width + major * lines, 1)
+        if minor == 0:
+            return near
+        far = pltpu.roll(value, minor * width + (major + 1) * lines, 1)
+        return jnp.where(part >= minor, near, far)
 
     eye = lax.broadcasted_iota(jnp.int32, (species, LANES), 0) == lax.broadcasted_iota(
         jnp.int32, (species, LANES), 1
     )
-    padded = jnp.concatenate(
-        [inflow_ref[...], jnp.zeros((1, LANES - species), F32)], axis=1
-    )
+    padded = jnp.concatenate([inflow_ref[...], jnp.zeros((1, LANES - species), F32)], axis=1)
     column = jnp.sum(jnp.where(eye, padded, 0.0), axis=1, keepdims=True)
     entry = jnp.broadcast_to(column, (species, LANES))
-
-    state = list(start)
-    for substep in range(SUB):
-        for i in range(total):
-            for g in range(groups):
-                value = state[i * groups + g] * inverse[i]
-                step = 1
-                for factor in factors[i][:-1]:
-                    value = value + factor * pltpu.roll(value, step, 1)
-                    step *= 2
-                state[i * groups + g] = value
-        for line in range(lines):
-            for g in range(groups):
-                carry = entry[ROWS * g : ROWS * (g + 1)]
-                for block in range(blocks):
-                    i = line * blocks + block
-                    value = state[i * groups + g]
-                    last = jnp.broadcast_to(value[:, LANES - 1 :], (ROWS, LANES))
-                    state[i * groups + g] = value + factors[i][-1] * carry
-                    carry = last + ends[i] * carry
-
-    base = jnp.concatenate(
-        [jnp.concatenate(state[i * groups : (i + 1) * groups], axis=0) for i in range(total)],
-        axis=1,
-    )
-
-    rows = all_groups * ROWS
+    entry = [entry[ROWS * g : ROWS * (g + 1)] for g in range(groups)]
+
+    scale = 1.0 / (1.0 + courant)
+    decay = courant * scale
+    first = [None] * groups
+    second = [None] * groups
+    local, ones, twos = [], [], []
+    for t in range(times):
+        scale_t = jnp.broadcast_to(scale[t : t + 1], (ROWS, LANES))
+        decay_t = jnp.broadcast_to(decay[t : t + 1], (ROWS, LANES))
+        one = decay_t if t == 0 else decay_t * ones[-1]
+        two = scale_t * one if t == 0 else scale_t * one + decay_t * twos[-1]
+        ones.append(one)
+        twos.append(two)
+        for g in range(groups):
+            value = start[ROWS * g : ROWS * (g + 1), LANES * t : LANES * (t + 1)] * scale_t
+            first[g] = value if t == 0 else value + decay_t * first[g]
+            value = scale_t * first[g]
+            second[g] = value if t == 0 else value + decay_t * second[g]
+            local.append(second[g])
+
+    a, b = ones[-1], twos[-1]
+    head = segment == 0
+    first = [jnp.where(head, f + a * e, f) for f, e in zip(first, entry)]
+    second = [jnp.where(head, s + b * e + a * e, s) for s, e in zip(second, entry)]
+    distance = 1
+    while distance < blocks * segments:
+        open_ = segment >= distance
+        a_open, b_open = jnp.where(open_, a, 0.0), jnp.where(open_, b, 0.0)
+        ahead = [earlier(f, distance) for f in first]
+        second = [
+            s + b_open * f + a_open * earlier(s, distance) for s, f in zip(second, ahead)
+        ]
+        first = [f + a_open * e for f, e in zip(first, ahead)]
+        if 2 * distance < blocks * segments:
+            a_ahead = earlier(a, distance)
+            b = b * a_ahead + a * earlier(b, distance)
+            a = a * a_ahead
+        distance *= 2
+    carry_one = [jnp.where(head, e, earlier(f, 1)) for e, f in zip(entry, first)]
+    carry_two = [jnp.where(head, e, earlier(s, 1)) for e, s in zip(entry, second)]
+    columns = []
+    for t in range(times):
+        columns.append(
+            jnp.concatenate(
+                [
+                    local[t * groups + g] + twos[t] * carry_one[g] + ones[t] * carry_two[g]
+                    for g in range(groups)
+                ],
+                axis=0,
+            )
+        )
+    base = jnp.concatenate(columns, axis=1)
+
     blank = jnp.zeros((rows - species, lines * nodes), F32)
     matrix = interaction_ref[...]
     matrix = jnp.concatenate([matrix, jnp.zeros((species, rows - species), F32)], axis=1)
@@ -219,30 +256,27 @@
         right = jnp.concatenate([high, high, low], axis=0)
         iterate = base - jnp.dot(left, right, preferred_element_type=F32)[:species]
 
+    length = jnp.zeros((ROWS, LANES), jnp.int32)
+    for one_line in range(lines):
+        length = jnp.where(line == one_line, length_ref[0, one_line], length)
+    node = block * LANES + part * times
     weights = []
-    for line in range(lines):
-        for block in range(blocks):
-            live = lane + LANES * block < length_ref[0, line]
-            weights.append(jnp.where(live, row(flux_ref, line, block), 0.0))
+    for t in range(times):
+        weights.append(
+            jnp.where(node + t < length, jnp.broadcast_to(flux[t : t + 1], (ROWS, LANES)), 0.0)
+        )
     weight = jnp.concatenate(weights, axis=1)
     first_row = lax.broadcasted_iota(jnp.int32, weight.shape, 0) == 0
     scaled = [iterate[ROWS * g : ROWS * (g + 1)] * weight for g in range(groups)]
     scaled.append(jnp.where(first_row, weight, 0.0))
-    high, low = split(jnp.concatenate(scaled, axis=0))
-    left = jnp.concatenate([high, low], axis=0)
-    slot_row = jnp.concatenate([s[:1] for s in slots], axis=1)
+    left = jnp.concatenate(split(jnp.concatenate(scaled, axis=0)), axis=0)
 
     def scatter(k, carry):
-        hot = (
-            (
-                lax.broadcasted_iota(jnp.int32, (2 * LANES, lines * nodes), 0)
-                == slot_row - k * 2 * LANES
-            )
-            .astype(F32)
-            .astype(BF16)
-        )
         sums = lax.dot_general(
-            left, hot, (((1,), (1,)), ((), ())), preferred_element_type=F32
+            left,
+            hot(k) if kept is None else kept,
+            (((1,), (1,)), ((), ())),
+            preferred_element_type=F32,
         )
         sums = sums[:rows] + sums[rows:]
         for half in range(2):

time: 48.1 us -> 31.4 us (0.65)
  Pallas kernels: 22 us -> 5.35 us
    pallas_call x3, Pallas kernels: 22 us -> 5.35 us  [call(): pl.pallas_call(kernel, out_shape=jax.ShapeDtypeStruct(shape, F32), in_spe...]
where the time goes in v2:
time: 31.4 us; the launch traced here: 31.1 us
  blocking collectives  23.9 us (76%)
  Pallas kernels  5.35 us (17%)
  local copies, waits for them, and re-layouts  1.76 us (6%)
    all_to_all x1, blocking collectives, shards(): lax.all_to_all(outgoing, 'grid', split_axis=0, concat_axis=0, tiled=True)  13.9 us
    all_to_all x1, blocking collectives, shards(): lax.all_to_all(sums, ('grid', 'bundle'), split_axis=0, concat_axis=0, til...  10 us
    pallas_call x3, Pallas kernels, call(): pl.pallas_call(kernel, out_shape=jax.ShapeDtypeStruct(shape, F32), in_spe...  5.35 us
    unnamed x20, local copies, waits for them, and re-layouts  1.76 us

profile of v2, /device:TPU:0, one launch (start us, length us, event | category | flops | bytes accessed | tf_op | source)
XLA Modules:
  0.0 31.1 jit_solution(14938659445893909913)
XLA Ops:
  0.0 0.0 copy-start
  0.0 1.0 %copy-done = f32[24,4096]{1,0:T(8,128)S(1)} copy-done((f32[24,4096]{1,0:T(8,128)S(1)}, f32[24,4096]{1,0:T(8,128)}, u32[]{:S(2)}) %copy-start) | copy-done | bytes 393240
  1.0 0.0 copy-start.2
  1.0 0.7 %copy-done.2 = s32[4,1,8,32]{3,2,1,0:T(8,128)S(1)} copy-done((s32[4,1,8,32]{3,2,1,0:T(8,128)S(1)}, s32[4,1,8,32]{3,2,1,0:T(8,128)}, u32[]{:S(2)}) %copy-start.2) | copy-done | bytes 4120
  1.7 0.0 copy-start.1
  1.7 0.5 %shard_map.91 = f32[8,8,128]{2,1,0:T(8,128)S(1)} custom-call(f32[24,4096]{1,0:T(8,128)S(1)} %copy-done, s32[4,1,8,32]{3,2,1,0:T(8,128)S(1)} %copy-done.2), custom_call_target="tpu_custom_call" | custom-call | tf_op jit(solution)/shard_map/pallas_call | solution.py:356
  2.3 0.0 copy-start.3
  2.3 0.0 copy-start.4
  2.3 0.0 copy-start.5
  2.3 0.0 copy-start.7
  2.3 0.0 copy-start.8
  2.3 0.0 copy-start.9
  2.3 13.9 %all_to_all.10.table_ref = f32[8,8,128]{2,1,0:T(8,128)S(1)} all-to-all(f32[8,8,128]{2,1,0:T(8,128)S(1)} %shard_map.91), channel_id=1, replica_groups=mesh['grid'=8,'bundle'=4] {'grid'}, dimensions={0} | all-to-all | bytes 65536 | tf_op jit(solution)/shard_map/all_to_all | solution.py:379
  16.2 0.0 copy-done.3
  16.2 0.0 copy-done.4
  16.2 0.0 copy-done.5
  16.2 0.0 copy-done.7
  16.2 0.0 copy-done.8
  16.2 0.0 copy-done.9
  16.2 3.2 %shard_map.92 = f32[8,4,8,128]{3,2,1,0:T(8,128)S(1)} custom-call(f32[8,8,128]{2,1,0:T(8,128)S(1)} %all_to_all.10.table_ref, s32[1,2,2048]{2,1,0:T(2,128)S(1)} %copy-done.3, s32[1,2]{1,0:T(1,128)S(1)} %copy-done.8, f32[1,2,2048]{2,1,0:T(2,128)S(1)} %copy-done.4, f32[1,2,2048]{2,1,0:T(2,128)S(1)} %copy-done.5, f32[1,24]{1,0:T(1,128)S(1)} %copy-done.9, ...), custom_call_target="tpu_custom_call" | custom-call | tf_op jit(solution)/shard_map/pallas_call | solution.py:356
  19.4 0.0 copy-start.6
  19.4 10.0 %all_to_all.11 = f32[32,8,128]{2,1,0:T(8,128)S(1)} all-to-all(f32[32,8,128]{2,1,0:T(8,128)S(1)} %bitcast.3), channel_id=1, replica_groups=mesh['grid'=8,'bundle'=4] {'grid','bundle'}, dimensions={0} | all-to-all | bytes 262144 | tf_op jit(solution)/shard_map/all_to_all | solution.py:387
  29.4 0.0 copy-done.1
  29.4 0.0 copy-done.6
  29.4 1.7 %shard_map.93 = f32[24,4096]{1,0:T(8,128)} custom-call(f32[8,4,8,128]{3,2,1,0:T(8,128)S(1)} %bitcast.4, s32[4,1,8,32]{3,2,1,0:T(8,128)S(1)} %copy-done.2, f32[24,4096]{1,0:T(8,128)S(1)} %copy-done.1, f32[1,4096]{1,0:T(1,128)S(1)} %bitcast.5), custom_call_target="tpu_custom_call" | custom-call | tf_op jit(solution)/shard_map/pallas_call | solution.py:356
Async XLA Ops:
  0.0 1.0 %copy-start = (f32[24,4096]{1,0:T(8,128)S(1)}, f32[24,4096]{1,0:T(8,128)}, u32[]{:S(2)}) copy-start(f32[24,4096]{1,0:T(8,128)} %cell_ref.3) | copy-start | bytes 1179652
  1.0 0.7 %copy-start.2 = (s32[4,1,8,32]{3,2,1,0:T(8,128)S(1)}, s32[4,1,8,32]{3,2,1,0:T(8,128)}, u32[]{:S(2)}) copy-start(s32[4,1,8,32]{3,2,1,0:T(8,128)} %request_ref.3) | copy-start | bytes 12292
  1.7 27.7 %copy-start.1 = (f32[24,4096]{1,0:T(8,128)S(1)}, f32[24,4096]{1,0:T(8,128)}, u32[]{:S(2)}) copy-start(f32[24,4096]{1,0:T(8,128)} %cell_ref.3) | copy-start | bytes 1179652
  2.3 14.0 %copy-start.3 = (s32[1,2,2048]{2,1,0:T(2,128)S(1)}, s32[1,2,2048]{2,1,0:T(2,128)}, u32[]{:S(2)}) copy-start(s32[1,2,2048]{2,1,0:T(2,128)} %slot_ref.1) | copy-start | bytes 49156
  2.3 14.0 %copy-start.4 = (f32[1,2,2048]{2,1,0:T(2,128)S(1)}, f32[1,2,2048]{2,1,0:T(2,128)}, u32[]{:S(2)}) copy-start(f32[1,2,2048]{2,1,0:T(2,128)} %courant_ref.1) | copy-start | bytes 49156
  2.3 14.0 %copy-start.5 = (f32[1,2,2048]{2,1,0:T(2,128)S(1)}, f32[1,2,2048]{2,1,0:T(2,128)}, u32[]{:S(2)}) copy-start(f32[1,2,2048]{2,1,0:T(2,128)} %flux_ref.1) | copy-start | bytes 49156
  2.3 13.9 %copy-start.7 = (f32[24,24]{1,0:T(8,128)S(1)}, f32[24,24]{1,0:T(8,128)}, u32[]{:S(2)}) copy-start(f32[24,24]{1,0:T(8,128)} %interaction_ref.1) | copy-start | bytes 6916
  2.3 13.9 %copy-start.8 = (s32[1,2]{1,0:T(1,128)S(1)}, s32[1,2]{1,0:T(1,128)}, u32[]{:S(2)}) copy-start(s32[1,2]{1,0:T(1,128)} %length_ref.1) | copy-start | bytes 28
  2.3 13.9 %copy-start.9 = (f32[1,24]{1,0:T(1,128)S(1)}, f32[1,24]{1,0:T(1,128)}, u32[]{:S(2)}) copy-start(f32[1,24]{1,0:T(1,128)} %inflow_ref.1) | copy-start | bytes 292
  19.4 10.0 %copy-start.6 = (f32[4096]{0:T(1024)S(1)}, f32[4096]{0:T(1024)}, u32[]{:S(2)}) copy-start(f32[4096]{0:T(1024)} %param.10) | copy-start | bytes 49156

commit v3 on v2

v3 whole, which is shorter than its diff:
```python
import functools

import jax
import jax.numpy as jnp
from jax import lax
from jax.experimental import pallas as pl
from jax.experimental.pallas import tpu as pltpu
from jax.sharding import PartitionSpec as P

SUB = 2
NEWTON = 3
LANES = 128
ROWS = 8
F32 = jnp.float32
BF16 = jnp.bfloat16
VMEM_BYTES = 32 * 1024 * 1024
DIRECT = 16


def repeat_steps(count, body, carry):
    if count == 1:
        return body(0, carry)
    return lax.fori_loop(0, count, body, carry)


def split(value):
    high = value.astype(BF16)
    low = (value - high.astype(F32)).astype(BF16)
    return high, low


def exchange_groups(tiles, cap):
    tiles = list(tiles)
    lane_group = lax.broadcasted_iota(jnp.int32, tiles[0].shape, 1) // cap
    step = 1
    while step < len(tiles):
        keep = (lane_group & step) == 0
        for i in range(len(tiles)):
            if i & step == 0:
                first, second = tiles[i], tiles[i | step]
                tiles[i] = jnp.where(keep, first, pltpu.roll(second, step * cap, 1))
                tiles[i | step] = jnp.where(keep, pltpu.roll(first, LANES - step * cap, 1), second)
        step *= 2
    return tiles


def spread_rows(block, cap):
    groups = block.shape[0]
    wide = jnp.concatenate([block] * groups, axis=1)
    rows = lax.broadcasted_iota(jnp.int32, wide.shape, 0)
    lanes = lax.broadcasted_iota(jnp.int32, wide.shape, 1) // cap
    return jnp.sum(jnp.where(rows == lanes, wide, 0), axis=0, keepdims=True)


def pick_kernel(cell_hbm, request_hbm, *refs):
    *out_refs, cell_ref, request_ref, tile_ref, cell_sem, request_sem = refs
    request_copy = pltpu.make_async_copy(
        request_hbm.at[lax.axis_index("bundle"), 0], request_ref, request_sem
    )
    cell_copy = pltpu.make_async_copy(cell_hbm, cell_ref, cell_sem)
    request_copy.start()
    cell_copy.start()
    species, cells = cell_ref.shape
    owners, cap = request_ref.shape
    groups = LANES // cap
    chunks = owners // (2 * groups)
    highs = cells // LANES
    request_copy.wait()

    def wanted(k):
        block = request_ref[pl.ds(k * 2 * groups, 2 * groups), :]
        index = jnp.concatenate(
            [spread_rows(block[:groups], cap), spread_rows(block[groups:], cap)], axis=1
        )
        low = index % LANES
        high = index // LANES
        hot = (lax.broadcasted_iota(jnp.int32, (LANES, 2 * LANES), 0) == low).astype(F32).astype(BF16)
        return high, jnp.concatenate([hot, hot], axis=0)

    kept = wanted(0) if chunks == 1 else None
    cell_copy.wait()
    cell = cell_ref[...]
    stacked = jnp.concatenate(
        [cell[:, LANES * h : LANES * (h + 1)] for h in range(highs)], axis=0
    )
    left = jnp.concatenate(split(stacked), axis=1)
    direct = len(out_refs) > 1
    into = tile_ref if direct else out_refs[0]

    def chunk(k, carry):
        first = k * 2 * groups
        high, right = wanted(k) if kept is None else kept
        product = jnp.dot(left, right, preferred_element_type=F32)
        picked = jnp.zeros((species, 2 * LANES), F32)
        for h in range(highs):
            picked = picked + jnp.where(high == h, product[species * h : species * (h + 1)], 0.0)
        blank = jnp.zeros((groups * ROWS - species, 2 * LANES), F32)
        picked = jnp.concatenate([picked, blank], axis=0)
        for half in range(2):
            tiles = exchange_groups(
                [
                    picked[ROWS * g : ROWS * (g + 1), LANES * half : LANES * (half + 1)]
                    for g in range(groups)
                ],
                cap,
            )
            for j in range(groups):
                into[first + half * groups + j] = tiles[j]
        return carry

    repeat_steps(chunks, chunk, 0)
    if direct:
        here = lax.axis_index("grid")
        for j in range(owners):
            out_refs[j][...] = tile_ref[lax.rem(here + j, owners)]


def to_segments(refs):
    lines, nodes = refs[0].shape[1:]
    blocks = nodes // LANES
    width = lines * blocks
    groups = LANES // width
    stacked = []
    for ref in refs:
        value = ref[0].astype(F32)
        stacked += [value[:, LANES * block : LANES * (block + 1)] for block in range(blocks)]
    stacked.append(jnp.zeros((LANES - width * len(refs), LANES), F32))
    turned = jnp.transpose(jnp.concatenate(stacked, axis=0))
    times = LANES // groups
    return exchange_groups([turned[times * g : times * (g + 1)] for g in range(groups)], width)


def one_hot(slot, k):
    local = (slot - lax.convert_element_type(k * 2 * LANES, F32)).astype(BF16)
    index = lax.broadcasted_iota(jnp.int32, (2 * LANES, LANES), 0).astype(F32).astype(BF16)
    one, zero = jnp.ones_like(index), jnp.zeros_like(index)
    return jnp.concatenate(
        [
            jnp.where(jnp.broadcast_to(local[t : t + 1], index.shape) == index, one, zero)
            for t in range(slot.shape[0])
        ],
        axis=1,
    )


class Places:
    def __init__(self, lines, nodes):
        self.lines = lines
        self.blocks = nodes // LANES
        self.width = lines * self.blocks
        self.segments = LANES // self.width
        self.times = LANES // self.segments
        lane = lax.broadcasted_iota(jnp.int32, (ROWS, LANES), 1)
        self.part = lane // self.width
        self.block = (lane % self.width) // lines
        self.segment = self.block * self.segments + self.part
        self.line = lane % lines
        self.distances = []
        distance = 1
        while distance < self.blocks * self.segments:
            self.distances.append(distance)
            distance *= 2

    def earlier(self, value, distance):
        major, minor = distance // self.segments, distance % self.segments
        near = pltpu.roll(value, minor * self.width + major * self.lines, 1)
        if minor == 0:
            return near
        far = pltpu.roll(value, minor * self.width + (major + 1) * self.lines, 1)
        return jnp.where(self.part >= minor, near, far)


def prepare_kernel(slot_ref, length_ref, courant_ref, flux_ref, rows_ref, jump_ref, *hot_refs):
    lines, nodes = slot_ref.shape[1:]
    places = Places(lines, nodes)
    times = places.times
    slot, courant, flux = to_segments([slot_ref, courant_ref, flux_ref])[:3]
    scale = 1.0 / (1.0 + courant)
    decay = courant * scale
    rows_ref[0] = scale
    rows_ref[1] = decay
    rows_ref[5] = slot

    one, two = decay[:1], scale[:1] * decay[:1]
    ones, twos = [one], [two]
    for t in range(1, times):
        one = decay[t : t + 1] * one
        two = scale[t : t + 1] * one + decay[t : t + 1] * two
        ones.append(one)
        twos.append(two)
    rows_ref[2] = jnp.concatenate(ones, axis=0)
    rows_ref[3] = jnp.concatenate(twos, axis=0)

    a = jnp.broadcast_to(one, (ROWS, LANES))
    b = jnp.broadcast_to(two, (ROWS, LANES))
    jump_ref[0], jump_ref[1] = a, b
    for i, distance in enumerate(places.distances):
        opened = places.segment >= distance
        jump_ref[2 * i + 2] = jnp.where(opened, a, 0.0)
        jump_ref[2 * i + 3] = jnp.where(opened, b, 0.0)
        ahead = places.earlier(a, distance)
        b = b * ahead + a * places.earlier(b, distance)
        a = a * ahead

    length = jnp.zeros((ROWS, LANES), jnp.int32)
    for line in range(lines):
        length = jnp.where(places.line == line, length_ref[0, line], length)
    start = places.block * LANES + places.part * times - length
    step = lax.broadcasted_iota(jnp.int32, flux.shape, 0)
    rows_ref[4] = jnp.where(step + start[:1] < 0, flux, 0.0)

    for hot_ref in hot_refs:
        hot_ref[...] = one_hot(slot, 0)


def lines_kernel(lines, cap, tables, kept, *refs):
    table_refs, refs = refs[:tables], refs[tables:]
    rows_ref, jump_ref, inflow_ref, interaction_ref = refs[:4]
    refs = refs[4:]
    hot_ref, refs = (refs[0], refs[1:]) if kept else (None, refs)
    *out_refs, tile_ref = refs
    direct = tables > 1
    all_groups = LANES // cap
    owners = tables if direct else table_refs[0].shape[0]
    here = lax.axis_index("grid")
    if direct:
        for j in range(owners):
            tile_ref[lax.rem(here + (owners - j), owners)] = table_refs[j][...]
    table_ref = tile_ref if direct else table_refs[0]
    species = inflow_ref.shape[1]
    times = rows_ref.shape[1]
    nodes = times * LANES // lines
    places = Places(lines, nodes)
    groups = species // ROWS
    rows = all_groups * ROWS
    chunk_owners = 2 * all_groups
    chunks = owners // chunk_owners

    def hot(k):
        return hot_ref[...] if kept else one_hot(rows_ref[5], k)

    def gather(k, state):
        halves = []
        for half in range(2):
            first = k * chunk_owners + half * all_groups
            halves.append(
                jnp.concatenate(
                    exchange_groups([table_ref[first + j] for j in range(all_groups)], cap), axis=0
                )
            )
        left = jnp.concatenate(split(jnp.concatenate(halves, axis=1)), axis=0)
        found = jnp.dot(left, hot(k), preferred_element_type=F32)
        found = found[:species] + found[rows : rows + species]
        return found if chunks == 1 else state + found

    start = repeat_steps(
        chunks, gather, jnp.zeros((species, lines * nodes), F32) if chunks > 1 else 0
    )

    eye = lax.broadcasted_iota(jnp.int32, (species, LANES), 0) == lax.broadcasted_iota(
        jnp.int32, (species, LANES), 1
    )
    padded = jnp.concatenate([inflow_ref[...], jnp.zeros((1, LANES - species), F32)], axis=1)
    column = jnp.sum(jnp.where(eye, padded, 0.0), axis=1, keepdims=True)
    entry = jnp.broadcast_to(column, (species, LANES))
    entry = [entry[ROWS * g : ROWS * (g + 1)] for g in range(groups)]

    def row(kind, t):
        return jnp.broadcast_to(rows_ref[kind, t : t + 1], (ROWS, LANES))

    first = [None] * groups
    second = [None] * groups
    local = []
    for t in range(times):
        scale, decay = row(0, t), row(1, t)
        for g in range(groups):
            value = start[ROWS * g : ROWS * (g + 1), LANES * t : LANES * (t + 1)] * scale
            first[g] = value if t == 0 else value + decay * first[g]
            value = scale * first[g]
            second[g] = value if t == 0 else value + decay * second[g]
            local.append(second[g])

    a, b = jump_ref[0], jump_ref[1]
    head = places.segment == 0
    first = [jnp.where(head, f + a * e, f) for f, e in zip(first, entry)]
    second = [jnp.where(head, s + b * e + a * e, s) for s, e in zip(second, entry)]
    for i, distance in enumerate(places.distances):
        a, b = jump_ref[2 * i + 2], jump_ref[2 * i + 3]
        ahead = [places.earlier(f, distance) for f in first]
        second = [s + b * f + a * places.earlier(s, distance) for s, f in zip(second, ahead)]
        first = [f + a * e for f, e in zip(first, ahead)]
    carry_one = [jnp.where(head, e, places.earlier(f, 1)) for e, f in zip(entry, first)]
    carry_two = [jnp.where(head, e, places.earlier(s, 1)) for e, s in zip(entry, second)]
    columns = []
    for t in range(times):
        one, two = row(2, t), row(3, t)
        columns.append(
            jnp.concatenate(
                [
                    local[t * groups + g] + two * carry_one[g] + one * carry_two[g]
                    for g in range(groups)
                ],
                axis=0,
            )
        )
    base = jnp.concatenate(columns, axis=1)

    blank = jnp.zeros((rows - species, lines * nodes), F32)
    matrix = interaction_ref[...]
    matrix = jnp.concatenate([matrix, jnp.zeros((species, rows - species), F32)], axis=1)
    matrix = jnp.concatenate([matrix, jnp.zeros((rows - species, rows), F32)], axis=0)
    matrix_high, matrix_low = split(matrix)
    left = jnp.concatenate([matrix_high, matrix_low, matrix_high], axis=1)
    iterate = base
    for step in range(NEWTON):
        high, low = split(jnp.concatenate([jnp.tanh(iterate), blank], axis=0))
        right = jnp.concatenate([high, high, low], axis=0)
        iterate = base - jnp.dot(left, right, preferred_element_type=F32)[:species]

    weight = jnp.concatenate([row(4, t) for t in range(times)], axis=1)
    first_row = lax.broadcasted_iota(jnp.int32, weight.shape, 0) == 0
    scaled = [iterate[ROWS * g : ROWS * (g + 1)] * weight for g in range(groups)]
    scaled.append(jnp.where(first_row, weight, 0.0))
    left = jnp.concatenate(split(jnp.concatenate(scaled, axis=0)), axis=0)
    into = tile_ref if direct else out_refs[0]

    def scatter(k, carry):
        sums = lax.dot_general(
            left, hot(k), (((1,), (1,)), ((), ())), preferred_element_type=F32
        )
        sums = sums[:rows] + sums[rows:]
        for half in range(2):
            tiles = exchange_groups(
                [
                    sums[ROWS * g : ROWS * (g + 1), LANES * half : LANES * (half + 1)]
                    for g in range(all_groups)
                ],
                cap,
            )
            for j in range(all_groups):
                into[k * chunk_owners + half * all_groups + j] = tiles[j]
        return carry

    repeat_steps(chunks, scatter, 0)
    if direct:
        for j in range(owners):
            out_refs[j][...] = tile_ref[lax.rem(here + j, owners)]


def blend_kernel(bundles, *refs):
    sums_refs, refs = refs[:bundles], refs[bundles:]
    request_ref, cell_ref, pore_ref, out_ref = refs
    owners = sums_refs[0].shape[0]
    bundle_here = lax.axis_index("bundle")
    species, cells = cell_ref.shape
    cap = request_ref.shape[3]
    groups = LANES // cap
    rows = groups * ROWS
    width = 2 * LANES
    highs = cells // width
    chunks = owners // ROWS
    tiles_each = bundles // groups

    def chunk(k, total):
        values, indices = [], []
        for t in range(tiles_each):
            block = jnp.concatenate(
                [
                    request_ref[
                        lax.rem(bundle_here + (bundles - t * groups - j), bundles),
                        0,
                        pl.ds(k * ROWS, ROWS),
                        :,
                    ]
                    for j in range(groups)
                ],
                axis=1,
            )
            for d in range(ROWS):
                tiles = exchange_groups(
                    [sums_refs[t * groups + j][k * ROWS + d] for j in range(groups)], cap
                )
                values.append(jnp.concatenate(tiles, axis=0))
                indices.append(block[d : d + 1])
        value = jnp.concatenate(values, axis=1)
        index = jnp.concatenate(indices, axis=1)
        entries = index.shape[1]
        low = index % width
        high = jnp.broadcast_to(index // width, (2 * ROWS, entries)).astype(F32).astype(BF16)
        hot = (
            (lax.broadcasted_iota(jnp.int32, (width, entries), 0) == low).astype(F32).astype(BF16)
        )
        parts = jnp.concatenate(split(value), axis=0)
        pieces = []
        for h in range(highs):
            mask = high == jnp.array(h, BF16)
            for r in range(2 * rows // (2 * ROWS)):
                piece = parts[2 * ROWS * r : 2 * ROWS * (r + 1)]
                pieces.append(jnp.where(mask, piece, jnp.zeros_like(piece)))
        left = jnp.concatenate(pieces, axis=0)
        product = lax.dot_general(
            left, hot, (((1,), (1,)), ((), ())), preferred_element_type=F32
        )
        return product if chunks == 1 else total + product

    total = repeat_steps(
        chunks, chunk, jnp.zeros((highs * 2 * rows, width), F32) if chunks > 1 else 0
    )
    for h in range(highs):
        part = total[2 * rows * h : 2 * rows * (h + 1)]
        part = part[:rows] + part[rows:]
        pore = pore_ref[:, width * h : width * (h + 1)]
        scale = pore + part[species : species + 1]
        columns = slice(width * h, width * (h + 1))
        out_ref[:, columns] = (pore * cell_ref[:, columns] + part[:species]) / scale


def call(kernel, shapes, operands, smem=(), hbm=(), scratch=(), flops=0):
    kinds = {i: pltpu.SMEM for i in smem} | {i: pltpu.HBM for i in hbm}
    return pl.pallas_call(
        kernel,
        out_shape=[jax.ShapeDtypeStruct(shape, kind) for shape, kind in shapes],
        in_specs=[
            pl.BlockSpec(memory_space=kinds.get(i, pltpu.VMEM)) for i in range(len(operands))
        ],
        out_specs=[pl.BlockSpec(memory_space=pltpu.VMEM)] * len(shapes),
        scratch_shapes=list(scratch),
        compiler_params=pltpu.CompilerParams(vmem_limit_bytes=VMEM_BYTES),
        cost_estimate=pl.CostEstimate(flops=flops, bytes_accessed=0, transcendentals=0),
    )(*operands)


def send_around(tiles, axis, count):
    return [tiles[0]] + [
        lax.ppermute(tiles[j], axis, [(i, (i + j) % count) for i in range(count)])
        for j in range(1, count)
    ]


def order_kernel(*refs):
    *tile_refs, out_ref = refs
    count = len(tile_refs)
    here = lax.axis_index("grid")
    for j in range(count):
        out_ref[lax.rem(here + (count - j), count)] = tile_refs[j][...]


def by_owner(tiles):
    return call(order_kernel, [((len(tiles), *tiles[0].shape), F32)], tiles)[0]


def shards(
    bundles,
    cell_state,
    pore_volume,
    request_cell,
    node_slot,
    line_length,
    courant,
    flux_weight,
    inflow,
    interaction,
):
    owners, cap = request_cell.shape[2:]
    lines, nodes = node_slot.shape[1:]
    times = lines * nodes // LANES
    direct = owners <= DIRECT
    kept = owners * cap == 2 * LANES
    tile = (ROWS, LANES)
    shapes = [(tile, F32)] * owners if direct else [((owners, *tile), F32)]
    tiles_scratch = pltpu.VMEM((owners, *tile) if direct else (1, *tile), F32)

    def over_grid(tiles):
        if direct:
            return send_around(tiles, "grid", owners)
        return [lax.all_to_all(tiles[0], "grid", split_axis=0, concat_axis=0, tiled=True)]

    outgoing = call(
        pick_kernel,
        shapes,
        (cell_state, request_cell),
        hbm=(0, 1),
        scratch=(
            pltpu.VMEM(cell_state.shape, F32),
            pltpu.VMEM((owners, cap), jnp.int32),
            tiles_scratch,
            pltpu.SemaphoreType.DMA,
            pltpu.SemaphoreType.DMA,
        ),
    )
    jumps = 2
    while 2 ** (jumps // 2 - 1) < nodes // times:
        jumps += 2
    prepared = call(
        prepare_kernel,
        [((6, times, LANES), F32), ((jumps, ROWS, LANES), F32)]
        + ([((2 * LANES, lines * nodes), BF16)] if kept else []),
        (node_slot, line_length, courant, flux_weight),
        smem=(1,),
        flops=10**8,
    )
    tables = over_grid(outgoing)
    sums = call(
        functools.partial(lines_kernel, lines, cap, len(tables), kept),
        shapes,
        (*tables, *prepared[:2], inflow, interaction, *prepared[2:]),
        scratch=(tiles_scratch,),
    )
    sums = over_grid(sums)
    own = sums[0] if not direct else by_owner(sums)
    every = send_around([own] * bundles, "bundle", bundles)
    return call(
        functools.partial(blend_kernel, bundles),
        [(cell_state.shape, F32)],
        (*every, request_cell, cell_state, pore_volume[None, :]),
    )[0]


def solution(mesh):
    placed = (
        P(None, "grid"),
        P("grid"),
        P(None, "grid", None, None),
        P("bundle", "grid", None),
        P("bundle", "grid"),
        P("bundle", "grid", None),
        P("bundle", "grid", None),
        P("bundle", None),
        P(),
    )
    return jax.shard_map(
        functools.partial(shards, mesh.shape["bundle"]),
        mesh=mesh,
        in_specs=placed,
        out_specs=P(None, "grid"),
        check_vma=False,
    )
```

time: 31.4 us -> 43.8 us (1.39)
  starting transfers between devices: 0 us -> 25.5 us
  blocking collectives: 23.9 us -> 0 us
  waiting for transfers between devices: 0 us -> 5.21 us
  local copies, waits for them, and re-layouts: 1.76 us -> 5.88 us
  Pallas kernels: 5.35 us -> 6.38 us
    ppermute x0 -> x17, starting transfers between devices: none -> 25.5 us  [send_around(): lax.ppermute(tiles[j], axis, [(i, (i + j) % count) for i in range(count)])]
    all_to_all x2 -> x0, blocking collectives: 23.9 us -> none  [the longest x1 13.9 us: shards(): lax.all_to_all(outgoing, 'grid', split_axis=0, concat_axis=0, tiled=True)]
    ppermute x0 -> x17, waiting for transfers between devices: none -> 5.21 us  [send_around(): lax.ppermute(tiles[j], axis, [(i, (i + j) % count) for i in range(count)])]
    unnamed x20, local copies, waits for them, and re-layouts: 1.76 us -> 5.88 us
    pallas_call x3 -> x5, Pallas kernels: 5.35 us -> 6.38 us  [call(): pl.pallas_call(kernel, out_shape=[jax.ShapeDtypeStruct(shape, kind) for s...]
  transfers between devices with their start and end apart: 0 -> 17, of which waited for: 0 -> 5; matrix products, arithmetic and copies ran while one was open for 0% -> 0% of each run, Pallas kernels for 0% -> 3%
where the time goes in v3:
time: 43.8 us; the launch traced here: 43.1 us
  starting transfers between devices  25.5 us (58%)
  Pallas kernels  6.38 us (15%)
  local copies, waits for them, and re-layouts  5.88 us (13%)
  waiting for transfers between devices  5.21 us (12%)
    ppermute x17, starting transfers between devices, send_around(): lax.ppermute(tiles[j], axis, [(i, (i + j) % count) for i in range(count)])  25.5 us
    pallas_call x5, Pallas kernels, call(): pl.pallas_call(kernel, out_shape=[jax.ShapeDtypeStruct(shape, kind) for s...  6.38 us
    unnamed x20, local copies, waits for them, and re-layouts  5.88 us
    ppermute x17, waiting for transfers between devices, send_around(): lax.ppermute(tiles[j], axis, [(i, (i + j) % count) for i in range(count)])  5.21 us
  transfers between devices with their start and end apart: 17, of which 5 were waited for; matrix products, arithmetic and copies ran while one was open for 0% of the time, Pallas kernels for 3%

profile of v3, /device:TPU:0, one launch (start us, length us, event | category | flops | bytes accessed | tf_op | source)
XLA Modules:
  0.0 43.1 jit_solution(4460384256346122495)
XLA Ops:
  0.0 0.0 copy-start
  0.0 1.0 %copy-done = f32[24,4096]{1,0:T(8,128)S(1)} copy-done((f32[24,4096]{1,0:T(8,128)S(1)}, f32[24,4096]{1,0:T(8,128)}, u32[]{:S(2)}) %copy-start) | copy-done | bytes 393240
  1.0 0.0 copy-start.2
  1.0 0.7 %copy-done.2 = s32[4,1,8,32]{3,2,1,0:T(8,128)S(1)} copy-done((s32[4,1,8,32]{3,2,1,0:T(8,128)S(1)}, s32[4,1,8,32]{3,2,1,0:T(8,128)}, u32[]{:S(2)}) %copy-start.2) | copy-done | bytes 4120
  1.7 0.0 copy-start.1
  1.7 0.0 copy-start.3
  1.7 0.7 %shard_map.91 = (f32[8,128]{1,0:T(8,128)S(1)}, f32[8,128]{1,0:T(8,128)S(1)}, f32[8,128]{1,0:T(8,128)S(1)}, f32[8,128]{1,0:T(8,128)S(1)}, f32[8,128]{1,0:T(8,128)...) custom-call(f32[24,4096]{1,0:T(8,128)S(1)} %copy-done, s32[4,1,8,32]{3,2,1,0:T(8,128)S(1)} %copy-done.2), custom_call_target="tpu_custom_call" | custom-call | tf_op jit(solution)/shard_map/pallas_call | solution.py:420
  2.5 3.0 %collective-permute-start = (f32[8,128]{1,0:T(8,128)S(1)}, f32[8,128]{1,0:T(8,128)S(1)}, u32[]{:S(2)}, u32[]{:S(2)}) collective-permute-start(f32[8,128]{1,0:T(8,128)S(1)} %get-tuple-element.25), channel_id=1, source_target_pairs={{0,4},{4,8},{8,12},{12,16},{16,20},{20,24},{24,28},{28,0},{1,5},{5... | collective-permute-start | bytes 12296 | tf_op jit(solution)/shard_map/ppermute | solution.py:435
  5.5 1.6 %collective-permute-start.1 = (f32[8,128]{1,0:T(8,128)S(1)}, f32[8,128]{1,0:T(8,128)S(1)}, u32[]{:S(2)}, u32[]{:S(2)}) collective-permute-start(f32[8,128]{1,0:T(8,128)S(1)} %get-tuple-element.26), channel_id=1, source_target_pairs={{0,8},{4,12},{8,16},{12,20},{16,24},{20,28},{24,0},{28,4},{1,9},{5... | collective-permute-start | bytes 12296 | tf_op jit(solution)/shard_map/ppermute | solution.py:435
  7.1 2.5 %collective-permute-start.2 = (f32[8,128]{1,0:T(8,128)S(1)}, f32[8,128]{1,0:T(8,128)S(1)}, u32[]{:S(2)}, u32[]{:S(2)}) collective-permute-start(f32[8,128]{1,0:T(8,128)S(1)} %get-tuple-element.27), channel_id=1, source_target_pairs={{0,12},{4,16},{8,20},{12,24},{16,28},{20,0},{24,4},{28,8},{1,13},{... | collective-permute-start | bytes 12296 | tf_op jit(solution)/shard_map/ppermute | solution.py:435
  9.6 1.2 %collective-permute-start.3 = (f32[8,128]{1,0:T(8,128)S(1)}, f32[8,128]{1,0:T(8,128)S(1)}, u32[]{:S(2)}, u32[]{:S(2)}) collective-permute-start(f32[8,128]{1,0:T(8,128)S(1)} %get-tuple-element.28), channel_id=1, source_target_pairs={{0,16},{4,20},{8,24},{12,28},{16,0},{20,4},{24,8},{28,12},{1,17},{... | collective-permute-start | bytes 12296 | tf_op jit(solution)/shard_map/ppermute | solution.py:435
  10.8 2.6 %collective-permute-start.4 = (f32[8,128]{1,0:T(8,128)S(1)}, f32[8,128]{1,0:T(8,128)S(1)}, u32[]{:S(2)}, u32[]{:S(2)}) collective-permute-start(f32[8,128]{1,0:T(8,128)S(1)} %get-tuple-element.29), channel_id=1, source_target_pairs={{0,20},{4,24},{8,28},{12,0},{16,4},{20,8},{24,12},{28,16},{1,21},{... | collective-permute-start | bytes 12296 | tf_op jit(solution)/shard_map/ppermute | solution.py:435
  13.5 0.0 collective-permute-done.refs_1_
  13.5 1.4 %collective-permute-start.5 = (f32[8,128]{1,0:T(8,128)S(1)}, f32[8,128]{1,0:T(8,128)S(1)}, u32[]{:S(2)}, u32[]{:S(2)}) collective-permute-start(f32[8,128]{1,0:T(8,128)S(1)} %get-tuple-element.30), channel_id=1, source_target_pairs={{0,24},{4,28},{8,0},{12,4},{16,8},{20,12},{24,16},{28,20},{1,25},{... | collective-permute-start | bytes 12296 | tf_op jit(solution)/shard_map/ppermute | solution.py:435
  14.8 0.0 collective-permute-done.1.refs_2_
  14.8 1.4 %collective-permute-start.6 = (f32[8,128]{1,0:T(8,128)S(1)}, f32[8,128]{1,0:T(8,128)S(1)}, u32[]{:S(2)}, u32[]{:S(2)}) collective-permute-start(f32[8,128]{1,0:T(8,128)S(1)} %get-tuple-element.31), channel_id=1, source_target_pairs={{0,28},{4,0},{8,4},{12,8},{16,12},{20,16},{24,20},{28,24},{1,29},{... | collective-permute-start | bytes 12296 | tf_op jit(solution)/shard_map/ppermute | solution.py:435
  16.2 0.0 copy-start.6
  16.2 0.7 %copy-done.6 = s32[1,2,2048]{2,1,0:T(2,128)S(1)} copy-done((s32[1,2,2048]{2,1,0:T(2,128)S(1)}, s32[1,2,2048]{2,1,0:T(2,128)}, u32[]{:S(2)}) %copy-start.6) | copy-done | bytes 16408
  17.0 0.0 copy-start.7
  17.0 0.7 %copy-done.7 = f32[1,2,2048]{2,1,0:T(2,128)S(1)} copy-done((f32[1,2,2048]{2,1,0:T(2,128)S(1)}, f32[1,2,2048]{2,1,0:T(2,128)}, u32[]{:S(2)}) %copy-start.7) | copy-done | bytes 16408
  17.7 0.0 copy-start.8
  17.7 0.7 %copy-done.8 = f32[1,2,2048]{2,1,0:T(2,128)S(1)} copy-done((f32[1,2,2048]{2,1,0:T(2,128)S(1)}, f32[1,2,2048]{2,1,0:T(2,128)}, u32[]{:S(2)}) %copy-start.8) | copy-done | bytes 16408
  18.4 0.0 copy-start.9
  18.4 0.7 %copy-done.9 = s32[1,2]{1,0:T(1,128)S(1)} copy-done((s32[1,2]{1,0:T(1,128)S(1)}, s32[1,2]{1,0:T(1,128)}, u32[]{:S(2)}) %copy-start.9) | copy-done | bytes 32
  19.1 1.5 %shard_map.92 = (f32[6,32,128]{2,1,0:T(8,128)S(1)}, f32[14,8,128]{2,1,0:T(8,128)S(1)}, bf16[256,4096]{1,0:T(8,128)(2,1)S(1)}) custom-call(s32[1,2,2048]{2,1,0:T(2,128)S(1)} %copy-done.6, s32[1,2]{1,0:T(1,128)S(1)} %copy-done.9, f32[1,2,2048]{2,1,0:T(2,128)S(1)} %copy-done.7, f32[1,2,2048]{2,1,0:T(2,128)S(1)} %copy-done.8), custom_call_target="tpu_custom_call" | custom-call | flops 100000000 | tf_op jit(solution)/shard_map/pallas_call | solution.py:420
  20.5 0.0 collective-permute-done.2.refs_3_
  20.5 0.0 collective-permute-done.3.refs_4_
  20.5 0.0 collective-permute-done.4.refs_5_
  20.5 0.0 collective-permute-done.5.refs_6_
  20.6 0.0 collective-permute-done.6.refs_7_
  20.6 0.0 copy-start.4
  20.6 0.7 %copy-done.4 = f32[24,24]{1,0:T(8,128)S(1)} copy-done((f32[24,24]{1,0:T(8,128)S(1)}, f32[24,24]{1,0:T(8,128)}, u32[]{:S(2)}) %copy-start.4) | copy-done | bytes 2328
  21.3 0.0 copy-start.5
  21.3 0.7 %copy-done.5 = f32[1,24]{1,0:T(1,128)S(1)} copy-done((f32[1,24]{1,0:T(1,128)S(1)}, f32[1,24]{1,0:T(1,128)}, u32[]{:S(2)}) %copy-start.5) | copy-done | bytes 120
  21.9 2.5 %shard_map.93 = (f32[8,128]{1,0:T(8,128)S(1)}, f32[8,128]{1,0:T(8,128)S(1)}, f32[8,128]{1,0:T(8,128)S(1)}, f32[8,128]{1,0:T(8,128)S(1)}, f32[8,128]{1,0:T(8,128)...) custom-call(f32[8,128]{1,0:T(8,128)S(1)} %get-tuple-element.24.refs_0_, ...), custom_call_target="tpu_custom_call" | custom-call | tf_op jit(solution)/shard_map/pallas_call | solution.py:420
  24.4 0.7 %collective-permute-start.7 = (f32[8,128]{1,0:T(8,128)S(1)}, f32[8,128]{1,0:T(8,128)S(1)}, u32[]{:S(2)}, u32[]{:S(2)}) collective-permute-start(f32[8,128]{1,0:T(8,128)S(1)} %get-tuple-element.36), channel_id=1, source_target_pairs={{0,4},{4,8},{8,12},{12,16},{16,20},{20,24},{24,28},{28,0},{1,5},{5... | collective-permute-start | bytes 12296 | tf_op jit(solution)/shard_map/ppermute | solution.py:435
  25.1 0.7 %collective-permute-start.8 = (f32[8,128]{1,0:T(8,128)S(1)}, f32[8,128]{1,0:T(8,128)S(1)}, u32[]{:S(2)}, u32[]{:S(2)}) collective-permute-start(f32[8,128]{1,0:T(8,128)S(1)} %get-tuple-element.37), channel_id=1, source_target_pairs={{0,8},{4,12},{8,16},{12,20},{16,24},{20,28},{24,0},{28,4},{1,9},{5... | collective-permute-start | bytes 12296 | tf_op jit(solution)/shard_map/ppermute | solution.py:435
  25.8 1.2 %collective-permute-start.9 = (f32[8,128]{1,0:T(8,128)S(1)}, f32[8,128]{1,0:T(8,128)S(1)}, u32[]{:S(2)}, u32[]{:S(2)}) collective-permute-start(f32[8,128]{1,0:T(8,128)S(1)} %get-tuple-element.38), channel_id=1, source_target_pairs={{0,12},{4,16},{8,20},{12,24},{16,28},{20,0},{24,4},{28,8},{1,13},{... | collective-permute-start | bytes 12296 | tf_op jit(solution)/shard_map/ppermute | solution.py:435
  27.0 3.5 %collective-permute-start.10 = (f32[8,128]{1,0:T(8,128)S(1)}, f32[8,128]{1,0:T(8,128)S(1)}, u32[]{:S(2)}, u32[]{:S(2)}) collective-permute-start(f32[8,128]{1,0:T(8,128)S(1)} %get-tuple-element.39), channel_id=1, source_target_pairs={{0,16},{4,20},{8,24},{12,28},{16,0},{20,4},{24,8},{28,12},{1,17},{... | collective-permute-start | bytes 12296 | tf_op jit(solution)/shard_map/ppermute | solution.py:435
  30.5 1.0 %collective-permute-start.11 = (f32[8,128]{1,0:T(8,128)S(1)}, f32[8,128]{1,0:T(8,128)S(1)}, u32[]{:S(2)}, u32[]{:S(2)}) collective-permute-start(f32[8,128]{1,0:T(8,128)S(1)} %get-tuple-element.40), channel_id=1, source_target_pairs={{0,20},{4,24},{8,28},{12,0},{16,4},{20,8},{24,12},{28,16},{1,21},{... | collective-permute-start | bytes 12296 | tf_op jit(solution)/shard_map/ppermute | solution.py:435
  31.4 0.0 collective-permute-done.7.refs_1_
  31.4 1.4 %collective-permute-start.12 = (f32[8,128]{1,0:T(8,128)S(1)}, f32[8,128]{1,0:T(8,128)S(1)}, u32[]{:S(2)}, u32[]{:S(2)}) collective-permute-start(f32[8,128]{1,0:T(8,128)S(1)} %get-tuple-element.41), channel_id=1, source_target_pairs={{0,24},{4,28},{8,0},{12,4},{16,8},{20,12},{24,16},{28,20},{1,25},{... | collective-permute-start | bytes 12296 | tf_op jit(solution)/shard_map/ppermute | solution.py:435
  32.8 0.0 collective-permute-done.8.refs_2_
  32.8 1.6 %collective-permute-start.13 = (f32[8,128]{1,0:T(8,128)S(1)}, f32[8,128]{1,0:T(8,128)S(1)}, u32[]{:S(2)}, u32[]{:S(2)}) collective-permute-start(f32[8,128]{1,0:T(8,128)S(1)} %get-tuple-element.42), channel_id=1, source_target_pairs={{0,28},{4,0},{8,4},{12,8},{16,12},{20,16},{24,20},{28,24},{1,29},{... | collective-permute-start | bytes 12296 | tf_op jit(solution)/shard_map/ppermute | solution.py:435
  34.4 0.0 collective-permute-done.9.refs_3_
  34.4 0.0 collective-permute-done.10.refs_4_
  34.4 0.5 %collective-permute-done.11.refs_5_ = f32[8,128]{1,0:T(8,128)S(1)} collective-permute-done((f32[8,128]{1,0:T(8,128)S(1)}, f32[8,128]{1,0:T(8,128)S(1)}, u32[]{:S(2)}, u32[]{:S(2)}) %collective-permute-start.11) | collective-permute-done | bytes 4128 | tf_op jit(solution)/shard_map/ppermute | solution.py:435
  35.0 0.1 collective-permute-done.12.refs_6_
  35.0 1.4 %collective-permute-done.13.refs_7_ = f32[8,128]{1,0:T(8,128)S(1)} collective-permute-done((f32[8,128]{1,0:T(8,128)S(1)}, f32[8,128]{1,0:T(8,128)S(1)}, u32[]{:S(2)}, u32[]{:S(2)}) %collective-permute-start.13) | collective-permute-done | bytes 4128 | tf_op jit(solution)/shard_map/ppermute | solution.py:435
  36.5 0.1 collective-permute-start.16
  36.5 1.6 %collective-permute-start.15 = (f32[8,8,128]{2,1,0:T(8,128)S(1)}, f32[8,8,128]{2,1,0:T(8,128)S(1)}, u32[]{:S(2)}, u32[]{:S(2)}) collective-permute-start(f32[8,8,128]{2,1,0:T(8,128)S(1)} %shard_map.94.refs_0_), channel_id=1, source_target_pairs={{0,2},{1,3},{2,0},{3,1},{4,6},{5,7},{6,4},{7,5},{8,10},{9,11},{10,... | collective-permute-start | bytes 98312 | tf_op jit(solution)/shard_map/ppermute | solution.py:435
  38.1 0.2 collective-permute-start.14
  38.2 0.0 collective-permute-done.16.refs_3_
  38.2 2.3 %collective-permute-done.15.refs_2_ = f32[8,8,128]{2,1,0:T(8,128)S(1)} collective-permute-done((f32[8,8,128]{2,1,0:T(8,128)S(1)}, f32[8,8,128]{2,1,0:T(8,128)S(1)}, u32[]{:S(2)}, u32[]{:S(2)}) %collective-permute-start.15) | collective-permute-done | bytes 32800 | tf_op jit(solution)/shard_map/ppermute | solution.py:435
  40.6 0.8 %collective-permute-done.14.refs_1_ = f32[8,8,128]{2,1,0:T(8,128)S(1)} collective-permute-done((f32[8,8,128]{2,1,0:T(8,128)S(1)}, f32[8,8,128]{2,1,0:T(8,128)S(1)}, u32[]{:S(2)}, u32[]{:S(2)}) %collective-permute-start.14) | collective-permute-done | bytes 32800 | tf_op jit(solution)/shard_map/ppermute | solution.py:435
  41.4 0.0 copy-done.1
  41.4 0.0 copy-done.3
  41.4 1.7 %shard_map.95 = f32[24,4096]{1,0:T(8,128)} custom-call(f32[8,8,128]{2,1,0:T(8,128)S(1)} %shard_map.94.refs_0_, f32[8,8,128]{2,1,0:T(8,128)S(1)} %collective-permute-done.14.refs_1_, f32[8,8,128]{2,1,0:T(8,128)S(1)} %collective-permute-done.15.refs_2_, f32[8,8,128]{2,1,0:T(8,128)S(1)} %collective-permute-done.16.refs_3_, s32[4,1,8,32]{3,2,1,0:T(8,128)S(1)} %copy-done.2, ...), custom_call_target="tpu_custom_call" | custom-call | tf_op jit(solution)/shard_map/pallas_call | solution.py:420
  (1 shorter events, 0.0 us)
Async XLA Ops:
  0.0 1.0 %copy-start = (f32[24,4096]{1,0:T(8,128)S(1)}, f32[24,4096]{1,0:T(8,128)}, u32[]{:S(2)}) copy-start(f32[24,4096]{1,0:T(8,128)} %refs_5_.1) | copy-start | bytes 1179652
  1.0 0.7 %copy-start.2 = (s32[4,1,8,32]{3,2,1,0:T(8,128)S(1)}, s32[4,1,8,32]{3,2,1,0:T(8,128)}, u32[]{:S(2)}) copy-start(s32[4,1,8,32]{3,2,1,0:T(8,128)} %refs_4_.1) | copy-start | bytes 12292
  1.7 39.7 %copy-start.1 = (f32[24,4096]{1,0:T(8,128)S(1)}, f32[24,4096]{1,0:T(8,128)}, u32[]{:S(2)}) copy-start(f32[24,4096]{1,0:T(8,128)} %refs_5_.1) | copy-start | bytes 1179652
  1.7 39.7 %copy-start.3 = (f32[4096]{0:T(1024)S(1)}, f32[4096]{0:T(1024)}, u32[]{:S(2)}) copy-start(f32[4096]{0:T(1024)} %param.10) | copy-start | bytes 49156
  2.5 11.0 %collective-permute-start = (f32[8,128]{1,0:T(8,128)S(1)}, f32[8,128]{1,0:T(8,128)S(1)}, u32[]{:S(2)}, u32[]{:S(2)}) collective-permute-start(f32[8,128]{1,0:T(8,128)S(1)} %get-tuple-element.25), channel_id=1, source_target_pairs={{0,4},{4,8},{8,12},{12,16},{16,20},{20,24},{24,28},{28,0},{1,5},{5... | collective-permute-start | bytes 12296 | tf_op jit(solution)/shard_map/ppermute | solution.py:435
  5.5 9.4 %collective-permute-start.1 = (f32[8,128]{1,0:T(8,128)S(1)}, f32[8,128]{1,0:T(8,128)S(1)}, u32[]{:S(2)}, u32[]{:S(2)}) collective-permute-start(f32[8,128]{1,0:T(8,128)S(1)} %get-tuple-element.26), channel_id=1, source_target_pairs={{0,8},{4,12},{8,16},{12,20},{16,24},{20,28},{24,0},{28,4},{1,9},{5... | collective-permute-start | bytes 12296 | tf_op jit(solution)/shard_map/ppermute | solution.py:435
  7.1 13.5 %collective-permute-start.2 = (f32[8,128]{1,0:T(8,128)S(1)}, f32[8,128]{1,0:T(8,128)S(1)}, u32[]{:S(2)}, u32[]{:S(2)}) collective-permute-start(f32[8,128]{1,0:T(8,128)S(1)} %get-tuple-element.27), channel_id=1, source_target_pairs={{0,12},{4,16},{8,20},{12,24},{16,28},{20,0},{24,4},{28,8},{1,13},{... | collective-permute-start | bytes 12296 | tf_op jit(solution)/shard_map/ppermute | solution.py:435
  9.6 10.9 %collective-permute-start.3 = (f32[8,128]{1,0:T(8,128)S(1)}, f32[8,128]{1,0:T(8,128)S(1)}, u32[]{:S(2)}, u32[]{:S(2)}) collective-permute-start(f32[8,128]{1,0:T(8,128)S(1)} %get-tuple-element.28), channel_id=1, source_target_pairs={{0,16},{4,20},{8,24},{12,28},{16,0},{20,4},{24,8},{28,12},{1,17},{... | collective-permute-start | bytes 12296 | tf_op jit(solution)/shard_map/ppermute | solution.py:435
  10.8 9.7 %collective-permute-start.4 = (f32[8,128]{1,0:T(8,128)S(1)}, f32[8,128]{1,0:T(8,128)S(1)}, u32[]{:S(2)}, u32[]{:S(2)}) collective-permute-start(f32[8,128]{1,0:T(8,128)S(1)} %get-tuple-element.29), channel_id=1, source_target_pairs={{0,20},{4,24},{8,28},{12,0},{16,4},{20,8},{24,12},{28,16},{1,21},{... | collective-permute-start | bytes 12296 | tf_op jit(solution)/shard_map/ppermute | solution.py:435
  13.5 7.1 %collective-permute-start.5 = (f32[8,128]{1,0:T(8,128)S(1)}, f32[8,128]{1,0:T(8,128)S(1)}, u32[]{:S(2)}, u32[]{:S(2)}) collective-permute-start(f32[8,128]{1,0:T(8,128)S(1)} %get-tuple-element.30), channel_id=1, source_target_pairs={{0,24},{4,28},{8,0},{12,4},{16,8},{20,12},{24,16},{28,20},{1,25},{... | collective-permute-start | bytes 12296 | tf_op jit(solution)/shard_map/ppermute | solution.py:435
  14.8 5.7 %collective-permute-start.6 = (f32[8,128]{1,0:T(8,128)S(1)}, f32[8,128]{1,0:T(8,128)S(1)}, u32[]{:S(2)}, u32[]{:S(2)}) collective-permute-start(f32[8,128]{1,0:T(8,128)S(1)} %get-tuple-element.31), channel_id=1, source_target_pairs={{0,28},{4,0},{8,4},{12,8},{16,12},{20,16},{24,20},{28,24},{1,29},{... | collective-permute-start | bytes 12296 | tf_op jit(solution)/shard_map/ppermute | solution.py:435
  16.2 0.7 %copy-start.6 = (s32[1,2,2048]{2,1,0:T(2,128)S(1)}, s32[1,2,2048]{2,1,0:T(2,128)}, u32[]{:S(2)}) copy-start(s32[1,2,2048]{2,1,0:T(2,128)} %slot_ref.1) | copy-start | bytes 49156
  17.0 0.7 %copy-start.7 = (f32[1,2,2048]{2,1,0:T(2,128)S(1)}, f32[1,2,2048]{2,1,0:T(2,128)}, u32[]{:S(2)}) copy-start(f32[1,2,2048]{2,1,0:T(2,128)} %courant_ref.1) | copy-start | bytes 49156
  17.7 0.7 %copy-start.8 = (f32[1,2,2048]{2,1,0:T(2,128)S(1)}, f32[1,2,2048]{2,1,0:T(2,128)}, u32[]{:S(2)}) copy-start(f32[1,2,2048]{2,1,0:T(2,128)} %flux_ref.1) | copy-start | bytes 49156
  18.4 0.7 %copy-start.9 = (s32[1,2]{1,0:T(1,128)S(1)}, s32[1,2]{1,0:T(1,128)}, u32[]{:S(2)}) copy-start(s32[1,2]{1,0:T(1,128)} %length_ref.1) | copy-start | bytes 28
  20.6 0.7 %copy-start.4 = (f32[24,24]{1,0:T(8,128)S(1)}, f32[24,24]{1,0:T(8,128)}, u32[]{:S(2)}) copy-start(f32[24,24]{1,0:T(8,128)} %refs_11_.1) | copy-start | bytes 6916
  21.3 0.7 %copy-start.5 = (f32[1,24]{1,0:T(1,128)S(1)}, f32[1,24]{1,0:T(1,128)}, u32[]{:S(2)}) copy-start(f32[1,24]{1,0:T(1,128)} %refs_10_.1) | copy-start | bytes 292
  24.4 7.0 %collective-permute-start.7 = (f32[8,128]{1,0:T(8,128)S(1)}, f32[8,128]{1,0:T(8,128)S(1)}, u32[]{:S(2)}, u32[]{:S(2)}) collective-permute-start(f32[8,128]{1,0:T(8,128)S(1)} %get-tuple-element.36), channel_id=1, source_target_pairs={{0,4},{4,8},{8,12},{12,16},{16,20},{20,24},{24,28},{28,0},{1,5},{5... | collective-permute-start | bytes 12296 | tf_op jit(solution)/shard_map/ppermute | solution.py:435
  25.1 7.7 %collective-permute-start.8 = (f32[8,128]{1,0:T(8,128)S(1)}, f32[8,128]{1,0:T(8,128)S(1)}, u32[]{:S(2)}, u32[]{:S(2)}) collective-permute-start(f32[8,128]{1,0:T(8,128)S(1)} %get-tuple-element.37), channel_id=1, source_target_pairs={{0,8},{4,12},{8,16},{12,20},{16,24},{20,28},{24,0},{28,4},{1,9},{5... | collective-permute-start | bytes 12296 | tf_op jit(solution)/shard_map/ppermute | solution.py:435
  25.8 8.6 %collective-permute-start.9 = (f32[8,128]{1,0:T(8,128)S(1)}, f32[8,128]{1,0:T(8,128)S(1)}, u32[]{:S(2)}, u32[]{:S(2)}) collective-permute-start(f32[8,128]{1,0:T(8,128)S(1)} %get-tuple-element.38), channel_id=1, source_target_pairs={{0,12},{4,16},{8,20},{12,24},{16,28},{20,0},{24,4},{28,8},{1,13},{... | collective-permute-start | bytes 12296 | tf_op jit(solution)/shard_map/ppermute | solution.py:435
  27.0 7.4 %collective-permute-start.10 = (f32[8,128]{1,0:T(8,128)S(1)}, f32[8,128]{1,0:T(8,128)S(1)}, u32[]{:S(2)}, u32[]{:S(2)}) collective-permute-start(f32[8,128]{1,0:T(8,128)S(1)} %get-tuple-element.39), channel_id=1, source_target_pairs={{0,16},{4,20},{8,24},{12,28},{16,0},{20,4},{24,8},{28,12},{1,17},{... | collective-permute-start | bytes 12296 | tf_op jit(solution)/shard_map/ppermute | solution.py:435
  30.5 4.5 %collective-permute-start.11 = (f32[8,128]{1,0:T(8,128)S(1)}, f32[8,128]{1,0:T(8,128)S(1)}, u32[]{:S(2)}, u32[]{:S(2)}) collective-permute-start(f32[8,128]{1,0:T(8,128)S(1)} %get-tuple-element.40), channel_id=1, source_target_pairs={{0,20},{4,24},{8,28},{12,0},{16,4},{20,8},{24,12},{28,16},{1,21},{... | collective-permute-start | bytes 12296 | tf_op jit(solution)/shard_map/ppermute | solution.py:435
  31.4 3.6 %collective-permute-start.12 = (f32[8,128]{1,0:T(8,128)S(1)}, f32[8,128]{1,0:T(8,128)S(1)}, u32[]{:S(2)}, u32[]{:S(2)}) collective-permute-start(f32[8,128]{1,0:T(8,128)S(1)} %get-tuple-element.41), channel_id=1, source_target_pairs={{0,24},{4,28},{8,0},{12,4},{16,8},{20,12},{24,16},{28,20},{1,25},{... | collective-permute-start | bytes 12296 | tf_op jit(solution)/shard_map/ppermute | solution.py:435
  32.8 3.6 %collective-permute-start.13 = (f32[8,128]{1,0:T(8,128)S(1)}, f32[8,128]{1,0:T(8,128)S(1)}, u32[]{:S(2)}, u32[]{:S(2)}) collective-permute-start(f32[8,128]{1,0:T(8,128)S(1)} %get-tuple-element.42), channel_id=1, source_target_pairs={{0,28},{4,0},{8,4},{12,8},{16,12},{20,16},{24,20},{28,24},{1,29},{... | collective-permute-start | bytes 12296 | tf_op jit(solution)/shard_map/ppermute | solution.py:435
  36.5 1.8 %collective-permute-start.16 = (f32[8,8,128]{2,1,0:T(8,128)S(1)}, f32[8,8,128]{2,1,0:T(8,128)S(1)}, u32[]{:S(2)}, u32[]{:S(2)}) collective-permute-start(f32[8,8,128]{2,1,0:T(8,128)S(1)} %shard_map.94.refs_0_), channel_id=1, source_target_pairs={{0,3},{1,0},{2,1},{3,2},{4,7},{5,4},{6,5},{7,6},{8,11},{9,8},{10,9... | collective-permute-start | bytes 98312 | tf_op jit(solution)/shard_map/ppermute | solution.py:435
  36.5 4.1 %collective-permute-start.15 = (f32[8,8,128]{2,1,0:T(8,128)S(1)}, f32[8,8,128]{2,1,0:T(8,128)S(1)}, u32[]{:S(2)}, u32[]{:S(2)}) collective-permute-start(f32[8,8,128]{2,1,0:T(8,128)S(1)} %shard_map.94.refs_0_), channel_id=1, source_target_pairs={{0,2},{1,3},{2,0},{3,1},{4,6},{5,7},{6,4},{7,5},{8,10},{9,11},{10,... | collective-permute-start | bytes 98312 | tf_op jit(solution)/shard_map/ppermute | solution.py:435
  38.1 3.3 %collective-permute-start.14 = (f32[8,8,128]{2,1,0:T(8,128)S(1)}, f32[8,8,128]{2,1,0:T(8,128)S(1)}, u32[]{:S(2)}, u32[]{:S(2)}) collective-permute-start(f32[8,8,128]{2,1,0:T(8,128)S(1)} %shard_map.94.refs_0_), channel_id=1, source_target_pairs={{0,1},{1,2},{2,3},{3,0},{4,5},{5,6},{6,7},{7,4},{8,9},{9,10},{10,1... | collective-permute-start | bytes 98312 | tf_op jit(solution)/shard_map/ppermute | solution.py:435

commit v4 on v3

--- a/solution.py
+++ b/solution.py
@@ -14,7 +14,7 @@
 F32 = jnp.float32
 BF16 = jnp.bfloat16
 VMEM_BYTES = 32 * 1024 * 1024
-DIRECT = 16
+WHOLE_BYTES = 63_000_000
 
 
 def repeat_steps(count, body, carry):
@@ -52,8 +52,7 @@
     return jnp.sum(jnp.where(rows == lanes, wide, 0), axis=0, keepdims=True)
 
 
-def pick_kernel(cell_hbm, request_hbm, *refs):
-    *out_refs, cell_ref, request_ref, tile_ref, cell_sem, request_sem = refs
+def pick_kernel(cell_hbm, request_hbm, out_ref, cell_ref, request_ref, cell_sem, request_sem):
     request_copy = pltpu.make_async_copy(
         request_hbm.at[lax.axis_index("bundle"), 0], request_ref, request_sem
     )
@@ -84,8 +83,6 @@
         [cell[:, LANES * h : LANES * (h + 1)] for h in range(highs)], axis=0
     )
     left = jnp.concatenate(split(stacked), axis=1)
-    direct = len(out_refs) > 1
-    into = tile_ref if direct else out_refs[0]
 
     def chunk(k, carry):
         first = k * 2 * groups
@@ -105,14 +102,10 @@
                 cap,
             )
             for j in range(groups):
-                into[first + half * groups + j] = tiles[j]
+                out_ref[first + half * groups + j] = tiles[j]
         return carry
 
     repeat_steps(chunks, chunk, 0)
-    if direct:
-        here = lax.axis_index("grid")
-        for j in range(owners):
-            out_refs[j][...] = tile_ref[lax.rem(here + j, owners)]
 
 
 def to_segments(refs):
@@ -170,7 +163,9 @@
         return jnp.where(self.part >= minor, near, far)
 
 
-def prepare_kernel(slot_ref, length_ref, courant_ref, flux_ref, rows_ref, jump_ref, *hot_refs):
+def prepare_kernel(
+    slot_ref, length_ref, courant_ref, flux_ref, after_ref, rows_ref, jump_ref, *hot_refs
+):
     lines, nodes = slot_ref.shape[1:]
     places = Places(lines, nodes)
     times = places.times
@@ -213,20 +208,10 @@
         hot_ref[...] = one_hot(slot, 0)
 
 
-def lines_kernel(lines, cap, tables, kept, *refs):
-    table_refs, refs = refs[:tables], refs[tables:]
-    rows_ref, jump_ref, inflow_ref, interaction_ref = refs[:4]
-    refs = refs[4:]
-    hot_ref, refs = (refs[0], refs[1:]) if kept else (None, refs)
-    *out_refs, tile_ref = refs
-    direct = tables > 1
+def lines_kernel(lines, cap, table_ref, rows_ref, jump_ref, inflow_ref, interaction_ref, *refs):
+    *hot_refs, out_ref = refs
+    owners, copies = out_ref.shape[:2]
     all_groups = LANES // cap
-    owners = tables if direct else table_refs[0].shape[0]
-    here = lax.axis_index("grid")
-    if direct:
-        for j in range(owners):
-            tile_ref[lax.rem(here + (owners - j), owners)] = table_refs[j][...]
-    table_ref = tile_ref if direct else table_refs[0]
     species = inflow_ref.shape[1]
     times = rows_ref.shape[1]
     nodes = times * LANES // lines
@@ -237,7 +222,7 @@
     chunks = owners // chunk_owners
 
     def hot(k):
-        return hot_ref[...] if kept else one_hot(rows_ref[5], k)
+        return hot_refs[0][...] if hot_refs else one_hot(rows_ref[5], k)
 
     def gather(k, state):
         halves = []
@@ -322,7 +307,6 @@
     scaled = [iterate[ROWS * g : ROWS * (g + 1)] * weight for g in range(groups)]
     scaled.append(jnp.where(first_row, weight, 0.0))
     left = jnp.concatenate(split(jnp.concatenate(scaled, axis=0)), axis=0)
-    into = tile_ref if direct else out_refs[0]
 
     def scatter(k, carry):
         sums = lax.dot_general(
@@ -338,20 +322,44 @@
                 cap,
             )
             for j in range(all_groups):
-                into[k * chunk_owners + half * all_groups + j] = tiles[j]
+                for copy in range(copies):
+                    out_ref[k * chunk_owners + half * all_groups + j, copy] = tiles[j]
         return carry
 
     repeat_steps(chunks, scatter, 0)
-    if direct:
-        for j in range(owners):
-            out_refs[j][...] = tile_ref[lax.rem(here + j, owners)]
-
-
-def blend_kernel(bundles, *refs):
-    sums_refs, refs = refs[:bundles], refs[bundles:]
-    request_ref, cell_ref, pore_ref, out_ref = refs
-    owners = sums_refs[0].shape[0]
-    bundle_here = lax.axis_index("bundle")
+
+
+def blend_entries(request_ref, k):
+    bundles, cap = request_ref.shape[0], request_ref.shape[3]
+    groups = LANES // cap
+    pieces = []
+    for t in range(bundles // groups):
+        block = jnp.concatenate(
+            [request_ref[t * groups + j, 0, pl.ds(k * ROWS, ROWS), :] for j in range(groups)],
+            axis=1,
+        )
+        pieces += [block[d : d + 1] for d in range(ROWS)]
+    return jnp.concatenate(pieces, axis=1)
+
+
+def blend_index(request_ref, k):
+    width = 2 * LANES
+    index = blend_entries(request_ref, k)
+    entries = index.shape[1]
+    high = jnp.broadcast_to(index // width, (2 * ROWS, entries)).astype(F32).astype(BF16)
+    low = jnp.broadcast_to(index % width, (2 * ROWS, entries)).astype(F32).astype(BF16)
+    place = lax.broadcasted_iota(jnp.int32, (width, entries), 0).astype(F32).astype(BF16)
+    low = jnp.concatenate([low] * (width // (2 * ROWS)), axis=0)
+    return high, jnp.where(place == low, jnp.ones_like(place), jnp.zeros_like(place))
+
+
+def index_kernel(request_ref, after_ref, high_ref, hot_ref):
+    high_ref[...], hot_ref[...] = blend_index(request_ref, 0)
+
+
+def blend_kernel(sums_ref, request_ref, pore_ref, cell_ref, *refs):
+    *kept_refs, out_hbm, out_ref, out_sem = refs
+    owners, bundles = sums_ref.shape[:2]
     species, cells = cell_ref.shape
     cap = request_ref.shape[3]
     groups = LANES // cap
@@ -359,37 +367,20 @@
     width = 2 * LANES
     highs = cells // width
     chunks = owners // ROWS
-    tiles_each = bundles // groups
 
     def chunk(k, total):
-        values, indices = [], []
-        for t in range(tiles_each):
-            block = jnp.concatenate(
-                [
-                    request_ref[
-                        lax.rem(bundle_here + (bundles - t * groups - j), bundles),
-                        0,
-                        pl.ds(k * ROWS, ROWS),
-                        :,
-                    ]
-                    for j in range(groups)
-                ],
-                axis=1,
-            )
+        values = []
+        for t in range(bundles // groups):
             for d in range(ROWS):
                 tiles = exchange_groups(
-                    [sums_refs[t * groups + j][k * ROWS + d] for j in range(groups)], cap
+                    [sums_ref[k * ROWS + d, t * groups + j] for j in range(groups)], cap
                 )
                 values.append(jnp.concatenate(tiles, axis=0))
-                indices.append(block[d : d + 1])
         value = jnp.concatenate(values, axis=1)
-        index = jnp.concatenate(indices, axis=1)
-        entries = index.shape[1]
-        low = index % width
-        high = jnp.broadcast_to(index // width, (2 * ROWS, entries)).astype(F32).astype(BF16)
-        hot = (
-            (lax.broadcasted_iota(jnp.int32, (width, entries), 0) == low).astype(F32).astype(BF16)
-        )
+        if kept_refs:
+            high, hot = kept_refs[0][...], kept_refs[1][...]
+        else:
+            high, hot = blend_index(request_ref, k)
         parts = jnp.concatenate(split(value), axis=0)
         pieces = []
         for h in range(highs):
@@ -406,47 +397,38 @@
     total = repeat_steps(
         chunks, chunk, jnp.zeros((highs * 2 * rows, width), F32) if chunks > 1 else 0
     )
+    copies = []
     for h in range(highs):
         part = total[2 * rows * h : 2 * rows * (h + 1)]
         part = part[:rows] + part[rows:]
         pore = pore_ref[:, width * h : width * (h + 1)]
         scale = pore + part[species : species + 1]
-        columns = slice(width * h, width * (h + 1))
+        columns = pl.ds(width * h, width)
         out_ref[:, columns] = (pore * cell_ref[:, columns] + part[:species]) / scale
-
-
-def call(kernel, shapes, operands, smem=(), hbm=(), scratch=(), flops=0):
-    kinds = {i: pltpu.SMEM for i in smem} | {i: pltpu.HBM for i in hbm}
+        if h % 4 == 3:
+            columns = pl.ds(width * (h - 3), 4 * width)
+            copies.append(
+                pltpu.make_async_copy(
+                    out_ref.at[:, columns], out_hbm.at[:, columns], out_sem.at[h // 4]
+                )
+            )
+            copies[-1].start()
+    for copy in copies:
+        copy.wait()
+
+
+def call(kernel, shapes, operands, kinds={}, scratch=(), flops=0, grant=VMEM_BYTES, out=pltpu.VMEM):
     return pl.pallas_call(
         kernel,
         out_shape=[jax.ShapeDtypeStruct(shape, kind) for shape, kind in shapes],
         in_specs=[
             pl.BlockSpec(memory_space=kinds.get(i, pltpu.VMEM)) for i in range(len(operands))
         ],
-        out_specs=[pl.BlockSpec(memory_space=pltpu.VMEM)] * len(shapes),
+        out_specs=[pl.BlockSpec(memory_space=out)] * len(shapes),
         scratch_shapes=list(scratch),
-        compiler_params=pltpu.CompilerParams(vmem_limit_bytes=VMEM_BYTES),
+        compiler_params=pltpu.CompilerParams(vmem_limit_bytes=grant),
         cost_estimate=pl.CostEstimate(flops=flops, bytes_accessed=0, transcendentals=0),
     )(*operands)
-
-
-def send_around(tiles, axis, count):
-    return [tiles[0]] + [
-        lax.ppermute(tiles[j], axis, [(i, (i + j) % count) for i in range(count)])
-        for j in range(1, count)
-    ]
-
-
-def order_kernel(*refs):
-    *tile_refs, out_ref = refs
-    count = len(tile_refs)
-    here = lax.axis_index("grid")
-    for j in range(count):
-        out_ref[lax.rem(here + (count - j), count)] = tile_refs[j][...]
-
-
-def by_owner(tiles):
-    return call(order_kernel, [((len(tiles), *tiles[0].shape), F32)], tiles)[0]
 
 
 def shards(
@@ -464,55 +446,57 @@
     owners, cap = request_cell.shape[2:]
     lines, nodes = node_slot.shape[1:]
     times = lines * nodes // LANES
-    direct = owners <= DIRECT
-    kept = owners * cap == 2 * LANES
+    cells = cell_state.shape[1]
     tile = (ROWS, LANES)
-    shapes = [(tile, F32)] * owners if direct else [((owners, *tile), F32)]
-    tiles_scratch = pltpu.VMEM((owners, *tile) if direct else (1, *tile), F32)
-
-    def over_grid(tiles):
-        if direct:
-            return send_around(tiles, "grid", owners)
-        return [lax.all_to_all(tiles[0], "grid", split_axis=0, concat_axis=0, tiled=True)]
-
     outgoing = call(
         pick_kernel,
-        shapes,
+        [((owners, *tile), F32)],
         (cell_state, request_cell),
-        hbm=(0, 1),
+        kinds={0: pltpu.HBM, 1: pltpu.HBM},
         scratch=(
             pltpu.VMEM(cell_state.shape, F32),
             pltpu.VMEM((owners, cap), jnp.int32),
-            tiles_scratch,
             pltpu.SemaphoreType.DMA,
             pltpu.SemaphoreType.DMA,
         ),
-    )
+        grant=WHOLE_BYTES,
+    )[0]
     jumps = 2
     while 2 ** (jumps // 2 - 1) < nodes // times:
         jumps += 2
     prepared = call(
         prepare_kernel,
         [((6, times, LANES), F32), ((jumps, ROWS, LANES), F32)]
-        + ([((2 * LANES, lines * nodes), BF16)] if kept else []),
-        (node_slot, line_length, courant, flux_weight),
-        smem=(1,),
-        flops=10**8,
-    )
-    tables = over_grid(outgoing)
+        + ([((2 * LANES, lines * nodes), BF16)] if owners * cap == 2 * LANES else []),
+        (node_slot, line_length, courant, flux_weight, outgoing),
+        kinds={1: pltpu.SMEM, 4: pl.ANY},
+        flops=10**9,
+    )
+    table = lax.all_to_all(outgoing, "grid", split_axis=0, concat_axis=0, tiled=True)
     sums = call(
-        functools.partial(lines_kernel, lines, cap, len(tables), kept),
-        shapes,
-        (*tables, *prepared[:2], inflow, interaction, *prepared[2:]),
-        scratch=(tiles_scratch,),
-    )
-    sums = over_grid(sums)
-    own = sums[0] if not direct else by_owner(sums)
-    every = send_around([own] * bundles, "bundle", bundles)
+        functools.partial(lines_kernel, lines, cap),
+        [((owners, bundles, *tile), F32)],
+        (table, *prepared[:2], inflow, interaction, *prepared[2:]),
+    )[0]
+    entries = bundles * ROWS * cap
+    indexed = []
+    if owners == ROWS:
+        indexed = call(
+            index_kernel,
+            [((2 * ROWS, entries), BF16), ((2 * LANES, entries), BF16)],
+            (request_cell, sums),
+            kinds={1: pl.ANY},
+            flops=10**9,
+        )
+    sums = sums.reshape(owners * bundles, *tile)
+    back = lax.all_to_all(sums, ("grid", "bundle"), split_axis=0, concat_axis=0, tiled=True)
+    back = back.reshape(owners, bundles, *tile)
     return call(
-        functools.partial(blend_kernel, bundles),
+        blend_kernel,
         [(cell_state.shape, F32)],
-        (*every, request_cell, cell_state, pore_volume[None, :]),
+        (back, request_cell, pore_volume[None, :], cell_state, *indexed),
+        scratch=(pltpu.VMEM(cell_state.shape, F32), pltpu.SemaphoreType.DMA((cells // (8 * LANES),))),
+        out=pltpu.HBM,
     )[0]
 
 

time: 43.8 us -> 34 us (0.78)
  starting transfers between devices: 25.5 us -> 11.7 us
  waiting for transfers between devices: 5.21 us -> 9.65 us
  local copies, waits for them, and re-layouts: 5.88 us -> 3.61 us
  Pallas kernels: 6.38 us -> 8.39 us
    ppermute x17 -> x0, starting transfers between devices: 25.5 us -> none  [send_around(): lax.ppermute(tiles[j], axis, [(i, (i + j) % count) for i in range(count)])]
    all_to_all x0 -> x2, starting transfers between devices: none -> 11.7 us  [the longest x1 7.29 us: shards(): lax.all_to_all(outgoing, 'grid', split_axis=0, concat_axis=0, tiled=True)]
    all_to_all x0 -> x2, waiting for transfers between devices: none -> 9.65 us  [the longest x1 8.05 us: shards(): lax.all_to_all(sums, ('grid', 'bundle'), split_axis=0, concat_axis=0, til...]
    ppermute x17 -> x0, waiting for transfers between devices: 5.21 us -> none  [send_around(): lax.ppermute(tiles[j], axis, [(i, (i + j) % count) for i in range(count)])]
    unnamed x20, local copies, waits for them, and re-layouts: 5.88 us -> 3.61 us
    pallas_call x5, Pallas kernels: 6.38 us -> 8.39 us  [call(): pl.pallas_call(kernel, out_shape=[jax.ShapeDtypeStruct(shape, kind) for s...]
  transfers between devices with their start and end apart: 17 -> 2, of which waited for: 5 -> 2; matrix products, arithmetic and copies ran while one was open for 0% -> 0% of each run, Pallas kernels for 3% -> 5%
where the time goes in v4:
time: 34 us; the launch traced here: 33.4 us
  starting transfers between devices  11.7 us (34%)
  waiting for transfers between devices  9.65 us (28%)
  Pallas kernels  8.39 us (25%)
  local copies, waits for them, and re-layouts  3.61 us (11%)
    pallas_call x5, Pallas kernels, call(): pl.pallas_call(kernel, out_shape=[jax.ShapeDtypeStruct(shape, kind) for s...  8.39 us
    all_to_all x1, waiting for transfers between devices, shards(): lax.all_to_all(sums, ('grid', 'bundle'), split_axis=0, concat_axis=0, til...  8.05 us
    all_to_all x1, starting transfers between devices, shards(): lax.all_to_all(outgoing, 'grid', split_axis=0, concat_axis=0, tiled=True)  7.29 us
    all_to_all x1, starting transfers between devices, shards(): lax.all_to_all(sums, ('grid', 'bundle'), split_axis=0, concat_axis=0, til...  4.43 us
    unnamed x20, local copies, waits for them, and re-layouts  3.61 us
    all_to_all x1, waiting for transfers between devices, shards(): lax.all_to_all(outgoing, 'grid', split_axis=0, concat_axis=0, tiled=True)  1.6 us
  transfers between devices with their start and end apart: 2, of which 2 were waited for; matrix products, arithmetic and copies ran while one was open for 0% of the time, Pallas kernels for 5%

profile of v4, /device:TPU:0, one launch (start us, length us, event | category | flops | bytes accessed | tf_op | source)
XLA Modules:
  0.0 33.4 jit_solution(9852261133414085159)
XLA Ops:
  0.0 0.0 copy-start.4
  0.0 0.0 copy-start.5
  0.0 2.1 %shard_map.91.after_ref = f32[8,8,128]{2,1,0:T(8,128)} custom-call(f32[24,4096]{1,0:T(8,128)} %cell_ref.1, s32[4,1,8,32]{3,2,1,0:T(8,128)} %request_ref.3), custom_call_target="tpu_custom_call" | custom-call | tf_op jit(solution)/shard_map/pallas_call | solution.py:421
  2.1 7.3 %all-to-all-start = ((f32[8,8,128]{2,1,0:T(8,128)}), f32[8,8,128]{2,1,0:T(8,128)S(1)}, u32[]{:S(2)}, u32[]{:S(2)}) async-start(f32[8,8,128]{2,1,0:T(8,128)} %shard_map.91.after_ref), calls=%async_computation | async-start | bytes 65536 | tf_op jit(solution)/shard_map/all_to_all | solution.py:475
  9.4 0.0 copy-start.1
  9.4 0.8 %copy-done.1 = f32[8,8,128]{2,1,0:T(8,128)S(1)} copy-done((f32[8,8,128]{2,1,0:T(8,128)S(1)}, f32[8,8,128]{2,1,0:T(8,128)}, u32[]{:S(2)}) %copy-start.1) | copy-done | bytes 32792
  10.2 0.0 copy-start.6
  10.2 0.7 %copy-done.6 = s32[1,2,2048]{2,1,0:T(2,128)S(1)} copy-done((s32[1,2,2048]{2,1,0:T(2,128)S(1)}, s32[1,2,2048]{2,1,0:T(2,128)}, u32[]{:S(2)}) %copy-start.6) | copy-done | bytes 16408
  10.9 0.0 copy-start.7
  10.9 0.7 %copy-done.7 = f32[1,2,2048]{2,1,0:T(2,128)S(1)} copy-done((f32[1,2,2048]{2,1,0:T(2,128)S(1)}, f32[1,2,2048]{2,1,0:T(2,128)}, u32[]{:S(2)}) %copy-start.7) | copy-done | bytes 16408
  11.6 0.0 copy-start.8
  11.6 0.7 %copy-done.8 = f32[1,2,2048]{2,1,0:T(2,128)S(1)} copy-done((f32[1,2,2048]{2,1,0:T(2,128)S(1)}, f32[1,2,2048]{2,1,0:T(2,128)}, u32[]{:S(2)}) %copy-start.8) | copy-done | bytes 16408
  12.3 0.0 copy-start.9
  12.3 0.7 %copy-done.9 = s32[1,2]{1,0:T(1,128)S(1)} copy-done((s32[1,2]{1,0:T(1,128)S(1)}, s32[1,2]{1,0:T(1,128)}, u32[]{:S(2)}) %copy-start.9) | copy-done | bytes 32
  13.0 1.5 %shard_map.92 = (f32[6,32,128]{2,1,0:T(8,128)S(1)}, f32[14,8,128]{2,1,0:T(8,128)S(1)}, bf16[256,4096]{1,0:T(8,128)(2,1)S(1)}) custom-call(s32[1,2,2048]{2,1,0:T(2,128)S(1)} %copy-done.6, s32[1,2]{1,0:T(1,128)S(1)} %copy-done.9, f32[1,2,2048]{2,1,0:T(2,128)S(1)} %copy-done.7, f32[1,2,2048]{2,1,0:T(2,128)S(1)} %copy-done.8, f32[8,8,128]{2,1,0:T(8,128)S(1)} %copy-done.1), custom_call_target="tpu_custom_call" | custom-call | flops 1000000000 | tf_op jit(solution)/shard_map/pallas_call | solution.py:421
  14.5 0.0 copy-start.2
  14.5 1.6 %all-to-all-done.table_ref = f32[8,8,128]{2,1,0:T(8,128)S(1)} async-done(((f32[8,8,128]{2,1,0:T(8,128)}), f32[8,8,128]{2,1,0:T(8,128)S(1)}, u32[]{:S(2)}, u32[]{:S(2)}) %all-to-all-start) | async-done | bytes 32800 | tf_op jit(solution)/shard_map/all_to_all | solution.py:475
  16.1 0.0 copy-done.4
  16.1 0.0 copy-done.5
  16.1 3.1 %shard_map.93.after_ref = f32[8,4,8,128]{3,2,1,0:T(8,128)} custom-call(f32[8,8,128]{2,1,0:T(8,128)S(1)} %all-to-all-done.table_ref, f32[6,32,128]{2,1,0:T(8,128)S(1)} %get-tuple-element.10.rows_ref, f32[14,8,128]{2,1,0:T(8,128)S(1)} %get-tuple-element.11.jump_ref, f32[1,24]{1,0:T(1,128)S(1)} %copy-done.5, f32[24,24]{1,0:T(8,128)S(1)} %copy-done.4, ...), custom_call_target="tpu_custom_call" | custom-call | tf_op jit(solution)/shard_map/pallas_call | solution.py:421
  19.2 0.0 copy-start
  19.2 0.0 copy-start.3
  19.2 4.4 %all-to-all-start.1 = ((f32[32,8,128]{2,1,0:T(8,128)}), f32[32,8,128]{2,1,0:T(8,128)S(1)}, u32[]{:S(2)}, u32[]{:S(2)}) async-start(f32[32,8,128]{2,1,0:T(8,128)} %bitcast), calls=%async_computation.1 | async-start | bytes 262144 | tf_op jit(solution)/shard_map/all_to_all | solution.py:492
  23.6 0.0 copy-done.2
  23.6 0.2 shard_map.94
  23.8 8.0 %all-to-all-done.1 = f32[32,8,128]{2,1,0:T(8,128)S(1)} async-done(((f32[32,8,128]{2,1,0:T(8,128)}), f32[32,8,128]{2,1,0:T(8,128)S(1)}, u32[]{:S(2)}, u32[]{:S(2)}) %all-to-all-start.1) | async-done | bytes 131104 | tf_op jit(solution)/shard_map/all_to_all | solution.py:492
  31.9 0.0 copy-done
  31.9 0.0 copy-done.3
  31.9 1.6 %shard_map.95 = f32[24,4096]{1,0:T(8,128)} custom-call(f32[8,4,8,128]{3,2,1,0:T(8,128)S(1)} %bitcast.3, s32[4,1,8,32]{3,2,1,0:T(8,128)S(1)} %copy-done.2, f32[1,4096]{1,0:T(1,128)S(1)} %bitcast.4, f32[24,4096]{1,0:T(8,128)S(1)} %copy-done, bf16[16,1024]{1,0:T(8,128)(2,1)S(1)} %get-tuple-element.13.refs_0_, bf16[256,1024]{1,0:T(8,128)(2,1)S(1)} %get-tuple-element.14.refs_1_), custom_call_target="tpu_custom_call" | custom-call | tf_op jit(solution)/shard_map/pallas_call | solution.py:421
Async XLA Ops:
  0.0 16.1 %copy-start.4 = (f32[24,24]{1,0:T(8,128)S(1)}, f32[24,24]{1,0:T(8,128)}, u32[]{:S(2)}) copy-start(f32[24,24]{1,0:T(8,128)} %interaction_ref.1) | copy-start | bytes 6916
  0.0 16.1 %copy-start.5 = (f32[1,24]{1,0:T(1,128)S(1)}, f32[1,24]{1,0:T(1,128)}, u32[]{:S(2)}) copy-start(f32[1,24]{1,0:T(1,128)} %inflow_ref.1) | copy-start | bytes 292
  2.1 14.0 %all-to-all-start = ((f32[8,8,128]{2,1,0:T(8,128)}), f32[8,8,128]{2,1,0:T(8,128)S(1)}, u32[]{:S(2)}, u32[]{:S(2)}) async-start(f32[8,8,128]{2,1,0:T(8,128)} %shard_map.91.after_ref), calls=%async_computation | async-start | bytes 65536 | tf_op jit(solution)/shard_map/all_to_all | solution.py:475
  9.4 0.8 %copy-start.1 = (f32[8,8,128]{2,1,0:T(8,128)S(1)}, f32[8,8,128]{2,1,0:T(8,128)}, u32[]{:S(2)}) copy-start(f32[8,8,128]{2,1,0:T(8,128)} %shard_map.91.after_ref) | copy-start | bytes 98308
  10.2 0.7 %copy-start.6 = (s32[1,2,2048]{2,1,0:T(2,128)S(1)}, s32[1,2,2048]{2,1,0:T(2,128)}, u32[]{:S(2)}) copy-start(s32[1,2,2048]{2,1,0:T(2,128)} %slot_ref.1) | copy-start | bytes 49156
  10.9 0.7 %copy-start.7 = (f32[1,2,2048]{2,1,0:T(2,128)S(1)}, f32[1,2,2048]{2,1,0:T(2,128)}, u32[]{:S(2)}) copy-start(f32[1,2,2048]{2,1,0:T(2,128)} %courant_ref.1) | copy-start | bytes 49156
  11.6 0.7 %copy-start.8 = (f32[1,2,2048]{2,1,0:T(2,128)S(1)}, f32[1,2,2048]{2,1,0:T(2,128)}, u32[]{:S(2)}) copy-start(f32[1,2,2048]{2,1,0:T(2,128)} %flux_ref.1) | copy-start | bytes 49156
  12.3 0.7 %copy-start.9 = (s32[1,2]{1,0:T(1,128)S(1)}, s32[1,2]{1,0:T(1,128)}, u32[]{:S(2)}) copy-start(s32[1,2]{1,0:T(1,128)} %length_ref.1) | copy-start | bytes 28
  14.5 9.2 %copy-start.2 = (s32[4,1,8,32]{3,2,1,0:T(8,128)S(1)}, s32[4,1,8,32]{3,2,1,0:T(8,128)}, u32[]{:S(2)}) copy-start(s32[4,1,8,32]{3,2,1,0:T(8,128)} %request_ref.3) | copy-start | bytes 12292
  19.2 12.7 %copy-start = (f32[24,4096]{1,0:T(8,128)S(1)}, f32[24,4096]{1,0:T(8,128)}, u32[]{:S(2)}) copy-start(f32[24,4096]{1,0:T(8,128)} %cell_ref.1) | copy-start | bytes 1179652
  19.2 12.7 %copy-start.3 = (f32[4096]{0:T(1024)S(1)}, f32[4096]{0:T(1024)}, u32[]{:S(2)}) copy-start(f32[4096]{0:T(1024)} %param.10) | copy-start | bytes 49156
  19.2 12.7 %all-to-all-start.1 = ((f32[32,8,128]{2,1,0:T(8,128)}), f32[32,8,128]{2,1,0:T(8,128)S(1)}, u32[]{:S(2)}, u32[]{:S(2)}) async-start(f32[32,8,128]{2,1,0:T(8,128)} %bitcast), calls=%async_computation.1 | async-start | bytes 262144 | tf_op jit(solution)/shard_map/all_to_all | solution.py:492

commit v5 on v2

v5 whole, which is shorter than its diff:
```python
import functools

import jax
import jax.numpy as jnp
from jax import lax
from jax.experimental import pallas as pl
from jax.experimental.pallas import tpu as pltpu
from jax.sharding import PartitionSpec as P

SUB = 2
NEWTON = 3
LANES = 128
ROWS = 8
F32 = jnp.float32
BF16 = jnp.bfloat16
VMEM_BYTES = 32 * 1024 * 1024
PICK_BYTES = 63_000_000


def repeat_steps(count, body, carry):
    if count == 1:
        return body(0, carry)
    return lax.fori_loop(0, count, body, carry)


def rounded(value):
    high = value.astype(BF16).astype(F32)
    return high, value - high


def split(value):
    return jnp.concatenate(rounded(value), axis=0).astype(BF16)


def select_groups(tiles, relative):
    count = len(tiles)
    results = []
    for i in range(count):
        value = tiles[0]
        for j in range(1, count):
            value = jnp.where(relative == (i + j) % count, tiles[j], value)
        results.append(value)
    return results


def lane_groups(cap, turn):
    groups = LANES // cap
    lane = lax.broadcasted_iota(jnp.int32, (ROWS, LANES), 1)
    return (lane // cap + (2 * groups - lax.rem(turn, groups))) % groups


def pack(rows, cap, turn, relative):
    groups = LANES // cap
    turned = [
        pltpu.roll(rows[g], lax.rem(turn + g, groups) * cap, 1) for g in range(groups)
    ]
    return select_groups(turned, relative)


def unpack(tiles, cap, relative, count):
    found = select_groups(tiles, relative)[:count]
    return [
        found[g] if g == 0 else pltpu.roll(found[g], LANES - g * cap, 1) for g in range(count)
    ]


def exchange_groups(tiles, width):
    tiles = list(tiles)
    lane_group = lax.broadcasted_iota(jnp.int32, tiles[0].shape, 1) // width
    step = 1
    while step < len(tiles):
        keep = (lane_group & step) == 0
        for i in range(len(tiles)):
            if i & step == 0:
                first, second = tiles[i], tiles[i | step]
                tiles[i] = jnp.where(keep, first, pltpu.roll(second, step * width, 1))
                tiles[i | step] = jnp.where(
                    keep, pltpu.roll(first, LANES - step * width, 1), second
                )
        step *= 2
    return tiles


def spread_rows(block, cap):
    groups = block.shape[0]
    wide = jnp.concatenate([block] * groups, axis=1)
    rows = lax.broadcasted_iota(jnp.int32, wide.shape, 0)
    lanes = lax.broadcasted_iota(jnp.int32, wide.shape, 1) // cap
    return jnp.sum(jnp.where(rows == lanes, wide, 0), axis=0, keepdims=True)


def pick_kernel(cell_hbm, request_hbm, out_ref, cell_ref, request_ref, cell_sem, request_sem):
    request_copy = pltpu.make_async_copy(
        request_hbm.at[lax.axis_index("bundle"), 0], request_ref, request_sem
    )
    cell_copy = pltpu.make_async_copy(cell_hbm, cell_ref, cell_sem)
    request_copy.start()
    cell_copy.start()
    species, cells = cell_ref.shape
    owners, cap = request_ref.shape
    groups = LANES // cap
    chunks = owners // (2 * groups)
    highs = cells // LANES
    here = lax.axis_index("grid")
    relative = lane_groups(cap, here)
    request_copy.wait()

    def wanted(k):
        block = request_ref[pl.ds(k * 2 * groups, 2 * groups), :]
        index = jnp.concatenate(
            [spread_rows(block[:groups], cap), spread_rows(block[groups:], cap)], axis=1
        )
        low = index % LANES
        high = index // LANES
        hot = (
            (lax.broadcasted_iota(jnp.int32, (LANES, 2 * LANES), 0) == low)
            .astype(F32)
            .astype(BF16)
        )
        return high, jnp.concatenate([hot, hot], axis=0)

    kept = wanted(0) if chunks == 1 else None
    cell_copy.wait()
    cell = cell_ref[...]
    stacked = jnp.concatenate(
        [cell[:, LANES * h : LANES * (h + 1)] for h in range(highs)], axis=0
    )
    left = jnp.concatenate(rounded(stacked), axis=1).astype(BF16)

    def chunk(k, carry):
        first = k * 2 * groups
        high, right = wanted(k) if kept is None else kept
        product = jnp.dot(left, right, preferred_element_type=F32)
        picked = jnp.zeros((species, 2 * LANES), F32)
        for h in range(highs):
            picked = picked + jnp.where(high == h, product[species * h : species * (h + 1)], 0.0)
        blank = jnp.zeros((groups * ROWS - species, 2 * LANES), F32)
        picked = jnp.concatenate([picked, blank], axis=0)
        for half in range(2):
            tiles = pack(
                [
                    picked[ROWS * g : ROWS * (g + 1), LANES * half : LANES * (half + 1)]
                    for g in range(groups)
                ],
                cap,
                here,
                relative,
            )
            for j in range(groups):
                out_ref[first + half * groups + j] = tiles[j]
        return carry

    repeat_steps(chunks, chunk, 0)


def to_segments(values):
    lines, nodes = values[0].shape
    blocks = nodes // LANES
    width = lines * blocks
    groups = LANES // width
    stacked = []
    for value in values:
        value = value.astype(F32)
        stacked += [value[:, LANES * block : LANES * (block + 1)] for block in range(blocks)]
    stacked.append(jnp.zeros((LANES - width * len(values), LANES), F32))
    turned = jnp.transpose(jnp.concatenate(stacked, axis=0))
    times = LANES // groups
    return exchange_groups([turned[times * g : times * (g + 1)] for g in range(groups)], width)


def lines_kernel(
    cap,
    table_ref,
    slot_ref,
    length_ref,
    courant_ref,
    flux_ref,
    inflow_ref,
    interaction_ref,
    out_ref,
):
    owners = table_ref.shape[0]
    copies = out_ref.shape[0] // owners
    species = inflow_ref.shape[1]
    lines, nodes = slot_ref.shape[1:]
    groups = species // ROWS
    all_groups = LANES // cap
    rows = all_groups * ROWS
    sent = out_ref.shape[2] // LANES
    blocks = nodes // LANES
    width = lines * blocks
    segments = LANES // width
    times = LANES // segments
    chunk_owners = 2 * all_groups
    chunks = owners // chunk_owners
    here, bundle = lax.axis_index("grid"), lax.axis_index("bundle")

    slot = slot_ref[0]
    within = (slot + lax.rem(here, all_groups) * cap) % LANES
    slot, courant, flux = to_segments([slot - slot % LANES + within, courant_ref[0], flux_ref[0]])[
        :3
    ]

    def hot(k):
        local = (slot - lax.convert_element_type(k * 2 * LANES, F32)).astype(BF16)
        index = lax.broadcasted_iota(jnp.int32, (2 * LANES, LANES), 0).astype(F32).astype(BF16)
        one, zero = jnp.ones_like(index), jnp.zeros_like(index)
        return jnp.concatenate(
            [
                jnp.where(jnp.broadcast_to(local[t : t + 1], index.shape) == index, one, zero)
                for t in range(times)
            ],
            axis=1,
        )

    kept = hot(0) if chunks == 1 else None

    relative = lane_groups(cap, here)

    def gather(k, state):
        halves = []
        for half in range(2):
            first = k * chunk_owners + half * all_groups
            halves.append(
                jnp.concatenate(
                    unpack(
                        [table_ref[first + j] for j in range(all_groups)], cap, relative, groups
                    ),
                    axis=0,
                )
            )
        left = split(jnp.concatenate(halves, axis=1))
        found = jnp.dot(left, hot(k) if kept is None else kept, preferred_element_type=F32)
        found = found[:species] + found[species:]
        return found if chunks == 1 else state + found

    start = repeat_steps(
        chunks, gather, jnp.zeros((species, lines * nodes), F32) if chunks > 1 else 0
    )

    lane = lax.broadcasted_iota(jnp.int32, (ROWS, LANES), 1)
    part = lane // width
    block = (lane % width) // lines
    segment = block * segments + part
    line = lane % lines

    def earlier(value, distance):
        major, minor = distance // segments, distance % segments
        near = pltpu.roll(value, minor * width + major * lines, 1)
        if minor == 0:
            return near
        far = pltpu.roll(value, minor * width + (major + 1) * lines, 1)
        return jnp.where(part >= minor, near, far)

    eye = lax.broadcasted_iota(jnp.int32, (species, LANES), 0) == lax.broadcasted_iota(
        jnp.int32, (species, LANES), 1
    )
    padded = jnp.concatenate([inflow_ref[...], jnp.zeros((1, LANES - species), F32)], axis=1)
    column = jnp.sum(jnp.where(eye, padded, 0.0), axis=1, keepdims=True)
    entry = jnp.broadcast_to(column, (species, LANES))
    entry = [entry[ROWS * g : ROWS * (g + 1)] for g in range(groups)]

    scale = 1.0 / (1.0 + courant)
    decay = courant * scale
    first = [None] * groups
    second = [None] * groups
    local, ones, twos = [], [], []
    for t in range(times):
        scale_t = jnp.broadcast_to(scale[t : t + 1], (ROWS, LANES))
        decay_t = jnp.broadcast_to(decay[t : t + 1], (ROWS, LANES))
        one = decay_t if t == 0 else decay_t * ones[-1]
        two = scale_t * one if t == 0 else scale_t * one + decay_t * twos[-1]
        ones.append(one)
        twos.append(two)
        for g in range(groups):
            value = start[ROWS * g : ROWS * (g + 1), LANES * t : LANES * (t + 1)] * scale_t
            first[g] = value if t == 0 else value + decay_t * first[g]
            value = scale_t * first[g]
            second[g] = value if t == 0 else value + decay_t * second[g]
            local.append(second[g])

    a, b = ones[-1], twos[-1]
    head = segment == 0
    first = [jnp.where(head, f + a * e, f) for f, e in zip(first, entry)]
    second = [jnp.where(head, s + b * e + a * e, s) for s, e in zip(second, entry)]
    distance = 1
    while distance < blocks * segments:
        opened = segment >= distance
        a_open, b_open = jnp.where(opened, a, 0.0), jnp.where(opened, b, 0.0)
        ahead = [earlier(f, distance) for f in first]
        second = [s + b_open * f + a_open * earlier(s, distance) for s, f in zip(second, ahead)]
        first = [f + a_open * e for f, e in zip(first, ahead)]
        if 2 * distance < blocks * segments:
            a_ahead = earlier(a, distance)
            b = b * a_ahead + a * earlier(b, distance)
            a = a * a_ahead
        distance *= 2
    carry_one = [jnp.where(head, e, earlier(f, 1)) for e, f in zip(entry, first)]
    carry_two = [jnp.where(head, e, earlier(s, 1)) for e, s in zip(entry, second)]
    columns = [
        jnp.concatenate(
            [
                local[t * groups + g] + twos[t] * carry_one[g] + ones[t] * carry_two[g]
                for g in range(groups)
            ],
            axis=0,
        )
        for t in range(times)
    ]

    matrix_high, matrix_low = rounded(interaction_ref[...])
    block_row = jnp.concatenate([matrix_high, matrix_low, matrix_high], axis=1)
    blank = jnp.zeros_like(block_row)
    left = jnp.concatenate(
        [
            jnp.concatenate([block_row, blank], axis=1),
            jnp.concatenate([blank, block_row], axis=1),
        ],
        axis=0,
    ).astype(BF16)
    half = times // 2
    base = jnp.concatenate(
        [
            jnp.concatenate(columns[:half], axis=1),
            jnp.concatenate(columns[half:], axis=1),
        ],
        axis=0,
    )
    iterate = base
    for step in range(NEWTON):
        high, low = rounded(jnp.tanh(iterate))
        right = jnp.concatenate(
            [
                high[:species],
                high[:species],
                low[:species],
                high[species:],
                high[species:],
                low[species:],
            ],
            axis=0,
        ).astype(BF16)
        iterate = base - jnp.dot(left, right, preferred_element_type=F32)
    iterate = jnp.concatenate([iterate[:species], iterate[species:]], axis=1)

    length = jnp.zeros((ROWS, LANES), jnp.int32)
    for one_line in range(lines):
        length = jnp.where(line == one_line, length_ref[0, one_line], length)
    node = block * LANES + part * times
    weight = jnp.concatenate(
        [
            jnp.where(node + t < length, jnp.broadcast_to(flux[t : t + 1], (ROWS, LANES)), 0.0)
            for t in range(times)
        ],
        axis=1,
    )
    first_row = lax.broadcasted_iota(jnp.int32, weight.shape, 0) == 0
    scaled = [iterate[ROWS * g : ROWS * (g + 1)] * weight for g in range(groups)]
    scaled.append(jnp.where(first_row, weight, 0.0))
    left = split(jnp.concatenate(scaled, axis=0))
    relative = lane_groups(cap, here + bundle)

    def scatter(k, carry):
        sums = lax.dot_general(
            left,
            hot(k) if kept is None else kept,
            (((1,), (1,)), ((), ())),
            preferred_element_type=F32,
        )
        sums = sums[:rows] + sums[rows:]
        last = [sums[species : species + 1]]
        last += [
            sums[ROWS * g + r : ROWS * g + r + 1] for g in range(groups) for r in range(sent, ROWS)
        ]
        last.append(jnp.zeros((ROWS - len(last), 2 * LANES), F32))
        sums = jnp.concatenate([sums[:species]] + last, axis=0)
        for half in range(2):
            tiles = pack(
                [
                    sums[ROWS * g : ROWS * (g + 1), LANES * half : LANES * (half + 1)]
                    for g in range(all_groups)
                ],
                cap,
                bundle,
                relative,
            )
            for j in range(all_groups):
                owner = k * chunk_owners + half * all_groups + j
                for copy in range(copies):
                    for r in range(sent):
                        out_ref[owner * copies + copy, :, LANES * r : LANES * (r + 1)] = tiles[j][
                            r : r + 1
                        ]
        return carry

    repeat_steps(chunks, scatter, 0)


def blend_kernel(bundles, sums_ref, request_ref, pore_ref, cell_ref, out_hbm, out_ref, out_sem):
    owners = sums_ref.shape[0] // bundles
    sent = sums_ref.shape[2] // LANES
    species, cells = cell_ref.shape
    cap = request_ref.shape[3]
    all_groups = LANES // cap
    groups = species // ROWS
    width = 2 * LANES
    highs = cells // width
    chunks = owners // ROWS
    here = lax.axis_index("grid")
    sublane = lax.broadcasted_iota(jnp.int32, (ROWS, LANES), 0)

    def tile(device, bundle):
        value = jnp.zeros((ROWS, LANES), F32)
        for r in range(sent):
            row = sums_ref[device * bundles + bundle, :, LANES * r : LANES * (r + 1)]
            value = jnp.where(sublane == r, jnp.broadcast_to(row, (ROWS, LANES)), value)
        return value

    def chunk(k, total):
        values, weights, indices = [], [], []
        for t in range(bundles // all_groups):
            block = jnp.concatenate(
                [
                    request_ref[
                        t * all_groups
                        + lax.rem(x + all_groups - lax.rem(here, all_groups), all_groups),
                        0,
                        pl.ds(k * ROWS, ROWS),
                        :,
                    ]
                    for x in range(all_groups)
                ],
                axis=1,
            )
            straight = block
            for turn in range(1, all_groups):
                block = jnp.where(
                    sublane % all_groups == turn, pltpu.roll(straight, turn * cap, 1), block
                )
            for d in range(ROWS):
                found = unpack(
                    [tile(k * ROWS + d, t * all_groups + j) for j in range(all_groups)],
                    cap,
                    lane_groups(cap, here + d),
                    all_groups,
                )
                weights.append(found[groups][:1])
                spare = 1
                for g in range(groups):
                    for r in range(sent, ROWS):
                        row = jnp.broadcast_to(
                            found[groups][spare : spare + 1], (ROWS, LANES)
                        )
                        found[g] = jnp.where(sublane == r, row, found[g])
                        spare += 1
                values.append(jnp.concatenate(found[:groups], axis=0))
                indices.append(block[d : d + 1])
        parts = split(jnp.concatenate(values, axis=1))
        weight_high, weight_low = rounded(jnp.concatenate(weights, axis=1))
        index = jnp.concatenate(indices, axis=1)
        entries = index.shape[1]
        high = jnp.broadcast_to(index // width, (2 * ROWS, entries)).astype(F32).astype(BF16)
        low = jnp.broadcast_to(index % width, (2 * ROWS, entries)).astype(F32).astype(BF16)
        low = jnp.concatenate([low] * (width // (2 * ROWS)), axis=0)
        place = lax.broadcasted_iota(jnp.int32, (width, entries), 0).astype(F32).astype(BF16)
        hot = jnp.where(place == low, jnp.ones_like(place), jnp.zeros_like(place))
        zero = jnp.zeros((2 * ROWS, entries), BF16)
        pieces = []
        for h in range(highs):
            mask = high == jnp.array(h, BF16)
            for r in range(2 * species // (2 * ROWS)):
                pieces.append(
                    jnp.where(mask, parts[2 * ROWS * r : 2 * ROWS * (r + 1)], zero)
                )
        for first in range(0, highs, 2 * ROWS):
            mask = high == (
                lax.broadcasted_iota(jnp.int32, (2 * ROWS, entries), 0) + first
            ).astype(F32).astype(BF16)
            for part in (weight_high, weight_low):
                row = jnp.broadcast_to(part, (2 * ROWS, entries)).astype(BF16)
                pieces.append(jnp.where(mask, row, zero))
        left = jnp.concatenate(pieces, axis=0)
        product = lax.dot_general(
            left, hot, (((1,), (1,)), ((), ())), preferred_element_type=F32
        )
        return product if chunks == 1 else total + product

    flux_rows = -(-highs // (2 * ROWS)) * 4 * ROWS
    total = repeat_steps(
        chunks,
        chunk,
        jnp.zeros((highs * 2 * species + flux_rows, width), F32) if chunks > 1 else 0,
    )
    flux = total[highs * 2 * species :]
    copies = []
    stride = max(highs // 4, 1)
    for h in range(highs):
        part = total[2 * species * h : 2 * species * (h + 1)]
        part = part[:species] + part[species:]
        row = h // (2 * ROWS) * 4 * ROWS + h % (2 * ROWS)
        pore = pore_ref[:, width * h : width * (h + 1)]
        inverse = 1.0 / (pore + flux[row : row + 1] + flux[row + 2 * ROWS : row + 2 * ROWS + 1])
        columns = pl.ds(width * h, width)
        out_ref[:, columns] = (pore * cell_ref[:, columns] + part) * inverse
        if h % stride == stride - 1:
            columns = pl.ds(width * (h - stride + 1), stride * width)
            copies.append(
                pltpu.make_async_copy(
                    out_ref.at[:, columns], out_hbm.at[:, columns], out_sem.at[h // stride]
                )
            )
            copies[-1].start()
    for copy in copies:
        copy.wait()


def call(kernel, shape, operands, kinds={}, scratch=(), grant=VMEM_BYTES, out=pltpu.VMEM):
    return pl.pallas_call(
        kernel,
        out_shape=jax.ShapeDtypeStruct(shape, F32),
        in_specs=[
            pl.BlockSpec(memory_space=kinds.get(i, pltpu.VMEM)) for i in range(len(operands))
        ],
        out_specs=pl.BlockSpec(memory_space=out),
        scratch_shapes=list(scratch),
        compiler_params=pltpu.CompilerParams(vmem_limit_bytes=grant),
    )(*operands)


def shards(
    bundles,
    cell_state,
    pore_volume,
    request_cell,
    node_slot,
    line_length,
    courant,
    flux_weight,
    inflow,
    interaction,
):
    owners, cap = request_cell.shape[2:]
    sent = -(-(cell_state.shape[0] + 1) // (LANES // cap))
    outgoing = call(
        pick_kernel,
        (owners, ROWS, LANES),
        (cell_state, request_cell),
        kinds={0: pltpu.HBM, 1: pltpu.HBM},
        scratch=(
            pltpu.VMEM(cell_state.shape, F32),
            pltpu.VMEM((owners, cap), jnp.int32),
            pltpu.SemaphoreType.DMA,
            pltpu.SemaphoreType.DMA,
        ),
        grant=PICK_BYTES,
    )
    table = lax.all_to_all(outgoing, "grid", split_axis=0, concat_axis=0, tiled=True)
    sums = call(
        functools.partial(lines_kernel, cap),
        (owners * bundles, 1, sent * LANES),
        (table, node_slot, line_length, courant, flux_weight, inflow, interaction),
        kinds={2: pltpu.SMEM},
    )
    back = lax.all_to_all(sums, ("grid", "bundle"), split_axis=0, concat_axis=0, tiled=True)
    return call(
        functools.partial(blend_kernel, bundles),
        cell_state.shape,
        (back, request_cell, pore_volume[None, :], cell_state),
        scratch=(pltpu.VMEM(cell_state.shape, F32), pltpu.SemaphoreType.DMA((4,))),
        out=pltpu.HBM,
    )


def solution(mesh):
    placed = (
        P(None, "grid"),
        P("grid"),
        P(None, "grid", None, None),
        P("bundle", "grid", None),
        P("bundle", "grid"),
        P("bundle", "grid", None),
        P("bundle", "grid", None),
        P("bundle", None),
        P(),
    )
    return jax.shard_map(
        functools.partial(shards, mesh.shape["bundle"]),
        mesh=mesh,
        in_specs=placed,
        out_specs=P(None, "grid"),
        check_vma=False,
    )
```

time: 31.4 us -> 31.2 us (level)
  local copies, waits for them, and re-layouts: 1.76 us -> 0.05 us
  Pallas kernels: 5.35 us -> 6.85 us
    unnamed x20 -> x18, local copies, waits for them, and re-layouts: 1.76 us -> 0.05 us
    pallas_call x3, Pallas kernels: 5.35 us -> 6.85 us  [call(): pl.pallas_call(kernel, out_shape=jax.ShapeDtypeStruct(shape, F32), in_spe...]
where the time goes in v5:
time: 31.2 us; the launch traced here: 30.9 us
  blocking collectives  23.9 us (77%)
  Pallas kernels  6.85 us (22%)
    all_to_all x1, blocking collectives, shards(): lax.all_to_all(outgoing, 'grid', split_axis=0, concat_axis=0, tiled=True)  14.1 us
    all_to_all x1, blocking collectives, shards(): lax.all_to_all(sums, ('grid', 'bundle'), split_axis=0, concat_axis=0, til...  9.81 us
    pallas_call x3, Pallas kernels, call(): pl.pallas_call(kernel, out_shape=jax.ShapeDtypeStruct(shape, F32), in_spe...  6.85 us

profile of v5, /device:TPU:0, one launch (start us, length us, event | category | flops | bytes accessed | tf_op | source)
XLA Modules:
  0.0 30.9 jit_solution(12426779956041500311)
XLA Ops:
  0.0 0.0 copy-start
  0.0 2.1 %shard_map.91 = f32[8,8,128]{2,1,0:T(8,128)} custom-call(f32[24,4096]{1,0:T(8,128)} %cell_ref.1, s32[4,1,8,32]{3,2,1,0:T(8,128)} %request_ref.1), custom_call_target="tpu_custom_call" | custom-call | tf_op jit(solution)/shard_map/pallas_call | solution.py:518
  2.1 0.0 copy-start.3
  2.1 0.0 copy-start.4
  2.1 0.0 copy-start.5
  2.1 0.0 copy-start.6
  2.1 0.0 copy-start.7
  2.1 0.0 copy-start.8
  2.1 14.1 %all_to_all.10.table_ref = f32[8,8,128]{2,1,0:T(8,128)S(1)} all-to-all(f32[8,8,128]{2,1,0:T(8,128)} %shard_map.91), channel_id=1, replica_groups=mesh['grid'=8,'bundle'=4] {'grid'}, dimensions={0} | all-to-all | bytes 65536 | tf_op jit(solution)/shard_map/all_to_all | solution.py:557
  16.2 0.0 copy-done.3
  16.2 0.0 copy-done.4
  16.2 0.0 copy-done.5
  16.3 0.0 copy-done.6
  16.3 0.0 copy-done.7
  16.3 0.0 copy-done.8
  16.3 3.2 %shard_map.92 = f32[32,1,896]{2,1,0:T(1,128)S(1)} custom-call(f32[8,8,128]{2,1,0:T(8,128)S(1)} %all_to_all.10.table_ref, s32[1,2,2048]{2,1,0:T(2,128)S(1)} %copy-done.3, s32[1,2]{1,0:T(1,128)S(1)} %copy-done.7, f32[1,2,2048]{2,1,0:T(2,128)S(1)} %copy-done.4, f32[1,2,2048]{2,1,0:T(2,128)S(1)} %copy-done.5, f32[1,24]{1,0:T(1,128)S(1)} %copy-done.8, ...), custom_call_target="tpu_custom_call" | custom-call | tf_op jit(solution)/shard_map/pallas_call | solution.py:518
  19.5 0.0 copy-start.1
  19.5 0.0 copy-start.2
  19.5 9.8 %all_to_all.11.sums_ref = f32[32,1,896]{2,1,0:T(1,128)S(1)} all-to-all(f32[32,1,896]{2,1,0:T(1,128)S(1)} %shard_map.92), channel_id=1, replica_groups=mesh['grid'=8,'bundle'=4] {'grid','bundle'}, dimensions={0} | all-to-all | bytes 229376 | tf_op jit(solution)/shard_map/all_to_all | solution.py:564
  29.3 0.0 copy-done
  29.3 0.0 copy-done.1
  29.3 0.0 copy-done.2
  29.3 1.6 %shard_map.93 = f32[24,4096]{1,0:T(8,128)} custom-call(f32[32,1,896]{2,1,0:T(1,128)S(1)} %all_to_all.11.sums_ref, s32[4,1,8,32]{3,2,1,0:T(8,128)S(1)} %copy-done.1, f32[1,4096]{1,0:T(1,128)S(1)} %bitcast.1, f32[24,4096]{1,0:T(8,128)S(1)} %copy-done), custom_call_target="tpu_custom_call" | custom-call | tf_op jit(solution)/shard_map/pallas_call | solution.py:518
Async XLA Ops:
  0.0 29.3 %copy-start = (f32[24,4096]{1,0:T(8,128)S(1)}, f32[24,4096]{1,0:T(8,128)}, u32[]{:S(2)}) copy-start(f32[24,4096]{1,0:T(8,128)} %cell_ref.1) | copy-start | bytes 1179652
  2.1 14.2 %copy-start.3 = (s32[1,2,2048]{2,1,0:T(2,128)S(1)}, s32[1,2,2048]{2,1,0:T(2,128)}, u32[]{:S(2)}) copy-start(s32[1,2,2048]{2,1,0:T(2,128)} %slot_ref.1) | copy-start | bytes 49156
  2.1 14.2 %copy-start.4 = (f32[1,2,2048]{2,1,0:T(2,128)S(1)}, f32[1,2,2048]{2,1,0:T(2,128)}, u32[]{:S(2)}) copy-start(f32[1,2,2048]{2,1,0:T(2,128)} %courant_ref.1) | copy-start | bytes 49156
  2.1 14.2 %copy-start.5 = (f32[1,2,2048]{2,1,0:T(2,128)S(1)}, f32[1,2,2048]{2,1,0:T(2,128)}, u32[]{:S(2)}) copy-start(f32[1,2,2048]{2,1,0:T(2,128)} %flux_ref.1) | copy-start | bytes 49156
  2.1 14.2 %copy-start.6 = (f32[24,24]{1,0:T(8,128)S(1)}, f32[24,24]{1,0:T(8,128)}, u32[]{:S(2)}) copy-start(f32[24,24]{1,0:T(8,128)} %interaction_ref.1) | copy-start | bytes 6916
  2.1 14.2 %copy-start.7 = (s32[1,2]{1,0:T(1,128)S(1)}, s32[1,2]{1,0:T(1,128)}, u32[]{:S(2)}) copy-start(s32[1,2]{1,0:T(1,128)} %length_ref.1) | copy-start | bytes 28
  2.1 14.2 %copy-start.8 = (f32[1,24]{1,0:T(1,128)S(1)}, f32[1,24]{1,0:T(1,128)}, u32[]{:S(2)}) copy-start(f32[1,24]{1,0:T(1,128)} %inflow_ref.1) | copy-start | bytes 292
  19.5 9.8 %copy-start.1 = (s32[4,1,8,32]{3,2,1,0:T(8,128)S(1)}, s32[4,1,8,32]{3,2,1,0:T(8,128)}, u32[]{:S(2)}) copy-start(s32[4,1,8,32]{3,2,1,0:T(8,128)} %request_ref.1) | copy-start | bytes 12292
  19.5 9.8 %copy-start.2 = (f32[4096]{0:T(1024)S(1)}, f32[4096]{0:T(1024)}, u32[]{:S(2)}) copy-start(f32[4096]{0:T(1024)} %param.10) | copy-start | bytes 49156

commit v6 on v5

--- a/solution.py
+++ b/solution.py
@@ -61,6 +61,17 @@
     found = select_groups(tiles, relative)[:count]
     return [
         found[g] if g == 0 else pltpu.roll(found[g], LANES - g * cap, 1) for g in range(count)
+    ]
+
+
+def exchange_rows(tiles, count):
+    parts = len(tiles)
+    depth = ROWS // parts
+    place = lax.broadcasted_iota(jnp.int32, tiles[0].shape, 0) // depth
+    turned = [tiles[i] if i == 0 else pltpu.roll(tiles[i], depth * i, 0) for i in range(parts)]
+    found = select_groups(turned, place)[:count]
+    return [
+        found[j] if j == 0 else pltpu.roll(found[j], ROWS - depth * j, 0) for j in range(count)
     ]
 
 
@@ -90,14 +101,16 @@
 
 
 def pick_kernel(cell_hbm, request_hbm, out_ref, cell_ref, request_ref, cell_sem, request_sem):
-    request_copy = pltpu.make_async_copy(
-        request_hbm.at[lax.axis_index("bundle"), 0], request_ref, request_sem
-    )
-    cell_copy = pltpu.make_async_copy(cell_hbm, cell_ref, cell_sem)
+    species = cell_hbm.shape[0]
+    share = jnp.minimum(lax.axis_index("bundle"), species // ROWS - 1)
+    request_copy = pltpu.make_async_copy(request_hbm, request_ref, request_sem)
+    cell_copy = pltpu.make_async_copy(
+        cell_hbm.at[pl.ds(pl.multiple_of(share * ROWS, ROWS), ROWS)], cell_ref, cell_sem
+    )
     request_copy.start()
     cell_copy.start()
-    species, cells = cell_ref.shape
-    owners, cap = request_ref.shape
+    cells = cell_ref.shape[1]
+    bundles, _, owners, cap = request_ref.shape
     groups = LANES // cap
     chunks = owners // (2 * groups)
     highs = cells // LANES
@@ -106,14 +119,15 @@
     request_copy.wait()
 
     def wanted(k):
-        block = request_ref[pl.ds(k * 2 * groups, 2 * groups), :]
-        index = jnp.concatenate(
-            [spread_rows(block[:groups], cap), spread_rows(block[groups:], cap)], axis=1
-        )
+        pieces = []
+        for bundle in range(bundles):
+            block = request_ref[bundle, 0, pl.ds(k * 2 * groups, 2 * groups), :]
+            pieces += [spread_rows(block[:groups], cap), spread_rows(block[groups:], cap)]
+        index = jnp.concatenate(pieces, axis=1)
         low = index % LANES
-        high = index // LANES
+        high = jnp.broadcast_to(index // LANES, (ROWS, index.shape[1]))
         hot = (
-            (lax.broadcasted_iota(jnp.int32, (LANES, 2 * LANES), 0) == low)
+            (lax.broadcasted_iota(jnp.int32, (LANES, index.shape[1]), 0) == low)
             .astype(F32)
             .astype(BF16)
         )
@@ -131,17 +145,13 @@
         first = k * 2 * groups
         high, right = wanted(k) if kept is None else kept
         product = jnp.dot(left, right, preferred_element_type=F32)
-        picked = jnp.zeros((species, 2 * LANES), F32)
+        picked = jnp.zeros(high.shape, F32)
         for h in range(highs):
-            picked = picked + jnp.where(high == h, product[species * h : species * (h + 1)], 0.0)
-        blank = jnp.zeros((groups * ROWS - species, 2 * LANES), F32)
-        picked = jnp.concatenate([picked, blank], axis=0)
+            picked = picked + jnp.where(high == h, product[ROWS * h : ROWS * (h + 1)], 0.0)
         for half in range(2):
+            columns = [LANES * (2 * bundle + half) for bundle in range(bundles)]
             tiles = pack(
-                [
-                    picked[ROWS * g : ROWS * (g + 1), LANES * half : LANES * (half + 1)]
-                    for g in range(groups)
-                ],
+                exchange_rows([picked[:, c : c + LANES] for c in columns], groups),
                 cap,
                 here,
                 relative,
@@ -221,14 +231,10 @@
         halves = []
         for half in range(2):
             first = k * chunk_owners + half * all_groups
-            halves.append(
-                jnp.concatenate(
-                    unpack(
-                        [table_ref[first + j] for j in range(all_groups)], cap, relative, groups
-                    ),
-                    axis=0,
-                )
+            tiles = unpack(
+                [table_ref[first + j] for j in range(all_groups)], cap, relative, all_groups
             )
+            halves.append(jnp.concatenate(exchange_rows(tiles, groups), axis=0))
         left = split(jnp.concatenate(halves, axis=1))
         found = jnp.dot(left, hot(k) if kept is None else kept, preferred_element_type=F32)
         found = found[:species] + found[species:]
@@ -345,7 +351,8 @@
 
     length = jnp.zeros((ROWS, LANES), jnp.int32)
     for one_line in range(lines):
-        length = jnp.where(line == one_line, length_ref[0, one_line], length)
+        one_length = jnp.broadcast_to(length_ref[:, one_line : one_line + 1], (ROWS, LANES))
+        length = jnp.where(line == one_line, one_length, length)
     node = block * LANES + part * times
     weight = jnp.concatenate(
         [
@@ -547,19 +554,20 @@
         (cell_state, request_cell),
         kinds={0: pltpu.HBM, 1: pltpu.HBM},
         scratch=(
-            pltpu.VMEM(cell_state.shape, F32),
-            pltpu.VMEM((owners, cap), jnp.int32),
+            pltpu.VMEM((ROWS, cell_state.shape[1]), F32),
+            pltpu.VMEM(request_cell.shape, jnp.int32),
             pltpu.SemaphoreType.DMA,
             pltpu.SemaphoreType.DMA,
         ),
         grant=PICK_BYTES,
     )
-    table = lax.all_to_all(outgoing, "grid", split_axis=0, concat_axis=0, tiled=True)
+    outgoing = outgoing.reshape(owners * bundles, ROWS // bundles, LANES)
+    table = lax.all_to_all(outgoing, ("grid", "bundle"), split_axis=0, concat_axis=0, tiled=True)
+    table = table.reshape(owners, ROWS, LANES)
     sums = call(
         functools.partial(lines_kernel, cap),
         (owners * bundles, 1, sent * LANES),
         (table, node_slot, line_length, courant, flux_weight, inflow, interaction),
-        kinds={2: pltpu.SMEM},
     )
     back = lax.all_to_all(sums, ("grid", "bundle"), split_axis=0, concat_axis=0, tiled=True)
     return call(

time: 31.2 us -> 31.6 us (1.013)
  local copies, waits for them, and re-layouts: 0.05 us -> 0.68 us
  Pallas kernels: 6.85 us -> 6.25 us
  blocking collectives: 23.9 us -> 24.3 us
    unnamed x18, local copies, waits for them, and re-layouts: 0.05 us -> 0.68 us
    pallas_call x3, Pallas kernels: 6.85 us -> 6.25 us  [call(): pl.pallas_call(kernel, out_shape=jax.ShapeDtypeStruct(shape, F32), in_spe...]
    all_to_all x1, blocking collectives: 14.1 us -> 14.6 us  [shards(): lax.all_to_all(outgoing, ('grid', 'bundle'), split_axis=0, concat_axis=0,...]
where the time goes in v6:
time: 31.6 us; the launch traced here: 31.3 us
  blocking collectives  24.3 us (77%)
  Pallas kernels  6.25 us (20%)
  local copies, waits for them, and re-layouts  0.68 us (2%)
    all_to_all x1, blocking collectives, shards(): lax.all_to_all(outgoing, ('grid', 'bundle'), split_axis=0, concat_axis=0,...  14.6 us
    all_to_all x1, blocking collectives, shards(): lax.all_to_all(sums, ('grid', 'bundle'), split_axis=0, concat_axis=0, til...  9.72 us
    pallas_call x3, Pallas kernels, call(): pl.pallas_call(kernel, out_shape=jax.ShapeDtypeStruct(shape, F32), in_spe...  6.25 us
    unnamed x18, local copies, waits for them, and re-layouts  0.68 us

profile of v6, /device:TPU:0, one launch (start us, length us, event | category | flops | bytes accessed | tf_op | source)
XLA Modules:
  0.0 31.3 jit_solution(14018339784678667897)
XLA Ops:
  0.0 0.0 copy-start
  0.0 2.0 %shard_map.91 = f32[8,8,128]{2,1,0:T(8,128)} custom-call(f32[24,4096]{1,0:T(8,128)} %cell_ref.1, s32[4,1,8,32]{3,2,1,0:T(8,128)} %request_ref.1), custom_call_target="tpu_custom_call" | custom-call | tf_op jit(solution)/shard_map/pallas_call | solution.py:525
  2.0 0.0 copy-start.3
  2.0 0.0 copy-start.4
  2.0 0.0 copy-start.5
  2.0 0.0 copy-start.6
  2.0 14.6 %all_to_all.10 = f32[32,2,128]{2,1,0:T(2,128)S(1)} all-to-all(f32[32,2,128]{2,1,0:T(2,128)} %bitcast.5), channel_id=1, replica_groups=mesh['grid'=8,'bundle'=4] {'grid','bundle'}, dimensions={0} | all-to-all | bytes 65536 | tf_op jit(solution)/shard_map/all_to_all | solution.py:565
  16.6 0.0 copy-start.7
  16.6 0.0 copy-start.8
  16.6 0.0 copy-done.3
  16.6 0.0 copy-done.4
  16.6 0.0 copy-done.5
  16.6 0.0 copy-done.6
  16.6 0.6 %copy-done.7 = s32[1,2]{1,0:T(1,128)S(1)} copy-done((s32[1,2]{1,0:T(1,128)S(1)}, s32[1,2]{1,0:T(1,128)}, u32[]{:S(2)}) %copy-start.7) | copy-done | bytes 32
  17.3 0.0 copy-done.8
  17.3 2.6 %shard_map.92 = f32[32,1,896]{2,1,0:T(1,128)S(1)} custom-call(f32[8,8,128]{2,1,0:T(8,128)S(1)} %bitcast.3, s32[1,2,2048]{2,1,0:T(2,128)S(1)} %copy-done.3, s32[1,2]{1,0:T(1,128)S(1)} %copy-done.7, f32[1,2,2048]{2,1,0:T(2,128)S(1)} %copy-done.4, f32[1,2,2048]{2,1,0:T(2,128)S(1)} %copy-done.5, f32[1,24]{1,0:T(1,128)S(1)} %copy-done.8, f32[24,24]{1,0:T(8,128)S(1)} %copy-done.6), custom_call_target="tpu_custom_call" | custom-call | tf_op jit(solution)/shard_map/pallas_call | solution.py:525
  19.9 0.0 copy-start.1
  19.9 0.0 copy-start.2
  20.0 9.7 %all_to_all.11.sums_ref = f32[32,1,896]{2,1,0:T(1,128)S(1)} all-to-all(f32[32,1,896]{2,1,0:T(1,128)S(1)} %shard_map.92), channel_id=1, replica_groups=mesh['grid'=8,'bundle'=4] {'grid','bundle'}, dimensions={0} | all-to-all | bytes 229376 | tf_op jit(solution)/shard_map/all_to_all | solution.py:572
  29.7 0.0 copy-done
  29.7 0.0 copy-done.1
  29.7 0.0 copy-done.2
  29.7 1.6 %shard_map.93 = f32[24,4096]{1,0:T(8,128)} custom-call(f32[32,1,896]{2,1,0:T(1,128)S(1)} %all_to_all.11.sums_ref, s32[4,1,8,32]{3,2,1,0:T(8,128)S(1)} %copy-done.1, f32[1,4096]{1,0:T(1,128)S(1)} %bitcast.4, f32[24,4096]{1,0:T(8,128)S(1)} %copy-done), custom_call_target="tpu_custom_call" | custom-call | tf_op jit(solution)/shard_map/pallas_call | solution.py:525
Async XLA Ops:
  0.0 29.7 %copy-start = (f32[24,4096]{1,0:T(8,128)S(1)}, f32[24,4096]{1,0:T(8,128)}, u32[]{:S(2)}) copy-start(f32[24,4096]{1,0:T(8,128)} %cell_ref.1) | copy-start | bytes 1179652
  2.0 14.6 %copy-start.3 = (s32[1,2,2048]{2,1,0:T(2,128)S(1)}, s32[1,2,2048]{2,1,0:T(2,128)}, u32[]{:S(2)}) copy-start(s32[1,2,2048]{2,1,0:T(2,128)} %slot_ref.1) | copy-start | bytes 49156
  2.0 14.6 %copy-start.4 = (f32[1,2,2048]{2,1,0:T(2,128)S(1)}, f32[1,2,2048]{2,1,0:T(2,128)}, u32[]{:S(2)}) copy-start(f32[1,2,2048]{2,1,0:T(2,128)} %courant_ref.1) | copy-start | bytes 49156
  2.0 14.6 %copy-start.5 = (f32[1,2,2048]{2,1,0:T(2,128)S(1)}, f32[1,2,2048]{2,1,0:T(2,128)}, u32[]{:S(2)}) copy-start(f32[1,2,2048]{2,1,0:T(2,128)} %flux_ref.1) | copy-start | bytes 49156
  2.0 14.6 %copy-start.6 = (f32[24,24]{1,0:T(8,128)S(1)}, f32[24,24]{1,0:T(8,128)}, u32[]{:S(2)}) copy-start(f32[24,24]{1,0:T(8,128)} %interaction_ref.1) | copy-start | bytes 6916
  16.6 0.7 %copy-start.7 = (s32[1,2]{1,0:T(1,128)S(1)}, s32[1,2]{1,0:T(1,128)}, u32[]{:S(2)}) copy-start(s32[1,2]{1,0:T(1,128)} %length_ref.1) | copy-start | bytes 28
  16.6 0.7 %copy-start.8 = (f32[1,24]{1,0:T(1,128)S(1)}, f32[1,24]{1,0:T(1,128)}, u32[]{:S(2)}) copy-start(f32[1,24]{1,0:T(1,128)} %inflow_ref.1) | copy-start | bytes 292
  19.9 9.7 %copy-start.1 = (s32[4,1,8,32]{3,2,1,0:T(8,128)S(1)}, s32[4,1,8,32]{3,2,1,0:T(8,128)}, u32[]{:S(2)}) copy-start(s32[4,1,8,32]{3,2,1,0:T(8,128)} %request_ref.1) | copy-start | bytes 12292
  19.9 9.7 %copy-start.2 = (f32[4096]{0:T(1024)S(1)}, f32[4096]{0:T(1024)}, u32[]{:S(2)}) copy-start(f32[4096]{0:T(1024)} %param.10) | copy-start | bytes 49156

commit v7 on v5

--- a/solution.py
+++ b/solution.py
@@ -15,6 +15,7 @@
 BF16 = jnp.bfloat16
 VMEM_BYTES = 32 * 1024 * 1024
 PICK_BYTES = 63_000_000
+CHUNKS = 4
 
 
 def repeat_steps(count, body, carry):
@@ -186,7 +187,6 @@
     groups = species // ROWS
     all_groups = LANES // cap
     rows = all_groups * ROWS
-    sent = out_ref.shape[2] // LANES
     blocks = nodes // LANES
     width = lines * blocks
     segments = LANES // width
@@ -285,16 +285,25 @@
     second = [jnp.where(head, s + b * e + a * e, s) for s, e in zip(second, entry)]
     distance = 1
     while distance < blocks * segments:
-        opened = segment >= distance
-        a_open, b_open = jnp.where(opened, a, 0.0), jnp.where(opened, b, 0.0)
-        ahead = [earlier(f, distance) for f in first]
-        second = [s + b_open * f + a_open * earlier(s, distance) for s, f in zip(second, ahead)]
-        first = [f + a_open * e for f, e in zip(first, ahead)]
-        if 2 * distance < blocks * segments:
-            a_ahead = earlier(a, distance)
-            b = b * a_ahead + a * earlier(b, distance)
-            a = a * a_ahead
-        distance *= 2
+        run_a, run_b = a, b
+        next_first, next_second = first, second
+        for k in range(1, 4):
+            if k * distance >= blocks * segments:
+                break
+            opened = segment >= k * distance
+            a_open, b_open = jnp.where(opened, run_a, 0.0), jnp.where(opened, run_b, 0.0)
+            ahead = [earlier(f, k * distance) for f in first]
+            next_first = [n + a_open * f for n, f in zip(next_first, ahead)]
+            next_second = [
+                n + b_open * f + a_open * earlier(s, k * distance)
+                for n, s, f in zip(next_second, second, ahead)
+            ]
+            a_ahead = earlier(a, k * distance)
+            run_b = run_b * a_ahead + run_a * earlier(b, k * distance)
+            run_a = run_a * a_ahead
+        first, second = next_first, next_second
+        a, b = run_a, run_b
+        distance *= 4
     carry_one = [jnp.where(head, e, earlier(f, 1)) for e, f in zip(entry, first)]
     carry_two = [jnp.where(head, e, earlier(s, 1)) for e, s in zip(entry, second)]
     columns = [
@@ -319,45 +328,52 @@
         axis=0,
     ).astype(BF16)
     half = times // 2
-    base = jnp.concatenate(
-        [
-            jnp.concatenate(columns[:half], axis=1),
-            jnp.concatenate(columns[half:], axis=1),
-        ],
-        axis=0,
-    )
-    iterate = base
-    for step in range(NEWTON):
-        high, low = rounded(jnp.tanh(iterate))
-        right = jnp.concatenate(
+    depth = half // CHUNKS
+    bases = [
+        jnp.concatenate(
             [
-                high[:species],
-                high[:species],
-                low[:species],
-                high[species:],
-                high[species:],
-                low[species:],
+                jnp.concatenate(columns[offset + c * depth : offset + (c + 1) * depth], axis=1)
+                for offset in (0, half)
             ],
             axis=0,
-        ).astype(BF16)
-        iterate = base - jnp.dot(left, right, preferred_element_type=F32)
-    iterate = jnp.concatenate([iterate[:species], iterate[species:]], axis=1)
+        )
+        for c in range(CHUNKS)
+    ]
+    iterates = list(bases)
+    for step in range(NEWTON):
+        for c in range(CHUNKS):
+            high, low = rounded(jnp.tanh(iterates[c]))
+            right = jnp.concatenate(
+                [
+                    high[:species],
+                    high[:species],
+                    low[:species],
+                    high[species:],
+                    high[species:],
+                    low[species:],
+                ],
+                axis=0,
+            ).astype(BF16)
+            iterates[c] = bases[c] - jnp.dot(left, right, preferred_element_type=F32)
 
     length = jnp.zeros((ROWS, LANES), jnp.int32)
     for one_line in range(lines):
-        length = jnp.where(line == one_line, length_ref[0, one_line], length)
+        one_length = jnp.broadcast_to(length_ref[:, one_line : one_line + 1], (ROWS, LANES))
+        length = jnp.where(line == one_line, one_length, length)
     node = block * LANES + part * times
-    weight = jnp.concatenate(
-        [
-            jnp.where(node + t < length, jnp.broadcast_to(flux[t : t + 1], (ROWS, LANES)), 0.0)
-            for t in range(times)
-        ],
-        axis=1,
-    )
-    first_row = lax.broadcasted_iota(jnp.int32, weight.shape, 0) == 0
-    scaled = [iterate[ROWS * g : ROWS * (g + 1)] * weight for g in range(groups)]
-    scaled.append(jnp.where(first_row, weight, 0.0))
-    left = split(jnp.concatenate(scaled, axis=0))
+    top = lax.broadcasted_iota(jnp.int32, (ROWS, LANES), 0) == 0
+    pieces = []
+    for t in range(times):
+        weight = jnp.broadcast_to(flux[t : t + 1], (ROWS, LANES))
+        weight = jnp.where(node + t < length, weight, 0.0)
+        chunk, place = t % half // depth, t % half % depth
+        found = iterates[chunk][
+            t // half * species : (t // half + 1) * species, LANES * place : LANES * (place + 1)
+        ]
+        scaled = [found[ROWS * g : ROWS * (g + 1)] * weight for g in range(groups)]
+        scaled.append(jnp.where(top, weight, 0.0))
+        pieces.append(jnp.concatenate(scaled, axis=0))
+    left = split(jnp.concatenate(pieces, axis=1))
     relative = lane_groups(cap, here + bundle)
 
     def scatter(k, carry):
@@ -368,12 +384,6 @@
             preferred_element_type=F32,
         )
         sums = sums[:rows] + sums[rows:]
-        last = [sums[species : species + 1]]
-        last += [
-            sums[ROWS * g + r : ROWS * g + r + 1] for g in range(groups) for r in range(sent, ROWS)
-        ]
-        last.append(jnp.zeros((ROWS - len(last), 2 * LANES), F32))
-        sums = jnp.concatenate([sums[:species]] + last, axis=0)
         for half in range(2):
             tiles = pack(
                 [
@@ -387,10 +397,7 @@
             for j in range(all_groups):
                 owner = k * chunk_owners + half * all_groups + j
                 for copy in range(copies):
-                    for r in range(sent):
-                        out_ref[owner * copies + copy, :, LANES * r : LANES * (r + 1)] = tiles[j][
-                            r : r + 1
-                        ]
+                    out_ref[owner * copies + copy] = tiles[j]
         return carry
 
     repeat_steps(chunks, scatter, 0)
@@ -398,7 +405,6 @@
 
 def blend_kernel(bundles, sums_ref, request_ref, pore_ref, cell_ref, out_hbm, out_ref, out_sem):
     owners = sums_ref.shape[0] // bundles
-    sent = sums_ref.shape[2] // LANES
     species, cells = cell_ref.shape
     cap = request_ref.shape[3]
     all_groups = LANES // cap
@@ -408,13 +414,6 @@
     chunks = owners // ROWS
     here = lax.axis_index("grid")
     sublane = lax.broadcasted_iota(jnp.int32, (ROWS, LANES), 0)
-
-    def tile(device, bundle):
-        value = jnp.zeros((ROWS, LANES), F32)
-        for r in range(sent):
-            row = sums_ref[device * bundles + bundle, :, LANES * r : LANES * (r + 1)]
-            value = jnp.where(sublane == r, jnp.broadcast_to(row, (ROWS, LANES)), value)
-        return value
 
     def chunk(k, total):
         values, weights, indices = [], [], []
@@ -439,20 +438,15 @@
                 )
             for d in range(ROWS):
                 found = unpack(
-                    [tile(k * ROWS + d, t * all_groups + j) for j in range(all_groups)],
+                    [
+                        sums_ref[(k * ROWS + d) * bundles + t * all_groups + j]
+                        for j in range(all_groups)
+                    ],
                     cap,
                     lane_groups(cap, here + d),
                     all_groups,
                 )
                 weights.append(found[groups][:1])
-                spare = 1
-                for g in range(groups):
-                    for r in range(sent, ROWS):
-                        row = jnp.broadcast_to(
-                            found[groups][spare : spare + 1], (ROWS, LANES)
-                        )
-                        found[g] = jnp.where(sublane == r, row, found[g])
-                        spare += 1
                 values.append(jnp.concatenate(found[:groups], axis=0))
                 indices.append(block[d : d + 1])
         parts = split(jnp.concatenate(values, axis=1))
@@ -540,7 +534,6 @@
     interaction,
 ):
     owners, cap = request_cell.shape[2:]
-    sent = -(-(cell_state.shape[0] + 1) // (LANES // cap))
     outgoing = call(
         pick_kernel,
         (owners, ROWS, LANES),
@@ -557,9 +550,8 @@
     table = lax.all_to_all(outgoing, "grid", split_axis=0, concat_axis=0, tiled=True)
     sums = call(
         functools.partial(lines_kernel, cap),
-        (owners * bundles, 1, sent * LANES),
+        (owners * bundles, ROWS, LANES),
         (table, node_slot, line_length, courant, flux_weight, inflow, interaction),
-        kinds={2: pltpu.SMEM},
     )
     back = lax.all_to_all(sums, ("grid", "bundle"), split_axis=0, concat_axis=0, tiled=True)
     return call(

time: 31.2 us -> 30.7 us (0.984)
  Pallas kernels: 6.85 us -> 6.1 us
    pallas_call x3, Pallas kernels: 6.85 us -> 6.1 us  [call(): pl.pallas_call(kernel, out_shape=jax.ShapeDtypeStruct(shape, F32), in_spe...]
where the time goes in v7:
time: 30.7 us; the launch traced here: 30.4 us
  blocking collectives  24.1 us (79%)
  Pallas kernels  6.1 us (20%)
    all_to_all x1, blocking collectives, shards(): lax.all_to_all(outgoing, 'grid', split_axis=0, concat_axis=0, tiled=True)  14.1 us
    all_to_all x1, blocking collectives, shards(): lax.all_to_all(sums, ('grid', 'bundle'), split_axis=0, concat_axis=0, til...  10 us
    pallas_call x3, Pallas kernels, call(): pl.pallas_call(kernel, out_shape=jax.ShapeDtypeStruct(shape, F32), in_spe...  6.1 us

profile of v7, /device:TPU:0, one launch (start us, length us, event | category | flops | bytes accessed | tf_op | source)
XLA Modules:
  0.0 30.4 jit_solution(5535821420796843249)
XLA Ops:
  0.0 0.0 copy-start
  0.0 2.1 %shard_map.91 = f32[8,8,128]{2,1,0:T(8,128)} custom-call(f32[24,4096]{1,0:T(8,128)} %cell_ref.1, s32[4,1,8,32]{3,2,1,0:T(8,128)} %request_ref.1), custom_call_target="tpu_custom_call" | custom-call | tf_op jit(solution)/shard_map/pallas_call | solution.py:512
  2.1 0.0 copy-start.2
  2.1 0.0 copy-start.3
  2.1 0.0 copy-start.4
  2.1 0.0 copy-start.6
  2.1 0.0 copy-start.7
  2.1 0.0 copy-start.8
  2.1 14.1 %all_to_all.10.table_ref = f32[8,8,128]{2,1,0:T(8,128)S(1)} all-to-all(f32[8,8,128]{2,1,0:T(8,128)} %shard_map.91), channel_id=1, replica_groups=mesh['grid'=8,'bundle'=4] {'grid'}, dimensions={0} | all-to-all | bytes 65536 | tf_op jit(solution)/shard_map/all_to_all | solution.py:550
  16.2 0.0 copy-done.2
  16.2 0.0 copy-done.3
  16.2 0.0 copy-done.4
  16.3 0.0 copy-done.6
  16.3 0.0 copy-done.7
  16.3 0.0 copy-done.8
  16.3 2.4 %shard_map.92 = f32[32,8,128]{2,1,0:T(8,128)S(1)} custom-call(f32[8,8,128]{2,1,0:T(8,128)S(1)} %all_to_all.10.table_ref, s32[1,2,2048]{2,1,0:T(2,128)S(1)} %copy-done.2, s32[1,2]{1,0:T(1,128)S(1)} %copy-done.7, f32[1,2,2048]{2,1,0:T(2,128)S(1)} %copy-done.3, f32[1,2,2048]{2,1,0:T(2,128)S(1)} %copy-done.4, f32[1,24]{1,0:T(1,128)S(1)} %copy-done.8, ...), custom_call_target="tpu_custom_call" | custom-call | tf_op jit(solution)/shard_map/pallas_call | solution.py:512
  18.7 0.0 copy-start.1
  18.7 0.0 copy-start.5
  18.7 10.0 %all_to_all.11.sums_ref = f32[32,8,128]{2,1,0:T(8,128)S(1)} all-to-all(f32[32,8,128]{2,1,0:T(8,128)S(1)} %shard_map.92), channel_id=1, replica_groups=mesh['grid'=8,'bundle'=4] {'grid','bundle'}, dimensions={0} | all-to-all | bytes 262144 | tf_op jit(solution)/shard_map/all_to_all | solution.py:556
  28.8 0.0 copy-done
  28.8 0.0 copy-done.1
  28.8 0.0 copy-done.5
  28.8 1.6 %shard_map.93 = f32[24,4096]{1,0:T(8,128)} custom-call(f32[32,8,128]{2,1,0:T(8,128)S(1)} %all_to_all.11.sums_ref, s32[4,1,8,32]{3,2,1,0:T(8,128)S(1)} %copy-done.1, f32[1,4096]{1,0:T(1,128)S(1)} %bitcast.1, f32[24,4096]{1,0:T(8,128)S(1)} %copy-done), custom_call_target="tpu_custom_call" | custom-call | tf_op jit(solution)/shard_map/pallas_call | solution.py:512
Async XLA Ops:
  0.0 28.8 %copy-start = (f32[24,4096]{1,0:T(8,128)S(1)}, f32[24,4096]{1,0:T(8,128)}, u32[]{:S(2)}) copy-start(f32[24,4096]{1,0:T(8,128)} %cell_ref.1) | copy-start | bytes 1179652
  2.1 14.2 %copy-start.2 = (s32[1,2,2048]{2,1,0:T(2,128)S(1)}, s32[1,2,2048]{2,1,0:T(2,128)}, u32[]{:S(2)}) copy-start(s32[1,2,2048]{2,1,0:T(2,128)} %slot_ref.1) | copy-start | bytes 49156
  2.1 14.2 %copy-start.3 = (f32[1,2,2048]{2,1,0:T(2,128)S(1)}, f32[1,2,2048]{2,1,0:T(2,128)}, u32[]{:S(2)}) copy-start(f32[1,2,2048]{2,1,0:T(2,128)} %courant_ref.1) | copy-start | bytes 49156
  2.1 14.2 %copy-start.4 = (f32[1,2,2048]{2,1,0:T(2,128)S(1)}, f32[1,2,2048]{2,1,0:T(2,128)}, u32[]{:S(2)}) copy-start(f32[1,2,2048]{2,1,0:T(2,128)} %flux_ref.1) | copy-start | bytes 49156
  2.1 14.2 %copy-start.6 = (f32[24,24]{1,0:T(8,128)S(1)}, f32[24,24]{1,0:T(8,128)}, u32[]{:S(2)}) copy-start(f32[24,24]{1,0:T(8,128)} %interaction_ref.1) | copy-start | bytes 6916
  2.1 14.2 %copy-start.7 = (s32[1,2]{1,0:T(1,128)S(1)}, s32[1,2]{1,0:T(1,128)}, u32[]{:S(2)}) copy-start(s32[1,2]{1,0:T(1,128)} %length_ref.1) | copy-start | bytes 28
  2.1 14.2 %copy-start.8 = (f32[1,24]{1,0:T(1,128)S(1)}, f32[1,24]{1,0:T(1,128)}, u32[]{:S(2)}) copy-start(f32[1,24]{1,0:T(1,128)} %inflow_ref.1) | copy-start | bytes 292
  18.7 10.1 %copy-start.1 = (s32[4,1,8,32]{3,2,1,0:T(8,128)S(1)}, s32[4,1,8,32]{3,2,1,0:T(8,128)}, u32[]{:S(2)}) copy-start(s32[4,1,8,32]{3,2,1,0:T(8,128)} %request_ref.1) | copy-start | bytes 12292
  18.7 10.0 %copy-start.5 = (f32[4096]{0:T(1024)S(1)}, f32[4096]{0:T(1024)}, u32[]{:S(2)}) copy-start(f32[4096]{0:T(1024)} %param.10) | copy-start | bytes 49156

commit v8 on v7

--- a/solution.py
+++ b/solution.py
@@ -14,7 +14,6 @@
 F32 = jnp.float32
 BF16 = jnp.bfloat16
 VMEM_BYTES = 32 * 1024 * 1024
-PICK_BYTES = 63_000_000
 CHUNKS = 4
 
 
@@ -90,24 +89,22 @@
     return jnp.sum(jnp.where(rows == lanes, wide, 0), axis=0, keepdims=True)
 
 
-def pick_kernel(cell_hbm, request_hbm, out_ref, cell_ref, request_ref, cell_sem, request_sem):
-    request_copy = pltpu.make_async_copy(
-        request_hbm.at[lax.axis_index("bundle"), 0], request_ref, request_sem
-    )
-    cell_copy = pltpu.make_async_copy(cell_hbm, cell_ref, cell_sem)
-    request_copy.start()
-    cell_copy.start()
+def first_kernel(out_ref):
+    out_ref[...] = jnp.zeros_like(out_ref)
+
+
+def pick_kernel(cell_ref, request_ref, first_ref, out_ref):
     species, cells = cell_ref.shape
-    owners, cap = request_ref.shape
+    owners, cap = request_ref.shape[2:]
+    bundle = lax.axis_index("bundle")
     groups = LANES // cap
     chunks = owners // (2 * groups)
     highs = cells // LANES
     here = lax.axis_index("grid")
     relative = lane_groups(cap, here)
-    request_copy.wait()
 
     def wanted(k):
-        block = request_ref[pl.ds(k * 2 * groups, 2 * groups), :]
+        block = request_ref[bundle, 0, pl.ds(k * 2 * groups, 2 * groups), :]
         index = jnp.concatenate(
             [spread_rows(block[:groups], cap), spread_rows(block[groups:], cap)], axis=1
         )
@@ -121,7 +118,6 @@
         return high, jnp.concatenate([hot, hot], axis=0)
 
     kept = wanted(0) if chunks == 1 else None
-    cell_copy.wait()
     cell = cell_ref[...]
     stacked = jnp.concatenate(
         [cell[:, LANES * h : LANES * (h + 1)] for h in range(highs)], axis=0
@@ -508,7 +504,7 @@
         copy.wait()
 
 
-def call(kernel, shape, operands, kinds={}, scratch=(), grant=VMEM_BYTES, out=pltpu.VMEM):
+def call(kernel, shape, operands, kinds={}, scratch=(), out=pltpu.VMEM, flops=0):
     return pl.pallas_call(
         kernel,
         out_shape=jax.ShapeDtypeStruct(shape, F32),
@@ -517,7 +513,8 @@
         ],
         out_specs=pl.BlockSpec(memory_space=out),
         scratch_shapes=list(scratch),
-        compiler_params=pltpu.CompilerParams(vmem_limit_bytes=grant),
+        compiler_params=pltpu.CompilerParams(vmem_limit_bytes=VMEM_BYTES),
+        cost_estimate=pl.CostEstimate(flops=flops, bytes_accessed=0, transcendentals=0),
     )(*operands)
 
 
@@ -534,18 +531,11 @@
     interaction,
 ):
     owners, cap = request_cell.shape[2:]
+    first = call(first_kernel, (ROWS, LANES), (), flops=10**9)
     outgoing = call(
         pick_kernel,
         (owners, ROWS, LANES),
-        (cell_state, request_cell),
-        kinds={0: pltpu.HBM, 1: pltpu.HBM},
-        scratch=(
-            pltpu.VMEM(cell_state.shape, F32),
-            pltpu.VMEM((owners, cap), jnp.int32),
-            pltpu.SemaphoreType.DMA,
-            pltpu.SemaphoreType.DMA,
-        ),
-        grant=PICK_BYTES,
+        (cell_state, request_cell, first),
     )
     table = lax.all_to_all(outgoing, "grid", split_axis=0, concat_axis=0, tiled=True)
     sums = call(

time: 30.7 us -> 29.8 us (0.971)
  Pallas kernels: 6.1 us -> 4.5 us
  local copies, waits for them, and re-layouts: 0.05 us -> 1.05 us
    pallas_call x3 -> x4, Pallas kernels: 6.1 us -> 4.5 us  [call(): pl.pallas_call(kernel, out_shape=jax.ShapeDtypeStruct(shape, F32), in_spe...]
    unnamed x18, local copies, waits for them, and re-layouts: 0.05 us -> 1.05 us
where the time goes in v8:
time: 29.8 us; the launch traced here: 29.6 us
  blocking collectives  23.9 us (80%)
  Pallas kernels  4.5 us (15%)
  local copies, waits for them, and re-layouts  1.05 us (4%)
    all_to_all x1, blocking collectives, shards(): lax.all_to_all(outgoing, 'grid', split_axis=0, concat_axis=0, tiled=True)  13.9 us
    all_to_all x1, blocking collectives, shards(): lax.all_to_all(sums, ('grid', 'bundle'), split_axis=0, concat_axis=0, til...  10 us
    pallas_call x4, Pallas kernels, call(): pl.pallas_call(kernel, out_shape=jax.ShapeDtypeStruct(shape, F32), in_spe...  4.5 us
    unnamed x18, local copies, waits for them, and re-layouts  1.05 us

profile of v8, /device:TPU:0, one launch (start us, length us, event | category | flops | bytes accessed | tf_op | source)
XLA Modules:
  0.0 29.6 jit_solution(4677703270072314568)
XLA Ops:
  0.0 0.0 copy-start.1
  0.0 0.0 copy-start
  0.0 0.7 %copy-done.1 = s32[4,1,8,32]{3,2,1,0:T(8,128)S(1)} copy-done((s32[4,1,8,32]{3,2,1,0:T(8,128)S(1)}, s32[4,1,8,32]{3,2,1,0:T(8,128)}, u32[]{:S(2)}) %copy-start.1) | copy-done | bytes 4120
  0.7 0.3 copy-done
  1.0 0.5 %shard_map.92 = f32[8,8,128]{2,1,0:T(8,128)S(1)} custom-call(f32[24,4096]{1,0:T(8,128)S(1)} %copy-done, s32[4,1,8,32]{3,2,1,0:T(8,128)S(1)} %copy-done.1, f32[8,128]{1,0:T(8,128)S(1)} %shard_map.91.first_ref), custom_call_target="tpu_custom_call" | custom-call | tf_op jit(solution)/shard_map/pallas_call | solution.py:508
  1.5 0.0 copy-start.2
  1.5 0.0 copy-start.3
  1.5 0.0 copy-start.4
  1.5 0.0 copy-start.6
  1.5 0.0 copy-start.7
  1.5 0.0 copy-start.8
  1.6 13.9 %all_to_all.10.table_ref = f32[8,8,128]{2,1,0:T(8,128)S(1)} all-to-all(f32[8,8,128]{2,1,0:T(8,128)S(1)} %shard_map.92), channel_id=1, replica_groups=mesh['grid'=8,'bundle'=4] {'grid'}, dimensions={0} | all-to-all | bytes 65536 | tf_op jit(solution)/shard_map/all_to_all | solution.py:540
  15.4 0.0 copy-done.2
  15.4 0.0 copy-done.3
  15.4 0.0 copy-done.4
  15.5 0.0 copy-done.6
  15.5 0.0 copy-done.7
  15.5 0.0 copy-done.8
  15.5 2.4 %shard_map.93 = f32[32,8,128]{2,1,0:T(8,128)S(1)} custom-call(f32[8,8,128]{2,1,0:T(8,128)S(1)} %all_to_all.10.table_ref, s32[1,2,2048]{2,1,0:T(2,128)S(1)} %copy-done.2, s32[1,2]{1,0:T(1,128)S(1)} %copy-done.7, f32[1,2,2048]{2,1,0:T(2,128)S(1)} %copy-done.3, f32[1,2,2048]{2,1,0:T(2,128)S(1)} %copy-done.4, f32[1,24]{1,0:T(1,128)S(1)} %copy-done.8, ...), custom_call_target="tpu_custom_call" | custom-call | tf_op jit(solution)/shard_map/pallas_call | solution.py:508
  17.9 0.0 copy-start.5
  17.9 10.0 %all_to_all.11.sums_ref = f32[32,8,128]{2,1,0:T(8,128)S(1)} all-to-all(f32[32,8,128]{2,1,0:T(8,128)S(1)} %shard_map.93), channel_id=1, replica_groups=mesh['grid'=8,'bundle'=4] {'grid','bundle'}, dimensions={0} | all-to-all | bytes 262144 | tf_op jit(solution)/shard_map/all_to_all | solution.py:546
  28.0 0.0 copy-done.5
  28.0 1.6 %shard_map.94 = f32[24,4096]{1,0:T(8,128)} custom-call(f32[32,8,128]{2,1,0:T(8,128)S(1)} %all_to_all.11.sums_ref, s32[4,1,8,32]{3,2,1,0:T(8,128)S(1)} %copy-done.1, f32[1,4096]{1,0:T(1,128)S(1)} %bitcast.1, f32[24,4096]{1,0:T(8,128)S(1)} %copy-done), custom_call_target="tpu_custom_call" | custom-call | tf_op jit(solution)/shard_map/pallas_call | solution.py:508
  (1 shorter events, 0.0 us)
Async XLA Ops:
  0.0 0.7 %copy-start.1 = (s32[4,1,8,32]{3,2,1,0:T(8,128)S(1)}, s32[4,1,8,32]{3,2,1,0:T(8,128)}, u32[]{:S(2)}) copy-start(s32[4,1,8,32]{3,2,1,0:T(8,128)} %request_ref.3) | copy-start | bytes 12292
  0.0 1.0 %copy-start = (f32[24,4096]{1,0:T(8,128)S(1)}, f32[24,4096]{1,0:T(8,128)}, u32[]{:S(2)}) copy-start(f32[24,4096]{1,0:T(8,128)} %cell_ref.3) | copy-start | bytes 1179652
  1.5 14.0 %copy-start.2 = (s32[1,2,2048]{2,1,0:T(2,128)S(1)}, s32[1,2,2048]{2,1,0:T(2,128)}, u32[]{:S(2)}) copy-start(s32[1,2,2048]{2,1,0:T(2,128)} %slot_ref.1) | copy-start | bytes 49156
  1.5 14.0 %copy-start.3 = (f32[1,2,2048]{2,1,0:T(2,128)S(1)}, f32[1,2,2048]{2,1,0:T(2,128)}, u32[]{:S(2)}) copy-start(f32[1,2,2048]{2,1,0:T(2,128)} %courant_ref.1) | copy-start | bytes 49156
  1.5 14.0 %copy-start.4 = (f32[1,2,2048]{2,1,0:T(2,128)S(1)}, f32[1,2,2048]{2,1,0:T(2,128)}, u32[]{:S(2)}) copy-start(f32[1,2,2048]{2,1,0:T(2,128)} %flux_ref.1) | copy-start | bytes 49156
  1.5 13.9 %copy-start.6 = (f32[24,24]{1,0:T(8,128)S(1)}, f32[24,24]{1,0:T(8,128)}, u32[]{:S(2)}) copy-start(f32[24,24]{1,0:T(8,128)} %interaction_ref.1) | copy-start | bytes 6916
  1.5 13.9 %copy-start.7 = (s32[1,2]{1,0:T(1,128)S(1)}, s32[1,2]{1,0:T(1,128)}, u32[]{:S(2)}) copy-start(s32[1,2]{1,0:T(1,128)} %length_ref.1) | copy-start | bytes 28
  1.5 13.9 %copy-start.8 = (f32[1,24]{1,0:T(1,128)S(1)}, f32[1,24]{1,0:T(1,128)}, u32[]{:S(2)}) copy-start(f32[1,24]{1,0:T(1,128)} %inflow_ref.1) | copy-start | bytes 292
  17.9 10.0 %copy-start.5 = (f32[4096]{0:T(1024)S(1)}, f32[4096]{0:T(1024)}, u32[]{:S(2)}) copy-start(f32[4096]{0:T(1024)} %param.10) | copy-start | bytes 49156

commit v9 on v8

--- a/solution.py
+++ b/solution.py
@@ -15,6 +15,7 @@
 BF16 = jnp.bfloat16
 VMEM_BYTES = 32 * 1024 * 1024
 CHUNKS = 4
+GATHERED = 16
 
 
 def repeat_steps(count, body, carry):
@@ -166,6 +167,7 @@
 
 
 def lines_kernel(
+    copies,
     cap,
     table_ref,
     slot_ref,
@@ -176,8 +178,7 @@
     interaction_ref,
     out_ref,
 ):
-    owners = table_ref.shape[0]
-    copies = out_ref.shape[0] // owners
+    owners = out_ref.shape[0] // copies
     species = inflow_ref.shape[1]
     lines, nodes = slot_ref.shape[1:]
     groups = species // ROWS
@@ -213,6 +214,9 @@
 
     relative = lane_groups(cap, here)
 
+    def incoming(owner):
+        return table_ref[owner * owners + here if table_ref.shape[0] > owners else owner]
+
     def gather(k, state):
         halves = []
         for half in range(2):
@@ -220,7 +224,7 @@
             halves.append(
                 jnp.concatenate(
                     unpack(
-                        [table_ref[first + j] for j in range(all_groups)], cap, relative, groups
+                        [incoming(first + j) for j in range(all_groups)], cap, relative, groups
                     ),
                     axis=0,
                 )
@@ -537,9 +541,12 @@
         (owners, ROWS, LANES),
         (cell_state, request_cell, first),
     )
-    table = lax.all_to_all(outgoing, "grid", split_axis=0, concat_axis=0, tiled=True)
+    if owners <= GATHERED:
+        table = lax.all_gather(outgoing, "grid", axis=0, tiled=True)
+    else:
+        table = lax.all_to_all(outgoing, "grid", split_axis=0, concat_axis=0, tiled=True)
     sums = call(
-        functools.partial(lines_kernel, cap),
+        functools.partial(lines_kernel, bundles, cap),
         (owners * bundles, ROWS, LANES),
         (table, node_slot, line_length, courant, flux_weight, inflow, interaction),
     )

time: 29.8 us -> 52.2 us (1.75)
  blocking collectives: 23.9 us -> 46.3 us
    all_gather x0 -> x1, blocking collectives: none -> 32.7 us  [shards(): table = lax.all_gather(outgoing, 'grid', axis=0, tiled=True)]
    all_to_all x1 -> x0, blocking collectives: 13.9 us -> none  [shards(): lax.all_to_all(outgoing, 'grid', split_axis=0, concat_axis=0, tiled=True)]
    all_to_all x1, blocking collectives: 10 us -> 13.6 us  [shards(): lax.all_to_all(sums, ('grid', 'bundle'), split_axis=0, concat_axis=0, til...]
where the time goes in v9:
time: 52.2 us; the launch traced here: 51.9 us
  blocking collectives  46.3 us (89%)
  Pallas kernels  4.52 us (9%)
  local copies, waits for them, and re-layouts  1.05 us (2%)
    all_gather x1, blocking collectives, shards(): table = lax.all_gather(outgoing, 'grid', axis=0, tiled=True)  32.7 us
    all_to_all x1, blocking collectives, shards(): lax.all_to_all(sums, ('grid', 'bundle'), split_axis=0, concat_axis=0, til...  13.6 us
    pallas_call x4, Pallas kernels, call(): pl.pallas_call(kernel, out_shape=jax.ShapeDtypeStruct(shape, F32), in_spe...  4.52 us
    unnamed x18, local copies, waits for them, and re-layouts  1.05 us

profile of v9, /device:TPU:0, one launch (start us, length us, event | category | flops | bytes accessed | tf_op | source)
XLA Modules:
  0.0 51.9 jit_solution(10942735979033065089)
XLA Ops:
  0.0 0.0 copy-start.1
  0.0 0.0 copy-start
  0.0 0.7 %copy-done.1 = s32[4,1,8,32]{3,2,1,0:T(8,128)S(1)} copy-done((s32[4,1,8,32]{3,2,1,0:T(8,128)S(1)}, s32[4,1,8,32]{3,2,1,0:T(8,128)}, u32[]{:S(2)}) %copy-start.1) | copy-done | bytes 4120
  0.7 0.3 copy-done
  1.0 0.5 shard_map.92
  1.5 0.0 copy-start.2
  1.5 0.0 copy-start.3
  1.5 0.0 copy-start.4
  1.5 0.0 copy-start.6
  1.5 0.0 copy-start.7
  1.5 0.0 copy-start.8
  1.6 32.7 %all_gather.3.table_ref = f32[64,8,128]{2,1,0:T(8,128)S(1)} all-gather(f32[8,8,128]{2,1,0:T(8,128)S(1)} %shard_map.92), channel_id=1, replica_groups=mesh['grid'=8,'bundle'=4] {'grid'}, dimensions={0}, use_global_device_ids=true | all-gather | bytes 294912 | tf_op jit(solution)/shard_map/all_gather | solution.py:545
  34.2 0.0 copy-done.2
  34.2 0.0 copy-done.3
  34.2 0.0 copy-done.4
  34.2 0.0 copy-done.6
  34.2 0.0 copy-done.7
  34.2 0.0 copy-done.8
  34.3 2.4 %shard_map.93 = f32[32,8,128]{2,1,0:T(8,128)S(1)} custom-call(f32[64,8,128]{2,1,0:T(8,128)S(1)} %all_gather.3.table_ref, s32[1,2,2048]{2,1,0:T(2,128)S(1)} %copy-done.2, s32[1,2]{1,0:T(1,128)S(1)} %copy-done.7, f32[1,2,2048]{2,1,0:T(2,128)S(1)} %copy-done.3, f32[1,2,2048]{2,1,0:T(2,128)S(1)} %copy-done.4, f32[1,24]{1,0:T(1,128)S(1)} %copy-done.8, ...), custom_call_target="tpu_custom_call" | custom-call | tf_op jit(solution)/shard_map/pallas_call | solution.py:512
  36.7 0.0 copy-start.5
  36.7 13.6 %all_to_all.5.sums_ref = f32[32,8,128]{2,1,0:T(8,128)S(1)} all-to-all(f32[32,8,128]{2,1,0:T(8,128)S(1)} %shard_map.93), channel_id=1, replica_groups=mesh['grid'=8,'bundle'=4] {'grid','bundle'}, dimensions={0} | all-to-all | bytes 262144 | tf_op jit(solution)/shard_map/all_to_all | solution.py:553
  50.3 0.0 copy-done.5
  50.3 1.6 %shard_map.94 = f32[24,4096]{1,0:T(8,128)} custom-call(f32[32,8,128]{2,1,0:T(8,128)S(1)} %all_to_all.5.sums_ref, s32[4,1,8,32]{3,2,1,0:T(8,128)S(1)} %copy-done.1, f32[1,4096]{1,0:T(1,128)S(1)} %bitcast.1, f32[24,4096]{1,0:T(8,128)S(1)} %copy-done), custom_call_target="tpu_custom_call" | custom-call | tf_op jit(solution)/shard_map/pallas_call | solution.py:512
  (1 shorter events, 0.0 us)
Async XLA Ops:
  0.0 0.7 %copy-start.1 = (s32[4,1,8,32]{3,2,1,0:T(8,128)S(1)}, s32[4,1,8,32]{3,2,1,0:T(8,128)}, u32[]{:S(2)}) copy-start(s32[4,1,8,32]{3,2,1,0:T(8,128)} %request_ref.3) | copy-start | bytes 12292
  0.0 1.0 %copy-start = (f32[24,4096]{1,0:T(8,128)S(1)}, f32[24,4096]{1,0:T(8,128)}, u32[]{:S(2)}) copy-start(f32[24,4096]{1,0:T(8,128)} %cell_ref.3) | copy-start | bytes 1179652
  1.5 32.7 %copy-start.2 = (s32[1,2,2048]{2,1,0:T(2,128)S(1)}, s32[1,2,2048]{2,1,0:T(2,128)}, u32[]{:S(2)}) copy-start(s32[1,2,2048]{2,1,0:T(2,128)} %slot_ref.1) | copy-start | bytes 49156
  1.5 32.7 %copy-start.3 = (f32[1,2,2048]{2,1,0:T(2,128)S(1)}, f32[1,2,2048]{2,1,0:T(2,128)}, u32[]{:S(2)}) copy-start(f32[1,2,2048]{2,1,0:T(2,128)} %courant_ref.1) | copy-start | bytes 49156
  1.5 32.7 %copy-start.4 = (f32[1,2,2048]{2,1,0:T(2,128)S(1)}, f32[1,2,2048]{2,1,0:T(2,128)}, u32[]{:S(2)}) copy-start(f32[1,2,2048]{2,1,0:T(2,128)} %flux_ref.1) | copy-start | bytes 49156
  1.5 32.7 %copy-start.6 = (f32[24,24]{1,0:T(8,128)S(1)}, f32[24,24]{1,0:T(8,128)}, u32[]{:S(2)}) copy-start(f32[24,24]{1,0:T(8,128)} %interaction_ref.1) | copy-start | bytes 6916
  1.5 32.7 %copy-start.7 = (s32[1,2]{1,0:T(1,128)S(1)}, s32[1,2]{1,0:T(1,128)}, u32[]{:S(2)}) copy-start(s32[1,2]{1,0:T(1,128)} %length_ref.1) | copy-start | bytes 28
  1.5 32.7 %copy-start.8 = (f32[1,24]{1,0:T(1,128)S(1)}, f32[1,24]{1,0:T(1,128)}, u32[]{:S(2)}) copy-start(f32[1,24]{1,0:T(1,128)} %inflow_ref.1) | copy-start | bytes 292
  36.7 13.6 %copy-start.5 = (f32[4096]{0:T(1024)S(1)}, f32[4096]{0:T(1024)}, u32[]{:S(2)}) copy-start(f32[4096]{0:T(1024)} %param.10) | copy-start | bytes 49156

commit v10 on v8

--- a/solution.py
+++ b/solution.py
@@ -150,15 +150,9 @@
     repeat_steps(chunks, chunk, 0)
 
 
-def to_segments(values):
-    lines, nodes = values[0].shape
-    blocks = nodes // LANES
-    width = lines * blocks
+def to_segments(values, width):
     groups = LANES // width
-    stacked = []
-    for value in values:
-        value = value.astype(F32)
-        stacked += [value[:, LANES * block : LANES * (block + 1)] for block in range(blocks)]
+    stacked = [value.astype(F32) for value in values]
     stacked.append(jnp.zeros((LANES - width * len(values), LANES), F32))
     turned = jnp.transpose(jnp.concatenate(stacked, axis=0))
     times = LANES // groups
@@ -166,6 +160,7 @@
 
 
 def lines_kernel(
+    lines,
     cap,
     table_ref,
     slot_ref,
@@ -175,39 +170,47 @@
     inflow_ref,
     interaction_ref,
     out_ref,
+    rows_ref,
 ):
     owners = table_ref.shape[0]
     copies = out_ref.shape[0] // owners
     species = inflow_ref.shape[1]
-    lines, nodes = slot_ref.shape[1:]
+    width = slot_ref.shape[0]
+    nodes = width * LANES // lines
     groups = species // ROWS
     all_groups = LANES // cap
     rows = all_groups * ROWS
     blocks = nodes // LANES
-    width = lines * blocks
     segments = LANES // width
     times = LANES // segments
     chunk_owners = 2 * all_groups
     chunks = owners // chunk_owners
     here, bundle = lax.axis_index("grid"), lax.axis_index("bundle")
 
-    slot = slot_ref[0]
+    slot = slot_ref[...]
     within = (slot + lax.rem(here, all_groups) * cap) % LANES
-    slot, courant, flux = to_segments([slot - slot % LANES + within, courant_ref[0], flux_ref[0]])[
-        :3
-    ]
+    slot, courant, flux = to_segments(
+        [slot - slot % LANES + within, courant_ref[...], flux_ref[...]], width
+    )[:3]
+    scale = 1.0 / (1.0 + courant)
+    rows_ref[0] = scale
+    rows_ref[1] = courant * scale
+    rows_ref[2] = flux
+    rows_ref[3] = slot
+
+    def row(kind, t, depth=ROWS):
+        return jnp.broadcast_to(rows_ref[kind, t : t + 1], (depth, LANES))
 
     def hot(k):
-        local = (slot - lax.convert_element_type(k * 2 * LANES, F32)).astype(BF16)
         index = lax.broadcasted_iota(jnp.int32, (2 * LANES, LANES), 0).astype(F32).astype(BF16)
         one, zero = jnp.ones_like(index), jnp.zeros_like(index)
-        return jnp.concatenate(
-            [
-                jnp.where(jnp.broadcast_to(local[t : t + 1], index.shape) == index, one, zero)
-                for t in range(times)
-            ],
-            axis=1,
-        )
+        base = lax.convert_element_type(k * 2 * LANES, F32)
+        columns = []
+        for t in range(times):
+            local = (row(3, t, 2 * ROWS) - base).astype(BF16)
+            local = jnp.concatenate([local] * (LANES // ROWS), axis=0)
+            columns.append(jnp.where(local == index, one, zero))
+        return jnp.concatenate(columns, axis=1)
 
     kept = hot(0) if chunks == 1 else None
 
@@ -256,14 +259,11 @@
     entry = jnp.broadcast_to(column, (species, LANES))
     entry = [entry[ROWS * g : ROWS * (g + 1)] for g in range(groups)]
 
-    scale = 1.0 / (1.0 + courant)
-    decay = courant * scale
     first = [None] * groups
     second = [None] * groups
     local, ones, twos = [], [], []
     for t in range(times):
-        scale_t = jnp.broadcast_to(scale[t : t + 1], (ROWS, LANES))
-        decay_t = jnp.broadcast_to(decay[t : t + 1], (ROWS, LANES))
+        scale_t, decay_t = row(0, t), row(1, t)
         one = decay_t if t == 0 else decay_t * ones[-1]
         two = scale_t * one if t == 0 else scale_t * one + decay_t * twos[-1]
         ones.append(one)
@@ -360,8 +360,7 @@
     top = lax.broadcasted_iota(jnp.int32, (ROWS, LANES), 0) == 0
     pieces = []
     for t in range(times):
-        weight = jnp.broadcast_to(flux[t : t + 1], (ROWS, LANES))
-        weight = jnp.where(node + t < length, weight, 0.0)
+        weight = jnp.where(node + t < length, row(2, t), 0.0)
         chunk, place = t % half // depth, t % half % depth
         found = iterates[chunk][
             t // half * species : (t // half + 1) * species, LANES * place : LANES * (place + 1)
@@ -538,10 +537,25 @@
         (cell_state, request_cell, first),
     )
     table = lax.all_to_all(outgoing, "grid", split_axis=0, concat_axis=0, tiled=True)
+    lines, nodes = node_slot.shape[1:]
+    blocks = nodes // LANES
+
+    def by_block(value):
+        return value.reshape(lines, blocks, LANES).swapaxes(0, 1).reshape(blocks * lines, LANES)
+
     sums = call(
-        functools.partial(lines_kernel, cap),
+        functools.partial(lines_kernel, lines, cap),
         (owners * bundles, ROWS, LANES),
-        (table, node_slot, line_length, courant, flux_weight, inflow, interaction),
+        (
+            table,
+            by_block(node_slot),
+            line_length,
+            by_block(courant),
+            by_block(flux_weight),
+            inflow,
+            interaction,
+        ),
+        scratch=(pltpu.VMEM((4, lines * blocks, LANES), F32),),
     )
     back = lax.all_to_all(sums, ("grid", "bundle"), split_axis=0, concat_axis=0, tiled=True)
     return call(

time: 29.8 us -> 30.5 us (1.023)
  local copies, waits for them, and re-layouts: 1.05 us -> 1.68 us
    unnamed x18, local copies, waits for them, and re-layouts: 1.05 us -> 1.68 us
where the time goes in v10:
time: 30.5 us; the launch traced here: 30.2 us
  blocking collectives  23.9 us (78%)
  Pallas kernels  4.51 us (15%)
  local copies, waits for them, and re-layouts  1.68 us (6%)
    all_to_all x1, blocking collectives, shards(): lax.all_to_all(outgoing, 'grid', split_axis=0, concat_axis=0, tiled=True)  13.9 us
    all_to_all x1, blocking collectives, shards(): lax.all_to_all(sums, ('grid', 'bundle'), split_axis=0, concat_axis=0, til...  10 us
    pallas_call x4, Pallas kernels, call(): pl.pallas_call(kernel, out_shape=jax.ShapeDtypeStruct(shape, F32), in_spe...  4.51 us
    unnamed x18, local copies, waits for them, and re-layouts  1.68 us

profile of v10, /device:TPU:0, one launch (start us, length us, event | category | flops | bytes accessed | tf_op | source)
XLA Modules:
  0.0 30.2 jit_solution(11261094375971550012)
XLA Ops:
  0.0 0.0 copy-start.1
  0.0 0.0 copy-start
  0.0 0.7 %copy-done.1 = s32[4,1,8,32]{3,2,1,0:T(8,128)S(1)} copy-done((s32[4,1,8,32]{3,2,1,0:T(8,128)S(1)}, s32[4,1,8,32]{3,2,1,0:T(8,128)}, u32[]{:S(2)}) %copy-start.1) | copy-done | bytes 4120
  0.7 0.3 copy-done
  1.0 0.5 %shard_map.92 = f32[8,8,128]{2,1,0:T(8,128)S(1)} custom-call(f32[24,4096]{1,0:T(8,128)S(1)} %copy-done, s32[4,1,8,32]{3,2,1,0:T(8,128)S(1)} %copy-done.1, f32[8,128]{1,0:T(8,128)S(1)} %shard_map.91.first_ref), custom_call_target="tpu_custom_call" | custom-call | tf_op jit(solution)/shard_map/pallas_call | solution.py:507
  1.5 0.0 copy-start.2
  1.5 0.0 copy-start.3
  1.5 0.0 copy-start.4
  1.5 0.0 copy-start.6
  1.5 13.9 %all_to_all.10.table_ref = f32[8,8,128]{2,1,0:T(8,128)S(1)} all-to-all(f32[8,8,128]{2,1,0:T(8,128)S(1)} %shard_map.92), channel_id=1, replica_groups=mesh['grid'=8,'bundle'=4] {'grid'}, dimensions={0} | all-to-all | bytes 65536 | tf_op jit(solution)/shard_map/all_to_all | solution.py:539
  15.4 0.0 copy-start.7
  15.4 0.0 copy-start.8
  15.4 0.0 copy-done.2
  15.4 0.0 copy-done.3
  15.4 0.0 copy-done.4
  15.4 0.0 copy-done.6
  15.5 0.6 %copy-done.7 = s32[1,2]{1,0:T(1,128)S(1)} copy-done((s32[1,2]{1,0:T(1,128)S(1)}, s32[1,2]{1,0:T(1,128)}, u32[]{:S(2)}) %copy-start.7) | copy-done | bytes 32
  16.1 0.0 copy-done.8
  16.1 2.4 %shard_map.93 = f32[32,8,128]{2,1,0:T(8,128)S(1)} custom-call(f32[8,8,128]{2,1,0:T(8,128)S(1)} %all_to_all.10.table_ref, s32[32,128]{1,0:T(8,128)S(1)} %bitcast.16, s32[1,2]{1,0:T(1,128)S(1)} %copy-done.7, f32[32,128]{1,0:T(8,128)S(1)} %bitcast.17, f32[32,128]{1,0:T(8,128)S(1)} %bitcast.18, f32[1,24]{1,0:T(1,128)S(1)} %copy-done.8, f32[24,24]{1,0:T(8,128)S(1)} %copy-done.6), custom_call_target="tpu_custom_call" | custom-call | tf_op jit(solution)/shard_map/pallas_call | solution.py:507
  18.5 0.0 copy-start.5
  18.6 10.0 %all_to_all.11.sums_ref = f32[32,8,128]{2,1,0:T(8,128)S(1)} all-to-all(f32[32,8,128]{2,1,0:T(8,128)S(1)} %shard_map.93), channel_id=1, replica_groups=mesh['grid'=8,'bundle'=4] {'grid','bundle'}, dimensions={0} | all-to-all | bytes 262144 | tf_op jit(solution)/shard_map/all_to_all | solution.py:560
  28.6 0.0 copy-done.5
  28.6 1.6 %shard_map.94 = f32[24,4096]{1,0:T(8,128)} custom-call(f32[32,8,128]{2,1,0:T(8,128)S(1)} %all_to_all.11.sums_ref, s32[4,1,8,32]{3,2,1,0:T(8,128)S(1)} %copy-done.1, f32[1,4096]{1,0:T(1,128)S(1)} %bitcast.19, f32[24,4096]{1,0:T(8,128)S(1)} %copy-done), custom_call_target="tpu_custom_call" | custom-call | tf_op jit(solution)/shard_map/pallas_call | solution.py:507
  (1 shorter events, 0.0 us)
Async XLA Ops:
  0.0 0.7 %copy-start.1 = (s32[4,1,8,32]{3,2,1,0:T(8,128)S(1)}, s32[4,1,8,32]{3,2,1,0:T(8,128)}, u32[]{:S(2)}) copy-start(s32[4,1,8,32]{3,2,1,0:T(8,128)} %request_ref.3) | copy-start | bytes 12292
  0.0 1.0 %copy-start = (f32[24,4096]{1,0:T(8,128)S(1)}, f32[24,4096]{1,0:T(8,128)}, u32[]{:S(2)}) copy-start(f32[24,4096]{1,0:T(8,128)} %cell_ref.3) | copy-start | bytes 1179652
  1.5 13.9 %copy-start.2 = (s32[1,2,2048]{2,1,0:T(2,128)S(1)}, s32[1,2,2048]{2,1,0:T(2,128)}, u32[]{:S(2)}) copy-start(s32[1,2,2048]{2,1,0:T(2,128)} %param.12) | copy-start | bytes 49156
  1.5 13.9 %copy-start.3 = (f32[1,2,2048]{2,1,0:T(2,128)S(1)}, f32[1,2,2048]{2,1,0:T(2,128)}, u32[]{:S(2)}) copy-start(f32[1,2,2048]{2,1,0:T(2,128)} %param.14) | copy-start | bytes 49156
  1.5 13.9 %copy-start.4 = (f32[1,2,2048]{2,1,0:T(2,128)S(1)}, f32[1,2,2048]{2,1,0:T(2,128)}, u32[]{:S(2)}) copy-start(f32[1,2,2048]{2,1,0:T(2,128)} %param.15) | copy-start | bytes 49156
  1.5 13.9 %copy-start.6 = (f32[24,24]{1,0:T(8,128)S(1)}, f32[24,24]{1,0:T(8,128)}, u32[]{:S(2)}) copy-start(f32[24,24]{1,0:T(8,128)} %interaction_ref.1) | copy-start | bytes 6916
  15.4 0.7 %copy-start.7 = (s32[1,2]{1,0:T(1,128)S(1)}, s32[1,2]{1,0:T(1,128)}, u32[]{:S(2)}) copy-start(s32[1,2]{1,0:T(1,128)} %length_ref.1) | copy-start | bytes 28
  15.4 0.7 %copy-start.8 = (f32[1,24]{1,0:T(1,128)S(1)}, f32[1,24]{1,0:T(1,128)}, u32[]{:S(2)}) copy-start(f32[1,24]{1,0:T(1,128)} %inflow_ref.1) | copy-start | bytes 292
  18.5 10.0 %copy-start.5 = (f32[4096]{0:T(1024)S(1)}, f32[4096]{0:T(1024)}, u32[]{:S(2)}) copy-start(f32[4096]{0:T(1024)} %param.10) | copy-start | bytes 49156

commit v11 on v10

--- a/solution.py
+++ b/solution.py
@@ -15,6 +15,7 @@
 BF16 = jnp.bfloat16
 VMEM_BYTES = 32 * 1024 * 1024
 CHUNKS = 4
+PAIRED = 16
 
 
 def repeat_steps(count, body, carry):
@@ -93,7 +94,8 @@
     out_ref[...] = jnp.zeros_like(out_ref)
 
 
-def pick_kernel(cell_ref, request_ref, first_ref, out_ref):
+def pick_kernel(cell_ref, request_ref, first_ref, length_ref, inflow_ref, *refs):
+    *out_refs, tile_ref = refs
     species, cells = cell_ref.shape
     owners, cap = request_ref.shape[2:]
     bundle = lax.axis_index("bundle")
@@ -144,10 +146,46 @@
                 relative,
             )
             for j in range(groups):
-                out_ref[first + half * groups + j] = tiles[j]
+                tile_ref[first + half * groups + j] = tiles[j]
         return carry
 
     repeat_steps(chunks, chunk, 0)
+    if len(out_refs) == 1:
+        out_refs[0][...] = tile_ref[...]
+    else:
+        keep_ref, send_ref = out_refs
+        for r in range(owners // 2):
+            keep_ref[0, r] = tile_ref[here ^ r]
+            send_ref[0, r] = tile_ref[here ^ (r + owners // 2)]
+
+
+def repack_kernel(old_ref, new_ref, keep_ref, send_ref):
+    sources, count = old_ref.shape[0], old_ref.shape[1] // 2
+    for i, ref in enumerate((old_ref, new_ref)):
+        for s in range(sources):
+            keep_ref[i * sources + s] = ref[s, :count]
+            send_ref[i * sources + s] = ref[s, count:]
+
+
+def exchange_pairs(keep, send, count):
+    bit = count // 2
+    while True:
+        received = lax.ppermute(send, "grid", [(i, i ^ bit) for i in range(count)])
+        if bit == 1:
+            return keep, received
+        sources, tiles = keep.shape[:2]
+        shape = (2 * sources, tiles // 2, ROWS, LANES)
+        keep, send = call(repack_kernel, [shape] * 2, (keep, received))
+        bit //= 2
+
+
+def source_order(count):
+    order = [0]
+    bit = count // 2
+    while bit:
+        order += [s ^ bit for s in order]
+        bit //= 2
+    return order
 
 
 def to_segments(values, width):
@@ -162,17 +200,23 @@
 def lines_kernel(
     lines,
     cap,
-    table_ref,
+    owners,
     slot_ref,
     length_ref,
     courant_ref,
     flux_ref,
     inflow_ref,
     interaction_ref,
-    out_ref,
-    rows_ref,
+    *refs,
 ):
-    owners = table_ref.shape[0]
+    *table_refs, out_ref, rows_ref, table_ref = refs
+    if len(table_refs) == 1:
+        table_ref = table_refs[0]
+    else:
+        order = source_order(owners)
+        for i in range(owners):
+            ref = table_refs[i // (owners // 2)]
+            table_ref[lax.axis_index("grid") ^ order[i]] = ref[i % (owners // 2), 0]
     copies = out_ref.shape[0] // owners
     species = inflow_ref.shape[1]
     width = slot_ref.shape[0]
@@ -503,14 +547,14 @@
         copy.wait()
 
 
-def call(kernel, shape, operands, kinds={}, scratch=(), out=pltpu.VMEM, flops=0):
+def call(kernel, shapes, operands, kinds={}, scratch=(), out=pltpu.VMEM, flops=0):
     return pl.pallas_call(
         kernel,
-        out_shape=jax.ShapeDtypeStruct(shape, F32),
+        out_shape=[jax.ShapeDtypeStruct(shape, F32) for shape in shapes],
         in_specs=[
             pl.BlockSpec(memory_space=kinds.get(i, pltpu.VMEM)) for i in range(len(operands))
         ],
-        out_specs=pl.BlockSpec(memory_space=out),
+        out_specs=[pl.BlockSpec(memory_space=out)] * len(shapes),
         scratch_shapes=list(scratch),
         compiler_params=pltpu.CompilerParams(vmem_limit_bytes=VMEM_BYTES),
         cost_estimate=pl.CostEstimate(flops=flops, bytes_accessed=0, transcendentals=0),
@@ -530,13 +574,20 @@
     interaction,
 ):
     owners, cap = request_cell.shape[2:]
-    first = call(first_kernel, (ROWS, LANES), (), flops=10**9)
+    tile = (ROWS, LANES)
+    paired = owners <= PAIRED and owners & (owners - 1) == 0
+    halves = [(1, owners // 2, *tile)] * 2
+    first = call(first_kernel, [tile], (), flops=10**9)[0]
     outgoing = call(
         pick_kernel,
-        (owners, ROWS, LANES),
-        (cell_state, request_cell, first),
+        halves if paired else [(owners, *tile)],
+        (cell_state, request_cell, first, line_length, inflow),
+        scratch=(pltpu.VMEM((owners, *tile), F32),),
     )
-    table = lax.all_to_all(outgoing, "grid", split_axis=0, concat_axis=0, tiled=True)
+    if paired:
+        tables = exchange_pairs(*outgoing, owners)
+    else:
+        tables = [lax.all_to_all(outgoing[0], "grid", split_axis=0, concat_axis=0, tiled=True)]
     lines, nodes = node_slot.shape[1:]
     blocks = nodes // LANES
 
@@ -544,27 +595,30 @@
         return value.reshape(lines, blocks, LANES).swapaxes(0, 1).reshape(blocks * lines, LANES)
 
     sums = call(
-        functools.partial(lines_kernel, lines, cap),
-        (owners * bundles, ROWS, LANES),
+        functools.partial(lines_kernel, lines, cap, owners),
+        [(owners * bundles, *tile)],
         (
-            table,
             by_block(node_slot),
             line_length,
             by_block(courant),
             by_block(flux_weight),
             inflow,
             interaction,
+            *tables,
         ),
-        scratch=(pltpu.VMEM((4, lines * blocks, LANES), F32),),
-    )
+        scratch=(
+            pltpu.VMEM((4, lines * blocks, LANES), F32),
+            pltpu.VMEM((owners, *tile) if paired else (1, *tile), F32),
+        ),
+    )[0]
     back = lax.all_to_all(sums, ("grid", "bundle"), split_axis=0, concat_axis=0, tiled=True)
     return call(
         functools.partial(blend_kernel, bundles),
-        cell_state.shape,
+        [cell_state.shape],
         (back, request_cell, pore_volume[None, :], cell_state),
         scratch=(pltpu.VMEM(cell_state.shape, F32), pltpu.SemaphoreType.DMA((4,))),
         out=pltpu.HBM,
-    )
+    )[0]
 
 
 def solution(mesh):

time: 30.5 us -> 33.5 us (1.098)
  blocking collectives: 23.9 us -> 14.3 us
  starting transfers between devices: 0 us -> 8.04 us
  waiting for transfers between devices: 0 us -> 5.39 us
  local copies, waits for them, and re-layouts: 1.68 us -> 1.06 us
    all_to_all x1 -> x0, blocking collectives: 13.9 us -> none  [shards(): lax.all_to_all(outgoing, 'grid', split_axis=0, concat_axis=0, tiled=True)]
    ppermute x0 -> x3, starting transfers between devices: none -> 8.04 us  [exchange_pairs(): received = lax.ppermute(send, 'grid', [(i, i ^ bit) for i in range(count)])]
    ppermute x0 -> x3, waiting for transfers between devices: none -> 5.39 us  [exchange_pairs(): received = lax.ppermute(send, 'grid', [(i, i ^ bit) for i in range(count)])]
    all_to_all x1, blocking collectives: 10 us -> 14.3 us  [shards(): lax.all_to_all(sums, ('grid', 'bundle'), split_axis=0, concat_axis=0, til...]
    unnamed x18, local copies, waits for them, and re-layouts: 1.68 us -> 1.06 us
    pallas_call x4 -> x6, Pallas kernels: 4.51 us -> 4.53 us  [call(): pl.pallas_call(kernel, out_shape=[jax.ShapeDtypeStruct(shape, F32) for sh...]
  transfers between devices with their start and end apart: 0 -> 3, of which waited for: 0 -> 3; matrix products, arithmetic and copies ran while one was open for 0% -> 0% of each run, Pallas kernels for 0% -> 0%
where the time goes in v11:
time: 33.5 us; the launch traced here: 33.3 us
  blocking collectives  14.3 us (43%)
  starting transfers between devices  8.04 us (24%)
  waiting for transfers between devices  5.39 us (16%)
  Pallas kernels  4.53 us (14%)
  local copies, waits for them, and re-layouts  1.06 us (3%)
    all_to_all x1, blocking collectives, shards(): lax.all_to_all(sums, ('grid', 'bundle'), split_axis=0, concat_axis=0, til...  14.3 us
    ppermute x3, starting transfers between devices, exchange_pairs(): received = lax.ppermute(send, 'grid', [(i, i ^ bit) for i in range(count)])  8.04 us
    ppermute x3, waiting for transfers between devices, exchange_pairs(): received = lax.ppermute(send, 'grid', [(i, i ^ bit) for i in range(count)])  5.39 us
    pallas_call x6, Pallas kernels, call(): pl.pallas_call(kernel, out_shape=[jax.ShapeDtypeStruct(shape, F32) for sh...  4.53 us
    unnamed x18, local copies, waits for them, and re-layouts  1.06 us
  transfers between devices with their start and end apart: 3, of which 3 were waited for; matrix products, arithmetic and copies ran while one was open for 0% of the time, Pallas kernels for 0%

profile of v11, /device:TPU:0, one launch (start us, length us, event | category | flops | bytes accessed | tf_op | source)
XLA Modules:
  0.0 33.3 jit_solution(15201222258911840835)
XLA Ops:
  0.0 0.0 copy-start.8
  0.0 0.0 copy-start.7
  0.0 0.0 copy-start.1
  0.0 0.0 copy-start
  0.0 0.6 %copy-done.8 = f32[1,24]{1,0:T(1,128)S(1)} copy-done((f32[1,24]{1,0:T(1,128)S(1)}, f32[1,24]{1,0:T(1,128)}, u32[]{:S(2)}) %copy-start.8) | copy-done | bytes 120
  0.7 0.0 copy-done.7
  0.7 0.1 copy-done.1
  0.8 0.3 copy-done
  1.0 0.5 %shard_map.92 = (f32[1,4,8,128]{3,2,1,0:T(8,128)S(1)}, f32[1,4,8,128]{3,2,1,0:T(8,128)S(1)}) custom-call(f32[24,4096]{1,0:T(8,128)S(1)} %copy-done, s32[4,1,8,32]{3,2,1,0:T(8,128)S(1)} %copy-done.1, f32[8,128]{1,0:T(8,128)S(1)} %shard_map.91.first_ref, s32[1,2]{1,0:T(1,128)S(1)} %copy-done.7, f32[1,24]{1,0:T(1,128)S(1)} %copy-done.8), custom_call_target="tpu_custom_call" | custom-call | tf_op jit(solution)/shard_map/pallas_call | solution.py:551
  1.5 4.1 %collective-permute-start = (f32[1,4,8,128]{3,2,1,0:T(8,128)S(1)}, f32[1,4,8,128]{3,2,1,0:T(8,128)S(1)}, u32[]{:S(2)}, u32[]{:S(2)}) collective-permute-start(f32[1,4,8,128]{3,2,1,0:T(8,128)S(1)} %get-tuple-element.12), channel_id=1, source_target_pairs={{0,16},{4,20},{8,24},{12,28},{16,0},{20,4},{24,8},{28,12},{1,17},{... | collective-permute-start | bytes 49160 | tf_op jit(solution)/shard_map/ppermute | solution.py:173
  5.6 1.7 %collective-permute-done.new_ref = f32[1,4,8,128]{3,2,1,0:T(8,128)S(1)} collective-permute-done((f32[1,4,8,128]{3,2,1,0:T(8,128)S(1)}, f32[1,4,8,128]{3,2,1,0:T(8,128)S(1)}, u32[]{:S(2)}, u32[]{:S(2)}) %collective-permute-start) | collective-permute-done | bytes 16416 | tf_op jit(solution)/shard_map/ppermute | solution.py:173
  7.3 0.0 copy-start.4
  7.4 0.0 copy-start.6
  7.4 2.0 %collective-permute-start.1 = (f32[2,2,8,128]{3,2,1,0:T(8,128)S(1)}, f32[2,2,8,128]{3,2,1,0:T(8,128)S(1)}, u32[]{:S(2)}, u32[]{:S(2)}) collective-permute-start(f32[2,2,8,128]{3,2,1,0:T(8,128)S(1)} %get-tuple-element.14), channel_id=1, source_target_pairs={{0,8},{4,12},{8,0},{12,4},{16,24},{20,28},{24,16},{28,20},{1,9},{5... | collective-permute-start | bytes 49160 | tf_op jit(solution)/shard_map/ppermute | solution.py:173
  9.3 1.8 %collective-permute-done.1.new_ref = f32[2,2,8,128]{3,2,1,0:T(8,128)S(1)} collective-permute-done((f32[2,2,8,128]{3,2,1,0:T(8,128)S(1)}, f32[2,2,8,128]{3,2,1,0:T(8,128)S(1)}, u32[]{:S(2)}, u32[]{:S(2)}) %collective-permute-start.1) | collective-permute-done | bytes 16416 | tf_op jit(solution)/shard_map/ppermute | solution.py:173
  11.2 0.0 copy-start.2
  11.2 0.0 copy-start.3
  11.2 2.0 %collective-permute-start.2 = (f32[4,1,8,128]{3,2,1,0:T(8,128)S(1)}, f32[4,1,8,128]{3,2,1,0:T(8,128)S(1)}, u32[]{:S(2)}, u32[]{:S(2)}) collective-permute-start(f32[4,1,8,128]{3,2,1,0:T(8,128)S(1)} %get-tuple-element.16), channel_id=1, source_target_pairs={{0,4},{4,0},{8,12},{12,8},{16,20},{20,16},{24,28},{28,24},{1,5},{5... | collective-permute-start | bytes 49160 | tf_op jit(solution)/shard_map/ppermute | solution.py:173
  13.1 1.8 %collective-permute-done.2.refs_1_ = f32[4,1,8,128]{3,2,1,0:T(8,128)S(1)} collective-permute-done((f32[4,1,8,128]{3,2,1,0:T(8,128)S(1)}, f32[4,1,8,128]{3,2,1,0:T(8,128)S(1)}, u32[]{:S(2)}, u32[]{:S(2)}) %collective-permute-start.2) | collective-permute-done | bytes 16416 | tf_op jit(solution)/shard_map/ppermute | solution.py:173
  15.0 0.0 copy-done.4
  15.0 0.0 copy-done.6
  15.0 0.0 copy-done.2
  15.0 0.0 copy-done.3
  15.0 2.4 %shard_map.95 = f32[32,8,128]{2,1,0:T(8,128)S(1)} custom-call(s32[32,128]{1,0:T(8,128)S(1)} %bitcast.16, s32[1,2]{1,0:T(1,128)S(1)} %copy-done.7, f32[32,128]{1,0:T(8,128)S(1)} %bitcast.17, f32[32,128]{1,0:T(8,128)S(1)} %bitcast.18, f32[1,24]{1,0:T(1,128)S(1)} %copy-done.8, f32[24,24]{1,0:T(8,128)S(1)} %copy-done.6, ...), custom_call_target="tpu_custom_call" | custom-call | tf_op jit(solution)/shard_map/pallas_call | solution.py:551
  17.5 0.0 copy-start.5
  17.5 14.3 %all_to_all.5.sums_ref = f32[32,8,128]{2,1,0:T(8,128)S(1)} all-to-all(f32[32,8,128]{2,1,0:T(8,128)S(1)} %shard_map.95), channel_id=1, replica_groups=mesh['grid'=8,'bundle'=4] {'grid','bundle'}, dimensions={0} | all-to-all | bytes 262144 | tf_op jit(solution)/shard_map/all_to_all | solution.py:614
  31.7 0.0 copy-done.5
  31.7 1.6 %shard_map.96 = f32[24,4096]{1,0:T(8,128)} custom-call(f32[32,8,128]{2,1,0:T(8,128)S(1)} %all_to_all.5.sums_ref, s32[4,1,8,32]{3,2,1,0:T(8,128)S(1)} %copy-done.1, f32[1,4096]{1,0:T(1,128)S(1)} %bitcast.19, f32[24,4096]{1,0:T(8,128)S(1)} %copy-done), custom_call_target="tpu_custom_call" | custom-call | tf_op jit(solution)/shard_map/pallas_call | solution.py:551
  (3 shorter events, 0.0 us)
Async XLA Ops:
  0.0 0.7 %copy-start.8 = (f32[1,24]{1,0:T(1,128)S(1)}, f32[1,24]{1,0:T(1,128)}, u32[]{:S(2)}) copy-start(f32[1,24]{1,0:T(1,128)} %inflow_ref.3) | copy-start | bytes 292
  0.0 0.7 %copy-start.7 = (s32[1,2]{1,0:T(1,128)S(1)}, s32[1,2]{1,0:T(1,128)}, u32[]{:S(2)}) copy-start(s32[1,2]{1,0:T(1,128)} %length_ref.3) | copy-start | bytes 28
  0.0 0.7 %copy-start.1 = (s32[4,1,8,32]{3,2,1,0:T(8,128)S(1)}, s32[4,1,8,32]{3,2,1,0:T(8,128)}, u32[]{:S(2)}) copy-start(s32[4,1,8,32]{3,2,1,0:T(8,128)} %request_ref.3) | copy-start | bytes 12292
  0.0 1.0 %copy-start = (f32[24,4096]{1,0:T(8,128)S(1)}, f32[24,4096]{1,0:T(8,128)}, u32[]{:S(2)}) copy-start(f32[24,4096]{1,0:T(8,128)} %cell_ref.3) | copy-start | bytes 1179652
  1.5 5.8 %collective-permute-start = (f32[1,4,8,128]{3,2,1,0:T(8,128)S(1)}, f32[1,4,8,128]{3,2,1,0:T(8,128)S(1)}, u32[]{:S(2)}, u32[]{:S(2)}) collective-permute-start(f32[1,4,8,128]{3,2,1,0:T(8,128)S(1)} %get-tuple-element.12), channel_id=1, source_target_pairs={{0,16},{4,20},{8,24},{12,28},{16,0},{20,4},{24,8},{28,12},{1,17},{... | collective-permute-start | bytes 49160 | tf_op jit(solution)/shard_map/ppermute | solution.py:173
  7.3 7.6 %copy-start.4 = (f32[1,2,2048]{2,1,0:T(2,128)S(1)}, f32[1,2,2048]{2,1,0:T(2,128)}, u32[]{:S(2)}) copy-start(f32[1,2,2048]{2,1,0:T(2,128)} %param.15) | copy-start | bytes 49156
  7.4 7.6 %copy-start.6 = (f32[24,24]{1,0:T(8,128)S(1)}, f32[24,24]{1,0:T(8,128)}, u32[]{:S(2)}) copy-start(f32[24,24]{1,0:T(8,128)} %interaction_ref.1) | copy-start | bytes 6916
  7.4 3.8 %collective-permute-start.1 = (f32[2,2,8,128]{3,2,1,0:T(8,128)S(1)}, f32[2,2,8,128]{3,2,1,0:T(8,128)S(1)}, u32[]{:S(2)}, u32[]{:S(2)}) collective-permute-start(f32[2,2,8,128]{3,2,1,0:T(8,128)S(1)} %get-tuple-element.14), channel_id=1, source_target_pairs={{0,8},{4,12},{8,0},{12,4},{16,24},{20,28},{24,16},{28,20},{1,9},{5... | collective-permute-start | bytes 49160 | tf_op jit(solution)/shard_map/ppermute | solution.py:173
  11.2 3.8 %copy-start.2 = (s32[1,2,2048]{2,1,0:T(2,128)S(1)}, s32[1,2,2048]{2,1,0:T(2,128)}, u32[]{:S(2)}) copy-start(s32[1,2,2048]{2,1,0:T(2,128)} %param.12) | copy-start | bytes 49156
  11.2 3.8 %copy-start.3 = (f32[1,2,2048]{2,1,0:T(2,128)S(1)}, f32[1,2,2048]{2,1,0:T(2,128)}, u32[]{:S(2)}) copy-start(f32[1,2,2048]{2,1,0:T(2,128)} %param.14) | copy-start | bytes 49156
  11.2 3.8 %collective-permute-start.2 = (f32[4,1,8,128]{3,2,1,0:T(8,128)S(1)}, f32[4,1,8,128]{3,2,1,0:T(8,128)S(1)}, u32[]{:S(2)}, u32[]{:S(2)}) collective-permute-start(f32[4,1,8,128]{3,2,1,0:T(8,128)S(1)} %get-tuple-element.16), channel_id=1, source_target_pairs={{0,4},{4,0},{8,12},{12,8},{16,20},{20,16},{24,28},{28,24},{1,5},{5... | collective-permute-start | bytes 49160 | tf_op jit(solution)/shard_map/ppermute | solution.py:173
  17.5 14.3 %copy-start.5 = (f32[4096]{0:T(1024)S(1)}, f32[4096]{0:T(1024)}, u32[]{:S(2)}) copy-start(f32[4096]{0:T(1024)} %param.10) | copy-start | bytes 49156

commit v12 on v10

--- a/solution.py
+++ b/solution.py
@@ -93,7 +93,7 @@
     out_ref[...] = jnp.zeros_like(out_ref)
 
 
-def pick_kernel(cell_ref, request_ref, first_ref, out_ref):
+def pick_kernel(cell_ref, request_ref, first_ref, length_ref, inflow_ref, out_ref):
     species, cells = cell_ref.shape
     owners, cap = request_ref.shape[2:]
     bundle = lax.axis_index("bundle")
@@ -338,7 +338,7 @@
     iterates = list(bases)
     for step in range(NEWTON):
         for c in range(CHUNKS):
-            high, low = rounded(jnp.tanh(iterates[c]))
+            high, low = rounded(1.0 - 2.0 / (jnp.exp(2.0 * iterates[c]) + 1.0))
             right = jnp.concatenate(
                 [
                     high[:species],
@@ -534,7 +534,7 @@
     outgoing = call(
         pick_kernel,
         (owners, ROWS, LANES),
-        (cell_state, request_cell, first),
+        (cell_state, request_cell, first, line_length, inflow),
     )
     table = lax.all_to_all(outgoing, "grid", split_axis=0, concat_axis=0, tiled=True)
     lines, nodes = node_slot.shape[1:]

time: 30.5 us -> 30 us (0.984)
  local copies, waits for them, and re-layouts: 1.68 us -> 1.07 us
    unnamed x18, local copies, waits for them, and re-layouts: 1.68 us -> 1.07 us
where the time goes in v12:
time: 30 us; the launch traced here: 29.7 us
  blocking collectives  23.9 us (80%)
  Pallas kernels  4.67 us (16%)
  local copies, waits for them, and re-layouts  1.07 us (4%)
    all_to_all x1, blocking collectives, shards(): lax.all_to_all(outgoing, 'grid', split_axis=0, concat_axis=0, tiled=True)  13.9 us
    all_to_all x1, blocking collectives, shards(): lax.all_to_all(sums, ('grid', 'bundle'), split_axis=0, concat_axis=0, til...  10 us
    pallas_call x4, Pallas kernels, call(): pl.pallas_call(kernel, out_shape=jax.ShapeDtypeStruct(shape, F32), in_spe...  4.67 us
    unnamed x18, local copies, waits for them, and re-layouts  1.07 us

profile of v12, /device:TPU:0, one launch (start us, length us, event | category | flops | bytes accessed | tf_op | source)
XLA Modules:
  0.0 29.7 jit_solution(10225204963220960662)
XLA Ops:
  0.0 0.0 copy-start.8
  0.0 0.0 copy-start.7
  0.0 0.0 copy-start.1
  0.0 0.0 copy-start
  0.0 0.6 %copy-done.8 = f32[1,24]{1,0:T(1,128)S(1)} copy-done((f32[1,24]{1,0:T(1,128)S(1)}, f32[1,24]{1,0:T(1,128)}, u32[]{:S(2)}) %copy-start.8) | copy-done | bytes 120
  0.7 0.0 copy-done.7
  0.7 0.1 copy-done.1
  0.8 0.3 copy-done
  1.0 0.5 %shard_map.92 = f32[8,8,128]{2,1,0:T(8,128)S(1)} custom-call(f32[24,4096]{1,0:T(8,128)S(1)} %copy-done, s32[4,1,8,32]{3,2,1,0:T(8,128)S(1)} %copy-done.1, f32[8,128]{1,0:T(8,128)S(1)} %shard_map.91.first_ref, s32[1,2]{1,0:T(1,128)S(1)} %copy-done.7, f32[1,24]{1,0:T(1,128)S(1)} %copy-done.8), custom_call_target="tpu_custom_call" | custom-call | tf_op jit(solution)/shard_map/pallas_call | solution.py:507
  1.5 0.0 copy-start.2
  1.5 0.0 copy-start.3
  1.5 0.0 copy-start.4
  1.5 0.0 copy-start.6
  1.6 13.9 %all_to_all.10.table_ref = f32[8,8,128]{2,1,0:T(8,128)S(1)} all-to-all(f32[8,8,128]{2,1,0:T(8,128)S(1)} %shard_map.92), channel_id=1, replica_groups=mesh['grid'=8,'bundle'=4] {'grid'}, dimensions={0} | all-to-all | bytes 65536 | tf_op jit(solution)/shard_map/all_to_all | solution.py:539
  15.5 0.0 copy-done.2
  15.5 0.0 copy-done.3
  15.5 0.0 copy-done.4
  15.5 0.0 copy-done.6
  15.5 2.6 %shard_map.93 = f32[32,8,128]{2,1,0:T(8,128)S(1)} custom-call(f32[8,8,128]{2,1,0:T(8,128)S(1)} %all_to_all.10.table_ref, s32[32,128]{1,0:T(8,128)S(1)} %bitcast.16, s32[1,2]{1,0:T(1,128)S(1)} %copy-done.7, f32[32,128]{1,0:T(8,128)S(1)} %bitcast.17, f32[32,128]{1,0:T(8,128)S(1)} %bitcast.18, f32[1,24]{1,0:T(1,128)S(1)} %copy-done.8, f32[24,24]{1,0:T(8,128)S(1)} %copy-done.6), custom_call_target="tpu_custom_call" | custom-call | tf_op jit(solution)/shard_map/pallas_call | solution.py:507
  18.1 0.0 copy-start.5
  18.1 10.0 %all_to_all.11.sums_ref = f32[32,8,128]{2,1,0:T(8,128)S(1)} all-to-all(f32[32,8,128]{2,1,0:T(8,128)S(1)} %shard_map.93), channel_id=1, replica_groups=mesh['grid'=8,'bundle'=4] {'grid','bundle'}, dimensions={0} | all-to-all | bytes 262144 | tf_op jit(solution)/shard_map/all_to_all | solution.py:560
  28.1 0.0 copy-done.5
  28.1 1.6 %shard_map.94 = f32[24,4096]{1,0:T(8,128)} custom-call(f32[32,8,128]{2,1,0:T(8,128)S(1)} %all_to_all.11.sums_ref, s32[4,1,8,32]{3,2,1,0:T(8,128)S(1)} %copy-done.1, f32[1,4096]{1,0:T(1,128)S(1)} %bitcast.19, f32[24,4096]{1,0:T(8,128)S(1)} %copy-done), custom_call_target="tpu_custom_call" | custom-call | tf_op jit(solution)/shard_map/pallas_call | solution.py:507
  (1 shorter events, 0.0 us)
Async XLA Ops:
  0.0 0.7 %copy-start.8 = (f32[1,24]{1,0:T(1,128)S(1)}, f32[1,24]{1,0:T(1,128)}, u32[]{:S(2)}) copy-start(f32[1,24]{1,0:T(1,128)} %inflow_ref.3) | copy-start | bytes 292
  0.0 0.7 %copy-start.7 = (s32[1,2]{1,0:T(1,128)S(1)}, s32[1,2]{1,0:T(1,128)}, u32[]{:S(2)}) copy-start(s32[1,2]{1,0:T(1,128)} %length_ref.3) | copy-start | bytes 28
  0.0 0.7 %copy-start.1 = (s32[4,1,8,32]{3,2,1,0:T(8,128)S(1)}, s32[4,1,8,32]{3,2,1,0:T(8,128)}, u32[]{:S(2)}) copy-start(s32[4,1,8,32]{3,2,1,0:T(8,128)} %request_ref.3) | copy-start | bytes 12292
  0.0 1.0 %copy-start = (f32[24,4096]{1,0:T(8,128)S(1)}, f32[24,4096]{1,0:T(8,128)}, u32[]{:S(2)}) copy-start(f32[24,4096]{1,0:T(8,128)} %cell_ref.3) | copy-start | bytes 1179652
  1.5 13.9 %copy-start.2 = (s32[1,2,2048]{2,1,0:T(2,128)S(1)}, s32[1,2,2048]{2,1,0:T(2,128)}, u32[]{:S(2)}) copy-start(s32[1,2,2048]{2,1,0:T(2,128)} %param.12) | copy-start | bytes 49156
  1.5 13.9 %copy-start.3 = (f32[1,2,2048]{2,1,0:T(2,128)S(1)}, f32[1,2,2048]{2,1,0:T(2,128)}, u32[]{:S(2)}) copy-start(f32[1,2,2048]{2,1,0:T(2,128)} %param.14) | copy-start | bytes 49156
  1.5 13.9 %copy-start.4 = (f32[1,2,2048]{2,1,0:T(2,128)S(1)}, f32[1,2,2048]{2,1,0:T(2,128)}, u32[]{:S(2)}) copy-start(f32[1,2,2048]{2,1,0:T(2,128)} %param.15) | copy-start | bytes 49156
  1.5 13.9 %copy-start.6 = (f32[24,24]{1,0:T(8,128)S(1)}, f32[24,24]{1,0:T(8,128)}, u32[]{:S(2)}) copy-start(f32[24,24]{1,0:T(8,128)} %interaction_ref.1) | copy-start | bytes 6916
  18.1 10.0 %copy-start.5 = (f32[4096]{0:T(1024)S(1)}, f32[4096]{0:T(1024)}, u32[]{:S(2)}) copy-start(f32[4096]{0:T(1024)} %param.10) | copy-start | bytes 49156

commit v13 on v12

--- a/solution.py
+++ b/solution.py
@@ -26,6 +26,11 @@
 def rounded(value):
     high = value.astype(BF16).astype(F32)
     return high, value - high
+
+
+def parts(value):
+    high = value.astype(BF16)
+    return high, (value - high.astype(F32)).astype(BF16)
 
 
 def split(value):
@@ -314,12 +319,15 @@
     ]
 
     matrix_high, matrix_low = rounded(interaction_ref[...])
-    block_row = jnp.concatenate([matrix_high, matrix_low, matrix_high], axis=1)
-    blank = jnp.zeros_like(block_row)
+    blank = jnp.zeros_like(matrix_high)
     left = jnp.concatenate(
         [
-            jnp.concatenate([block_row, blank], axis=1),
-            jnp.concatenate([blank, block_row], axis=1),
+            jnp.concatenate(
+                [matrix_high, blank, matrix_low, blank, matrix_high, blank], axis=1
+            ),
+            jnp.concatenate(
+                [blank, matrix_high, blank, matrix_low, blank, matrix_high], axis=1
+            ),
         ],
         axis=0,
     ).astype(BF16)
@@ -338,18 +346,8 @@
     iterates = list(bases)
     for step in range(NEWTON):
         for c in range(CHUNKS):
-            high, low = rounded(1.0 - 2.0 / (jnp.exp(2.0 * iterates[c]) + 1.0))
-            right = jnp.concatenate(
-                [
-                    high[:species],
-                    high[:species],
-                    low[:species],
-                    high[species:],
-                    high[species:],
-                    low[species:],
-                ],
-                axis=0,
-            ).astype(BF16)
+            high, low = parts(jnp.tanh(iterates[c]))
+            right = jnp.concatenate([high, high, low], axis=0)
             iterates[c] = bases[c] - jnp.dot(left, right, preferred_element_type=F32)
 
     length = jnp.zeros((ROWS, LANES), jnp.int32)
@@ -392,7 +390,7 @@
             for j in range(all_groups):
                 owner = k * chunk_owners + half * all_groups + j
                 for copy in range(copies):
-                    out_ref[owner * copies + copy] = tiles[j]
+                    out_ref[copy * owners + owner] = tiles[j]
         return carry
 
     repeat_steps(chunks, scatter, 0)
@@ -434,7 +432,7 @@
             for d in range(ROWS):
                 found = unpack(
                     [
-                        sums_ref[(k * ROWS + d) * bundles + t * all_groups + j]
+                        sums_ref[(t * all_groups + j) * owners + k * ROWS + d]
                         for j in range(all_groups)
                     ],
                     cap,
@@ -444,7 +442,7 @@
                 weights.append(found[groups][:1])
                 values.append(jnp.concatenate(found[:groups], axis=0))
                 indices.append(block[d : d + 1])
-        parts = split(jnp.concatenate(values, axis=1))
+        both = split(jnp.concatenate(values, axis=1))
         weight_high, weight_low = rounded(jnp.concatenate(weights, axis=1))
         index = jnp.concatenate(indices, axis=1)
         entries = index.shape[1]
@@ -455,12 +453,6 @@
         hot = jnp.where(place == low, jnp.ones_like(place), jnp.zeros_like(place))
         zero = jnp.zeros((2 * ROWS, entries), BF16)
         pieces = []
-        for h in range(highs):
-            mask = high == jnp.array(h, BF16)
-            for r in range(2 * species // (2 * ROWS)):
-                pieces.append(
-                    jnp.where(mask, parts[2 * ROWS * r : 2 * ROWS * (r + 1)], zero)
-                )
         for first in range(0, highs, 2 * ROWS):
             mask = high == (
                 lax.broadcasted_iota(jnp.int32, (2 * ROWS, entries), 0) + first
@@ -468,10 +460,21 @@
             for part in (weight_high, weight_low):
                 row = jnp.broadcast_to(part, (2 * ROWS, entries)).astype(BF16)
                 pieces.append(jnp.where(mask, row, zero))
-        left = jnp.concatenate(pieces, axis=0)
-        product = lax.dot_general(
-            left, hot, (((1,), (1,)), ((), ())), preferred_element_type=F32
-        )
+        for h in range(highs):
+            mask = high == jnp.array(h, BF16)
+            for r in range(2 * species // (2 * ROWS)):
+                pieces.append(jnp.where(mask, both[2 * ROWS * r : 2 * ROWS * (r + 1)], zero))
+        half = (len(pieces) + len(pieces) // 2 % 2) // 2
+        products = [
+            lax.dot_general(
+                jnp.concatenate(some, axis=0),
+                hot,
+                (((1,), (1,)), ((), ())),
+                preferred_element_type=F32,
+            )
+            for some in (pieces[:half], pieces[half:])
+        ]
+        product = jnp.concatenate(products, axis=0)
         return product if chunks == 1 else total + product
 
     flux_rows = -(-highs // (2 * ROWS)) * 4 * ROWS
@@ -480,7 +483,7 @@
         chunk,
         jnp.zeros((highs * 2 * species + flux_rows, width), F32) if chunks > 1 else 0,
     )
-    flux = total[highs * 2 * species :]
+    flux, total = total[:flux_rows], total[flux_rows:]
     copies = []
     stride = max(highs // 4, 1)
     for h in range(highs):
@@ -557,7 +560,7 @@
         ),
         scratch=(pltpu.VMEM((4, lines * blocks, LANES), F32),),
     )
-    back = lax.all_to_all(sums, ("grid", "bundle"), split_axis=0, concat_axis=0, tiled=True)
+    back = lax.all_to_all(sums, ("bundle", "grid"), split_axis=0, concat_axis=0, tiled=True)
     return call(
         functools.partial(blend_kernel, bundles),
         cell_state.shape,

time: 30 us -> 29.2 us (0.973)
  blocking collectives: 23.9 us -> 23.4 us
    all_to_all x1, blocking collectives: 10 us -> 9.53 us  [shards(): lax.all_to_all(sums, ('bundle', 'grid'), split_axis=0, concat_axis=0, til...]
where the time goes in v13:
time: 29.2 us; the launch traced here: 29 us
  blocking collectives  23.4 us (80%)
  Pallas kernels  4.42 us (15%)
  local copies, waits for them, and re-layouts  1.07 us (4%)
    all_to_all x1, blocking collectives, shards(): lax.all_to_all(outgoing, 'grid', split_axis=0, concat_axis=0, tiled=True)  13.9 us
    all_to_all x1, blocking collectives, shards(): lax.all_to_all(sums, ('bundle', 'grid'), split_axis=0, concat_axis=0, til...  9.53 us
    pallas_call x4, Pallas kernels, call(): pl.pallas_call(kernel, out_shape=jax.ShapeDtypeStruct(shape, F32), in_spe...  4.42 us
    unnamed x18, local copies, waits for them, and re-layouts  1.07 us

profile of v13, /device:TPU:0, one launch (start us, length us, event | category | flops | bytes accessed | tf_op | source)
XLA Modules:
  0.0 29.0 jit_solution(11850673490867172787)
XLA Ops:
  0.0 0.0 copy-start.8
  0.0 0.0 copy-start.7
  0.0 0.0 copy-start.1
  0.0 0.0 copy-start
  0.0 0.6 %copy-done.8 = f32[1,24]{1,0:T(1,128)S(1)} copy-done((f32[1,24]{1,0:T(1,128)S(1)}, f32[1,24]{1,0:T(1,128)}, u32[]{:S(2)}) %copy-start.8) | copy-done | bytes 120
  0.7 0.0 copy-done.7
  0.7 0.1 copy-done.1
  0.8 0.3 %copy-done = f32[24,4096]{1,0:T(8,128)S(1)} copy-done((f32[24,4096]{1,0:T(8,128)S(1)}, f32[24,4096]{1,0:T(8,128)}, u32[]{:S(2)}) %copy-start) | copy-done | bytes 393240
  1.0 0.5 %shard_map.92 = f32[8,8,128]{2,1,0:T(8,128)S(1)} custom-call(f32[24,4096]{1,0:T(8,128)S(1)} %copy-done, s32[4,1,8,32]{3,2,1,0:T(8,128)S(1)} %copy-done.1, f32[8,128]{1,0:T(8,128)S(1)} %shard_map.91.first_ref, s32[1,2]{1,0:T(1,128)S(1)} %copy-done.7, f32[1,24]{1,0:T(1,128)S(1)} %copy-done.8), custom_call_target="tpu_custom_call" | custom-call | tf_op jit(solution)/shard_map/pallas_call | solution.py:510
  1.5 0.0 copy-start.2
  1.5 0.0 copy-start.3
  1.5 0.0 copy-start.4
  1.5 0.0 copy-start.6
  1.6 13.9 %all_to_all.10.table_ref = f32[8,8,128]{2,1,0:T(8,128)S(1)} all-to-all(f32[8,8,128]{2,1,0:T(8,128)S(1)} %shard_map.92), channel_id=1, replica_groups=mesh['grid'=8,'bundle'=4] {'grid'}, dimensions={0} | all-to-all | bytes 65536 | tf_op jit(solution)/shard_map/all_to_all | solution.py:542
  15.5 0.0 copy-done.2
  15.5 0.0 copy-done.3
  15.5 0.0 copy-done.4
  15.5 0.0 copy-done.6
  15.5 2.4 %shard_map.93 = f32[32,8,128]{2,1,0:T(8,128)S(1)} custom-call(f32[8,8,128]{2,1,0:T(8,128)S(1)} %all_to_all.10.table_ref, s32[32,128]{1,0:T(8,128)S(1)} %bitcast.16, s32[1,2]{1,0:T(1,128)S(1)} %copy-done.7, f32[32,128]{1,0:T(8,128)S(1)} %bitcast.17, f32[32,128]{1,0:T(8,128)S(1)} %bitcast.18, f32[1,24]{1,0:T(1,128)S(1)} %copy-done.8, f32[24,24]{1,0:T(8,128)S(1)} %copy-done.6), custom_call_target="tpu_custom_call" | custom-call | tf_op jit(solution)/shard_map/pallas_call | solution.py:510
  17.9 0.0 copy-start.5
  17.9 9.5 %all_to_all.11.sums_ref = f32[32,8,128]{2,1,0:T(8,128)S(1)} all-to-all(f32[32,8,128]{2,1,0:T(8,128)S(1)} %shard_map.93), channel_id=1, replica_groups=mesh['grid'=8,'bundle'=4] {'bundle','grid'}, dimensions={0} | all-to-all | bytes 262144 | tf_op jit(solution)/shard_map/all_to_all | solution.py:563
  27.4 0.0 copy-done.5
  27.4 1.5 %shard_map.94 = f32[24,4096]{1,0:T(8,128)} custom-call(f32[32,8,128]{2,1,0:T(8,128)S(1)} %all_to_all.11.sums_ref, s32[4,1,8,32]{3,2,1,0:T(8,128)S(1)} %copy-done.1, f32[1,4096]{1,0:T(1,128)S(1)} %bitcast.19, f32[24,4096]{1,0:T(8,128)S(1)} %copy-done), custom_call_target="tpu_custom_call" | custom-call | tf_op jit(solution)/shard_map/pallas_call | solution.py:510
  (1 shorter events, 0.0 us)
Async XLA Ops:
  0.0 0.7 %copy-start.8 = (f32[1,24]{1,0:T(1,128)S(1)}, f32[1,24]{1,0:T(1,128)}, u32[]{:S(2)}) copy-start(f32[1,24]{1,0:T(1,128)} %inflow_ref.3) | copy-start | bytes 292
  0.0 0.7 %copy-start.7 = (s32[1,2]{1,0:T(1,128)S(1)}, s32[1,2]{1,0:T(1,128)}, u32[]{:S(2)}) copy-start(s32[1,2]{1,0:T(1,128)} %length_ref.3) | copy-start | bytes 28
  0.0 0.7 %copy-start.1 = (s32[4,1,8,32]{3,2,1,0:T(8,128)S(1)}, s32[4,1,8,32]{3,2,1,0:T(8,128)}, u32[]{:S(2)}) copy-start(s32[4,1,8,32]{3,2,1,0:T(8,128)} %request_ref.3) | copy-start | bytes 12292
  0.0 1.0 %copy-start = (f32[24,4096]{1,0:T(8,128)S(1)}, f32[24,4096]{1,0:T(8,128)}, u32[]{:S(2)}) copy-start(f32[24,4096]{1,0:T(8,128)} %cell_ref.3) | copy-start | bytes 1179652
  1.5 13.9 %copy-start.2 = (s32[1,2,2048]{2,1,0:T(2,128)S(1)}, s32[1,2,2048]{2,1,0:T(2,128)}, u32[]{:S(2)}) copy-start(s32[1,2,2048]{2,1,0:T(2,128)} %param.12) | copy-start | bytes 49156
  1.5 13.9 %copy-start.3 = (f32[1,2,2048]{2,1,0:T(2,128)S(1)}, f32[1,2,2048]{2,1,0:T(2,128)}, u32[]{:S(2)}) copy-start(f32[1,2,2048]{2,1,0:T(2,128)} %param.14) | copy-start | bytes 49156
  1.5 13.9 %copy-start.4 = (f32[1,2,2048]{2,1,0:T(2,128)S(1)}, f32[1,2,2048]{2,1,0:T(2,128)}, u32[]{:S(2)}) copy-start(f32[1,2,2048]{2,1,0:T(2,128)} %param.15) | copy-start | bytes 49156
  1.5 13.9 %copy-start.6 = (f32[24,24]{1,0:T(8,128)S(1)}, f32[24,24]{1,0:T(8,128)}, u32[]{:S(2)}) copy-start(f32[24,24]{1,0:T(8,128)} %interaction_ref.1) | copy-start | bytes 6916
  17.9 9.5 %copy-start.5 = (f32[4096]{0:T(1024)S(1)}, f32[4096]{0:T(1024)}, u32[]{:S(2)}) copy-start(f32[4096]{0:T(1024)} %param.10) | copy-start | bytes 49156

commit v14 on v13

--- a/solution.py
+++ b/solution.py
@@ -98,31 +98,32 @@
     out_ref[...] = jnp.zeros_like(out_ref)
 
 
-def pick_kernel(cell_ref, request_ref, first_ref, length_ref, inflow_ref, out_ref):
+def pick_index(request_ref, k):
+    bundle = lax.axis_index("bundle")
+    groups = LANES // request_ref.shape[3]
+    cap = request_ref.shape[3]
+    block = request_ref[bundle, 0, pl.ds(k * 2 * groups, 2 * groups), :]
+    index = jnp.concatenate(
+        [spread_rows(block[:groups], cap), spread_rows(block[groups:], cap)], axis=1
+    )
+    high = jnp.broadcast_to(index // LANES, (ROWS, 2 * LANES))
+    hot = (
+        (lax.broadcasted_iota(jnp.int32, (LANES, 2 * LANES), 0) == index % LANES)
+        .astype(F32)
+        .astype(BF16)
+    )
+    return high, jnp.concatenate([hot, hot], axis=0)
+
+
+def pick_kernel(cell_ref, request_ref, first_ref, *refs):
+    *kept_refs, out_ref = refs
     species, cells = cell_ref.shape
     owners, cap = request_ref.shape[2:]
-    bundle = lax.axis_index("bundle")
     groups = LANES // cap
     chunks = owners // (2 * groups)
     highs = cells // LANES
     here = lax.axis_index("grid")
     relative = lane_groups(cap, here)
-
-    def wanted(k):
-        block = request_ref[bundle, 0, pl.ds(k * 2 * groups, 2 * groups), :]
-        index = jnp.concatenate(
-            [spread_rows(block[:groups], cap), spread_rows(block[groups:], cap)], axis=1
-        )
-        low = index % LANES
-        high = index // LANES
-        hot = (
-            (lax.broadcasted_iota(jnp.int32, (LANES, 2 * LANES), 0) == low)
-            .astype(F32)
-            .astype(BF16)
-        )
-        return high, jnp.concatenate([hot, hot], axis=0)
-
-    kept = wanted(0) if chunks == 1 else None
     cell = cell_ref[...]
     stacked = jnp.concatenate(
         [cell[:, LANES * h : LANES * (h + 1)] for h in range(highs)], axis=0
@@ -131,9 +132,13 @@
 
     def chunk(k, carry):
         first = k * 2 * groups
-        high, right = wanted(k) if kept is None else kept
+        if kept_refs:
+            high, right = kept_refs[0][...], kept_refs[1][...]
+        else:
+            high, right = pick_index(request_ref, k)
         product = jnp.dot(left, right, preferred_element_type=F32)
         picked = jnp.zeros((species, 2 * LANES), F32)
+        high = jnp.concatenate([high] * (species // ROWS), axis=0)
         for h in range(highs):
             picked = picked + jnp.where(high == h, product[species * h : species * (h + 1)], 0.0)
         blank = jnp.zeros((groups * ROWS - species, 2 * LANES), F32)
@@ -396,7 +401,51 @@
     repeat_steps(chunks, scatter, 0)
 
 
-def blend_kernel(bundles, sums_ref, request_ref, pore_ref, cell_ref, out_hbm, out_ref, out_sem):
+def blend_index(request_ref, k):
+    bundles, cap = request_ref.shape[0], request_ref.shape[3]
+    all_groups = LANES // cap
+    width = 2 * LANES
+    here = lax.axis_index("grid")
+    sublane = lax.broadcasted_iota(jnp.int32, (ROWS, LANES), 0)
+    indices = []
+    for t in range(bundles // all_groups):
+        straight = jnp.concatenate(
+            [
+                request_ref[
+                    t * all_groups
+                    + lax.rem(x + all_groups - lax.rem(here, all_groups), all_groups),
+                    0,
+                    pl.ds(k * ROWS, ROWS),
+                    :,
+                ]
+                for x in range(all_groups)
+            ],
+            axis=1,
+        )
+        block = straight
+        for turn in range(1, all_groups):
+            block = jnp.where(
+                sublane % all_groups == turn, pltpu.roll(straight, turn * cap, 1), block
+            )
+        indices += [block[d : d + 1] for d in range(ROWS)]
+    index = jnp.concatenate(indices, axis=1)
+    entries = index.shape[1]
+    high = jnp.broadcast_to(index // width, (2 * ROWS, entries)).astype(F32).astype(BF16)
+    low = jnp.broadcast_to(index % width, (2 * ROWS, entries)).astype(F32).astype(BF16)
+    low = jnp.concatenate([low] * (width // (2 * ROWS)), axis=0)
+    place = lax.broadcasted_iota(jnp.int32, (width, entries), 0).astype(F32).astype(BF16)
+    return high, jnp.where(place == low, jnp.ones_like(place), jnp.zeros_like(place))
+
+
+def index_kernel(
+    request_ref, first_ref, length_ref, inflow_ref, pick_high, pick_hot, blend_high, blend_hot
+):
+    pick_high[...], pick_hot[...] = pick_index(request_ref, 0)
+    blend_high[...], blend_hot[...] = blend_index(request_ref, 0)
+
+
+def blend_kernel(bundles, sums_ref, request_ref, pore_ref, cell_ref, *refs):
+    *kept_refs, out_hbm, out_ref, out_sem = refs
     owners = sums_ref.shape[0] // bundles
     species, cells = cell_ref.shape
     cap = request_ref.shape[3]
@@ -406,29 +455,10 @@
     highs = cells // width
     chunks = owners // ROWS
     here = lax.axis_index("grid")
-    sublane = lax.broadcasted_iota(jnp.int32, (ROWS, LANES), 0)
 
     def chunk(k, total):
-        values, weights, indices = [], [], []
+        values, weights = [], []
         for t in range(bundles // all_groups):
-            block = jnp.concatenate(
-                [
-                    request_ref[
-                        t * all_groups
-                        + lax.rem(x + all_groups - lax.rem(here, all_groups), all_groups),
-                        0,
-                        pl.ds(k * ROWS, ROWS),
-                        :,
-                    ]
-                    for x in range(all_groups)
-                ],
-                axis=1,
-            )
-            straight = block
-            for turn in range(1, all_groups):
-                block = jnp.where(
-                    sublane % all_groups == turn, pltpu.roll(straight, turn * cap, 1), block
-                )
             for d in range(ROWS):
                 found = unpack(
                     [
@@ -441,16 +471,13 @@
                 )
                 weights.append(found[groups][:1])
                 values.append(jnp.concatenate(found[:groups], axis=0))
-                indices.append(block[d : d + 1])
         both = split(jnp.concatenate(values, axis=1))
         weight_high, weight_low = rounded(jnp.concatenate(weights, axis=1))
-        index = jnp.concatenate(indices, axis=1)
-        entries = index.shape[1]
-        high = jnp.broadcast_to(index // width, (2 * ROWS, entries)).astype(F32).astype(BF16)
-        low = jnp.broadcast_to(index % width, (2 * ROWS, entries)).astype(F32).astype(BF16)
-        low = jnp.concatenate([low] * (width // (2 * ROWS)), axis=0)
-        place = lax.broadcasted_iota(jnp.int32, (width, entries), 0).astype(F32).astype(BF16)
-        hot = jnp.where(place == low, jnp.ones_like(place), jnp.zeros_like(place))
+        if kept_refs:
+            high, hot = kept_refs[0][...], kept_refs[1][...]
+        else:
+            high, hot = blend_index(request_ref, k)
+        entries = hot.shape[1]
         zero = jnp.zeros((2 * ROWS, entries), BF16)
         pieces = []
         for first in range(0, highs, 2 * ROWS):
@@ -506,14 +533,14 @@
         copy.wait()
 
 
-def call(kernel, shape, operands, kinds={}, scratch=(), out=pltpu.VMEM, flops=0):
+def call(kernel, shapes, operands, kinds={}, scratch=(), out=pltpu.VMEM, flops=0):
     return pl.pallas_call(
         kernel,
-        out_shape=jax.ShapeDtypeStruct(shape, F32),
+        out_shape=[jax.ShapeDtypeStruct(shape, kind) for shape, kind in shapes],
         in_specs=[
             pl.BlockSpec(memory_space=kinds.get(i, pltpu.VMEM)) for i in range(len(operands))
         ],
-        out_specs=pl.BlockSpec(memory_space=out),
+        out_specs=[pl.BlockSpec(memory_space=out)] * len(shapes),
         scratch_shapes=list(scratch),
         compiler_params=pltpu.CompilerParams(vmem_limit_bytes=VMEM_BYTES),
         cost_estimate=pl.CostEstimate(flops=flops, bytes_accessed=0, transcendentals=0),
@@ -533,12 +560,25 @@
     interaction,
 ):
     owners, cap = request_cell.shape[2:]
-    first = call(first_kernel, (ROWS, LANES), (), flops=10**9)
+    first = call(first_kernel, [((ROWS, LANES), F32)], (), flops=10**9)[0]
+    indices = []
+    if owners == ROWS and owners * cap == 2 * LANES:
+        entries = owners * bundles * cap
+        indices = call(
+            index_kernel,
+            [
+                ((ROWS, 2 * LANES), jnp.int32),
+                ((2 * LANES, 2 * LANES), BF16),
+                ((2 * ROWS, entries), BF16),
+                ((2 * LANES, entries), BF16),
+            ],
+            (request_cell, first, line_length, inflow),
+        )
     outgoing = call(
         pick_kernel,
-        (owners, ROWS, LANES),
-        (cell_state, request_cell, first, line_length, inflow),
-    )
+        [((owners, ROWS, LANES), F32)],
+        (cell_state, request_cell, first, *indices[:2]),
+    )[0]
     table = lax.all_to_all(outgoing, "grid", split_axis=0, concat_axis=0, tiled=True)
     lines, nodes = node_slot.shape[1:]
     blocks = nodes // LANES
@@ -548,7 +588,7 @@
 
     sums = call(
         functools.partial(lines_kernel, lines, cap),
-        (owners * bundles, ROWS, LANES),
+        [((owners * bundles, ROWS, LANES), F32)],
         (
             table,
             by_block(node_slot),
@@ -559,15 +599,15 @@
             interaction,
         ),
         scratch=(pltpu.VMEM((4, lines * blocks, LANES), F32),),
-    )
+    )[0]
     back = lax.all_to_all(sums, ("bundle", "grid"), split_axis=0, concat_axis=0, tiled=True)
     return call(
         functools.partial(blend_kernel, bundles),
-        cell_state.shape,
-        (back, request_cell, pore_volume[None, :], cell_state),
+        [(cell_state.shape, F32)],
+        (back, request_cell, pore_volume[None, :], cell_state, *indices[2:]),
         scratch=(pltpu.VMEM(cell_state.shape, F32), pltpu.SemaphoreType.DMA((4,))),
         out=pltpu.HBM,
-    )
+    )[0]
 
 
 def solution(mesh):

time: 29.2 us -> 29 us (level)
    pallas_call x4 -> x5, Pallas kernels: 4.42 us -> 4.42 us  [call(): pl.pallas_call(kernel, out_shape=[jax.ShapeDtypeStruct(shape, kind) for s...]
where the time goes in v14:
time: 29 us; the launch traced here: 28.7 us
  blocking collectives  23.4 us (81%)
  Pallas kernels  4.42 us (15%)
  local copies, waits for them, and re-layouts  0.81 us (3%)
    all_to_all x1, blocking collectives, shards(): lax.all_to_all(outgoing, 'grid', split_axis=0, concat_axis=0, tiled=True)  13.9 us
    all_to_all x1, blocking collectives, shards(): lax.all_to_all(sums, ('bundle', 'grid'), split_axis=0, concat_axis=0, til...  9.54 us
    pallas_call x5, Pallas kernels, call(): pl.pallas_call(kernel, out_shape=[jax.ShapeDtypeStruct(shape, kind) for s...  4.42 us
    unnamed x18, local copies, waits for them, and re-layouts  0.81 us

profile of v14, /device:TPU:0, one launch (start us, length us, event | category | flops | bytes accessed | tf_op | source)
XLA Modules:
  0.0 28.7 jit_solution(18003957276363124767)
XLA Ops:
  0.0 0.0 copy-start.1
  0.0 0.0 copy-start.8
  0.0 0.0 copy-start.7
  0.0 0.0 copy-start
  0.0 0.7 %copy-done.1 = s32[4,1,8,32]{3,2,1,0:T(8,128)S(1)} copy-done((s32[4,1,8,32]{3,2,1,0:T(8,128)S(1)}, s32[4,1,8,32]{3,2,1,0:T(8,128)}, u32[]{:S(2)}) %copy-start.1) | copy-done | bytes 4120
  0.7 0.0 copy-done.8
  0.7 0.0 copy-done.7
  0.7 0.2 shard_map.92
  1.0 0.1 copy-done
  1.0 0.4 %shard_map.93 = f32[8,8,128]{2,1,0:T(8,128)S(1)} custom-call(f32[24,4096]{1,0:T(8,128)S(1)} %copy-done, s32[4,1,8,32]{3,2,1,0:T(8,128)S(1)} %copy-done.1, f32[8,128]{1,0:T(8,128)S(1)} %shard_map.91.first_ref, s32[8,256]{1,0:T(8,128)S(1)} %get-tuple-element.9.refs_0_, bf16[256,256]{1,0:T(8,128)(2,1)S(1)} %get-tuple-element.10.refs_1_), custom_call_target="tpu_custom_call" | custom-call | tf_op jit(solution)/shard_map/pallas_call | solution.py:537
  1.4 0.0 copy-start.3
  1.4 0.0 copy-start.4
  1.4 0.0 copy-start.5
  1.4 0.0 copy-start.6
  1.4 13.9 %all_to_all.10.table_ref = f32[8,8,128]{2,1,0:T(8,128)S(1)} all-to-all(f32[8,8,128]{2,1,0:T(8,128)S(1)} %shard_map.93), channel_id=1, replica_groups=mesh['grid'=8,'bundle'=4] {'grid'}, dimensions={0} | all-to-all | bytes 65536 | tf_op jit(solution)/shard_map/all_to_all | solution.py:582
  15.3 0.0 copy-done.3
  15.3 0.0 copy-done.4
  15.3 0.0 copy-done.5
  15.3 0.0 copy-done.6
  15.4 2.4 %shard_map.94 = f32[32,8,128]{2,1,0:T(8,128)S(1)} custom-call(f32[8,8,128]{2,1,0:T(8,128)S(1)} %all_to_all.10.table_ref, s32[32,128]{1,0:T(8,128)S(1)} %bitcast.17, s32[1,2]{1,0:T(1,128)S(1)} %copy-done.7, f32[32,128]{1,0:T(8,128)S(1)} %bitcast.18, f32[32,128]{1,0:T(8,128)S(1)} %bitcast.19, f32[1,24]{1,0:T(1,128)S(1)} %copy-done.8, f32[24,24]{1,0:T(8,128)S(1)} %copy-done.6), custom_call_target="tpu_custom_call" | custom-call | tf_op jit(solution)/shard_map/pallas_call | solution.py:537
  17.8 0.0 copy-start.2
  17.8 9.5 %all_to_all.11.sums_ref = f32[32,8,128]{2,1,0:T(8,128)S(1)} all-to-all(f32[32,8,128]{2,1,0:T(8,128)S(1)} %shard_map.94), channel_id=1, replica_groups=mesh['grid'=8,'bundle'=4] {'bundle','grid'}, dimensions={0} | all-to-all | bytes 262144 | tf_op jit(solution)/shard_map/all_to_all | solution.py:603
  27.3 0.0 copy-done.2
  27.3 1.4 %shard_map.95 = f32[24,4096]{1,0:T(8,128)} custom-call(f32[32,8,128]{2,1,0:T(8,128)S(1)} %all_to_all.11.sums_ref, s32[4,1,8,32]{3,2,1,0:T(8,128)S(1)} %copy-done.1, f32[1,4096]{1,0:T(1,128)S(1)} %bitcast.16, f32[24,4096]{1,0:T(8,128)S(1)} %copy-done, bf16[16,1024]{1,0:T(8,128)(2,1)S(1)} %get-tuple-element.11.refs_0_, ...), custom_call_target="tpu_custom_call" | custom-call | tf_op jit(solution)/shard_map/pallas_call | solution.py:537
  (1 shorter events, 0.0 us)
Async XLA Ops:
  0.0 0.7 %copy-start.1 = (s32[4,1,8,32]{3,2,1,0:T(8,128)S(1)}, s32[4,1,8,32]{3,2,1,0:T(8,128)}, u32[]{:S(2)}) copy-start(s32[4,1,8,32]{3,2,1,0:T(8,128)} %request_ref.5) | copy-start | bytes 12292
  0.0 0.7 %copy-start.8 = (f32[1,24]{1,0:T(1,128)S(1)}, f32[1,24]{1,0:T(1,128)}, u32[]{:S(2)}) copy-start(f32[1,24]{1,0:T(1,128)} %inflow_ref.3) | copy-start | bytes 292
  0.0 0.7 %copy-start.7 = (s32[1,2]{1,0:T(1,128)S(1)}, s32[1,2]{1,0:T(1,128)}, u32[]{:S(2)}) copy-start(s32[1,2]{1,0:T(1,128)} %length_ref.3) | copy-start | bytes 28
  0.0 1.0 %copy-start = (f32[24,4096]{1,0:T(8,128)S(1)}, f32[24,4096]{1,0:T(8,128)}, u32[]{:S(2)}) copy-start(f32[24,4096]{1,0:T(8,128)} %cell_ref.3) | copy-start | bytes 1179652
  1.4 13.9 %copy-start.3 = (s32[1,2,2048]{2,1,0:T(2,128)S(1)}, s32[1,2,2048]{2,1,0:T(2,128)}, u32[]{:S(2)}) copy-start(s32[1,2,2048]{2,1,0:T(2,128)} %param.12) | copy-start | bytes 49156
  1.4 13.9 %copy-start.4 = (f32[1,2,2048]{2,1,0:T(2,128)S(1)}, f32[1,2,2048]{2,1,0:T(2,128)}, u32[]{:S(2)}) copy-start(f32[1,2,2048]{2,1,0:T(2,128)} %param.14) | copy-start | bytes 49156
  1.4 13.9 %copy-start.5 = (f32[1,2,2048]{2,1,0:T(2,128)S(1)}, f32[1,2,2048]{2,1,0:T(2,128)}, u32[]{:S(2)}) copy-start(f32[1,2,2048]{2,1,0:T(2,128)} %param.15) | copy-start | bytes 49156
  1.4 13.9 %copy-start.6 = (f32[24,24]{1,0:T(8,128)S(1)}, f32[24,24]{1,0:T(8,128)}, u32[]{:S(2)}) copy-start(f32[24,24]{1,0:T(8,128)} %interaction_ref.1) | copy-start | bytes 6916
  17.8 9.6 %copy-start.2 = (f32[4096]{0:T(1024)S(1)}, f32[4096]{0:T(1024)}, u32[]{:S(2)}) copy-start(f32[4096]{0:T(1024)} %param.10) | copy-start | bytes 49156

commit v15 on v14

--- a/solution.py
+++ b/solution.py
@@ -15,6 +15,15 @@
 BF16 = jnp.bfloat16
 VMEM_BYTES = 32 * 1024 * 1024
 CHUNKS = 4
+
+
+def near_size(bundles):
+    return 2 if bundles % 2 == 0 else 1
+
+
+def turned_place(bundle, bundles):
+    near = near_size(bundles)
+    return bundle % near * (bundles // near) + bundle // near
 
 
 def repeat_steps(count, body, carry):
@@ -99,7 +108,7 @@
 
 
 def pick_index(request_ref, k):
-    bundle = lax.axis_index("bundle")
+    bundle = bundle_place()
     groups = LANES // request_ref.shape[3]
     cap = request_ref.shape[3]
     block = request_ref[bundle, 0, pl.ds(k * 2 * groups, 2 * groups), :]
@@ -195,7 +204,7 @@
     times = LANES // segments
     chunk_owners = 2 * all_groups
     chunks = owners // chunk_owners
-    here, bundle = lax.axis_index("grid"), lax.axis_index("bundle")
+    here, bundle = lax.axis_index("grid"), bundle_place()
 
     slot = slot_ref[...]
     within = (slot + lax.rem(here, all_groups) * cap) % LANES
@@ -395,7 +404,7 @@
             for j in range(all_groups):
                 owner = k * chunk_owners + half * all_groups + j
                 for copy in range(copies):
-                    out_ref[copy * owners + owner] = tiles[j]
+                    out_ref[turned_place(copy, copies) * owners + owner] = tiles[j]
         return carry
 
     repeat_steps(chunks, scatter, 0)
@@ -462,7 +471,7 @@
             for d in range(ROWS):
                 found = unpack(
                     [
-                        sums_ref[(t * all_groups + j) * owners + k * ROWS + d]
+                        sums_ref[turned_place(t * all_groups + j, bundles) * owners + k * ROWS + d]
                         for j in range(all_groups)
                     ],
                     cap,
@@ -547,6 +556,10 @@
     )(*operands)
 
 
+def bundle_place():
+    return lax.axis_index("far") * lax.axis_size("near") + lax.axis_index("near")
+
+
 def shards(
     bundles,
     cell_state,
@@ -600,7 +613,7 @@
         ),
         scratch=(pltpu.VMEM((4, lines * blocks, LANES), F32),),
     )[0]
-    back = lax.all_to_all(sums, ("bundle", "grid"), split_axis=0, concat_axis=0, tiled=True)
+    back = lax.all_to_all(sums, ("near", "far", "grid"), split_axis=0, concat_axis=0, tiled=True)
     return call(
         functools.partial(blend_kernel, bundles),
         [(cell_state.shape, F32)],
@@ -611,20 +624,25 @@
 
 
 def solution(mesh):
+    bundles = mesh.shape["bundle"]
+    near = near_size(bundles)
+    devices = mesh.devices.reshape(mesh.shape["grid"], bundles // near, near)
+    finer = jax.sharding.Mesh(devices, ("grid", "far", "near"))
+    bundle = ("far", "near")
     placed = (
         P(None, "grid"),
         P("grid"),
         P(None, "grid", None, None),
-        P("bundle", "grid", None),
-        P("bundle", "grid"),
-        P("bundle", "grid", None),
-        P("bundle", "grid", None),
-        P("bundle", None),
+        P(bundle, "grid", None),
+        P(bundle, "grid"),
+        P(bundle, "grid", None),
+        P(bundle, "grid", None),
+        P(bundle, None),
         P(),
     )
     return jax.shard_map(
-        functools.partial(shards, mesh.shape["bundle"]),
-        mesh=mesh,
+        functools.partial(shards, bundles),
+        mesh=finer,
         in_specs=placed,
         out_specs=P(None, "grid"),
         check_vma=False,

time: 29 us -> 29.3 us (1.010)
  blocking collectives: 23.4 us -> 23.7 us
where the time goes in v15:
time: 29.3 us; the launch traced here: 29 us
  blocking collectives  23.7 us (81%)
  Pallas kernels  4.42 us (15%)
  local copies, waits for them, and re-layouts  0.81 us (3%)
    all_to_all x1, blocking collectives, shards(): lax.all_to_all(outgoing, 'grid', split_axis=0, concat_axis=0, tiled=True)  13.9 us
    all_to_all x1, blocking collectives, shards(): lax.all_to_all(sums, ('near', 'far', 'grid'), split_axis=0, concat_axis=0...  9.8 us
    pallas_call x5, Pallas kernels, call(): pl.pallas_call(kernel, out_shape=[jax.ShapeDtypeStruct(shape, kind) for s...  4.42 us
    unnamed x18, local copies, waits for them, and re-layouts  0.81 us

profile of v15, /device:TPU:0, one launch (start us, length us, event | category | flops | bytes accessed | tf_op | source)
XLA Modules:
  0.0 29.0 jit_solution(8901704603120919762)
XLA Ops:
  0.0 0.0 copy-start.1
  0.0 0.0 copy-start.8
  0.0 0.0 copy-start.7
  0.0 0.0 copy-start
  0.0 0.7 %copy-done.1 = s32[4,1,8,32]{3,2,1,0:T(8,128)S(1)} copy-done((s32[4,1,8,32]{3,2,1,0:T(8,128)S(1)}, s32[4,1,8,32]{3,2,1,0:T(8,128)}, u32[]{:S(2)}) %copy-start.1) | copy-done | bytes 4120
  0.7 0.0 copy-done.8
  0.7 0.0 copy-done.7
  0.7 0.2 shard_map.92
  1.0 0.1 copy-done
  1.0 0.4 %shard_map.93 = f32[8,8,128]{2,1,0:T(8,128)S(1)} custom-call(f32[24,4096]{1,0:T(8,128)S(1)} %copy-done, s32[4,1,8,32]{3,2,1,0:T(8,128)S(1)} %copy-done.1, f32[8,128]{1,0:T(8,128)S(1)} %shard_map.91.first_ref, s32[8,256]{1,0:T(8,128)S(1)} %get-tuple-element.9.refs_0_, bf16[256,256]{1,0:T(8,128)(2,1)S(1)} %get-tuple-element.10.refs_1_), custom_call_target="tpu_custom_call" | custom-call | tf_op jit(solution)/shard_map/pallas_call | solution.py:546
  1.4 0.0 copy-start.3
  1.4 0.0 copy-start.4
  1.4 0.0 copy-start.5
  1.4 0.0 copy-start.6
  1.4 13.9 %all_to_all.10.table_ref = f32[8,8,128]{2,1,0:T(8,128)S(1)} all-to-all(f32[8,8,128]{2,1,0:T(8,128)S(1)} %shard_map.93), channel_id=1, replica_groups=mesh['grid'=8,'far'=2,'near'=2] {'grid'}, dimensions={0} | all-to-all | bytes 65536 | tf_op jit(solution)/shard_map/all_to_all | solution.py:595
  15.3 0.0 copy-done.3
  15.3 0.0 copy-done.4
  15.3 0.0 copy-done.5
  15.3 0.0 copy-done.6
  15.4 2.4 %shard_map.94 = f32[32,8,128]{2,1,0:T(8,128)S(1)} custom-call(f32[8,8,128]{2,1,0:T(8,128)S(1)} %all_to_all.10.table_ref, s32[32,128]{1,0:T(8,128)S(1)} %bitcast.17, s32[1,2]{1,0:T(1,128)S(1)} %copy-done.7, f32[32,128]{1,0:T(8,128)S(1)} %bitcast.18, f32[32,128]{1,0:T(8,128)S(1)} %bitcast.19, f32[1,24]{1,0:T(1,128)S(1)} %copy-done.8, f32[24,24]{1,0:T(8,128)S(1)} %copy-done.6), custom_call_target="tpu_custom_call" | custom-call | tf_op jit(solution)/shard_map/pallas_call | solution.py:546
  17.8 0.0 copy-start.2
  17.8 9.8 %all_to_all.11.sums_ref = f32[32,8,128]{2,1,0:T(8,128)S(1)} all-to-all(f32[32,8,128]{2,1,0:T(8,128)S(1)} %shard_map.94), channel_id=1, replica_groups=mesh['grid'=8,'far'=2,'near'=2] {'near','far','grid'}, dimensions={0} | all-to-all | bytes 262144 | tf_op jit(solution)/shard_map/all_to_all | solution.py:616
  27.6 0.0 copy-done.2
  27.6 1.4 %shard_map.95 = f32[24,4096]{1,0:T(8,128)} custom-call(f32[32,8,128]{2,1,0:T(8,128)S(1)} %all_to_all.11.sums_ref, s32[4,1,8,32]{3,2,1,0:T(8,128)S(1)} %copy-done.1, f32[1,4096]{1,0:T(1,128)S(1)} %bitcast.16, f32[24,4096]{1,0:T(8,128)S(1)} %copy-done, bf16[16,1024]{1,0:T(8,128)(2,1)S(1)} %get-tuple-element.11.refs_0_, ...), custom_call_target="tpu_custom_call" | custom-call | tf_op jit(solution)/shard_map/pallas_call | solution.py:546
  (1 shorter events, 0.0 us)
Async XLA Ops:
  0.0 0.7 %copy-start.1 = (s32[4,1,8,32]{3,2,1,0:T(8,128)S(1)}, s32[4,1,8,32]{3,2,1,0:T(8,128)}, u32[]{:S(2)}) copy-start(s32[4,1,8,32]{3,2,1,0:T(8,128)} %request_ref.5) | copy-start | bytes 12292
  0.0 0.7 %copy-start.8 = (f32[1,24]{1,0:T(1,128)S(1)}, f32[1,24]{1,0:T(1,128)}, u32[]{:S(2)}) copy-start(f32[1,24]{1,0:T(1,128)} %inflow_ref.3) | copy-start | bytes 292
  0.0 0.7 %copy-start.7 = (s32[1,2]{1,0:T(1,128)S(1)}, s32[1,2]{1,0:T(1,128)}, u32[]{:S(2)}) copy-start(s32[1,2]{1,0:T(1,128)} %length_ref.3) | copy-start | bytes 28
  0.0 1.0 %copy-start = (f32[24,4096]{1,0:T(8,128)S(1)}, f32[24,4096]{1,0:T(8,128)}, u32[]{:S(2)}) copy-start(f32[24,4096]{1,0:T(8,128)} %cell_ref.3) | copy-start | bytes 1179652
  1.4 13.9 %copy-start.3 = (s32[1,2,2048]{2,1,0:T(2,128)S(1)}, s32[1,2,2048]{2,1,0:T(2,128)}, u32[]{:S(2)}) copy-start(s32[1,2,2048]{2,1,0:T(2,128)} %param.12) | copy-start | bytes 49156
  1.4 13.9 %copy-start.4 = (f32[1,2,2048]{2,1,0:T(2,128)S(1)}, f32[1,2,2048]{2,1,0:T(2,128)}, u32[]{:S(2)}) copy-start(f32[1,2,2048]{2,1,0:T(2,128)} %param.14) | copy-start | bytes 49156
  1.4 13.9 %copy-start.5 = (f32[1,2,2048]{2,1,0:T(2,128)S(1)}, f32[1,2,2048]{2,1,0:T(2,128)}, u32[]{:S(2)}) copy-start(f32[1,2,2048]{2,1,0:T(2,128)} %param.15) | copy-start | bytes 49156
  1.4 13.9 %copy-start.6 = (f32[24,24]{1,0:T(8,128)S(1)}, f32[24,24]{1,0:T(8,128)}, u32[]{:S(2)}) copy-start(f32[24,24]{1,0:T(8,128)} %interaction_ref.1) | copy-start | bytes 6916
  17.8 9.8 %copy-start.2 = (f32[4096]{0:T(1024)S(1)}, f32[4096]{0:T(1024)}, u32[]{:S(2)}) copy-start(f32[4096]{0:T(1024)} %param.10) | copy-start | bytes 49156

commit v16 on v14

--- a/solution.py
+++ b/solution.py
@@ -196,6 +196,9 @@
     chunk_owners = 2 * all_groups
     chunks = owners // chunk_owners
     here, bundle = lax.axis_index("grid"), lax.axis_index("bundle")
+    half = times // 2
+    depth = half // CHUNKS
+    units = 2 * CHUNKS
 
     slot = slot_ref[...]
     within = (slot + lax.rem(here, all_groups) * cap) % LANES
@@ -220,7 +223,9 @@
             local = (row(3, t, 2 * ROWS) - base).astype(BF16)
             local = jnp.concatenate([local] * (LANES // ROWS), axis=0)
             columns.append(jnp.where(local == index, one, zero))
-        return jnp.concatenate(columns, axis=1)
+        return [
+            jnp.concatenate(columns[t : t + depth], axis=1) for t in range(0, times, depth)
+        ]
 
     kept = hot(0) if chunks == 1 else None
 
@@ -239,13 +244,22 @@
                 )
             )
         left = split(jnp.concatenate(halves, axis=1))
-        found = jnp.dot(left, hot(k) if kept is None else kept, preferred_element_type=F32)
-        found = found[:species] + found[species:]
-        return found if chunks == 1 else state + found
+        if kept is not None:
+            return left
+        found = [jnp.dot(left, columns, preferred_element_type=F32) for columns in hot(k)]
+        return [s + f[:species] + f[species:] for s, f in zip(state, found)]
 
     start = repeat_steps(
-        chunks, gather, jnp.zeros((species, lines * nodes), F32) if chunks > 1 else 0
-    )
+        chunks,
+        gather,
+        [jnp.zeros((species, depth * LANES), F32)] * units if chunks > 1 else 0,
+    )
+
+    def started(unit):
+        if kept is None:
+            return start[unit]
+        found = jnp.dot(start, kept[unit], preferred_element_type=F32)
+        return found[:species] + found[species:]
 
     lane = lax.broadcasted_iota(jnp.int32, (ROWS, LANES), 1)
     part = lane // width
@@ -272,14 +286,19 @@
     first = [None] * groups
     second = [None] * groups
     local, ones, twos = [], [], []
+    ahead_unit = started(0)
     for t in range(times):
+        if t % depth == 0:
+            unit = ahead_unit
+            ahead_unit = started(t // depth + 1) if t // depth + 1 < units else None
         scale_t, decay_t = row(0, t), row(1, t)
         one = decay_t if t == 0 else decay_t * ones[-1]
         two = scale_t * one if t == 0 else scale_t * one + decay_t * twos[-1]
         ones.append(one)
         twos.append(two)
         for g in range(groups):
-            value = start[ROWS * g : ROWS * (g + 1), LANES * t : LANES * (t + 1)] * scale_t
+            lanes = slice(LANES * (t % depth), LANES * (t % depth + 1))
+            value = unit[ROWS * g : ROWS * (g + 1), lanes] * scale_t
             first[g] = value if t == 0 else value + decay_t * first[g]
             value = scale_t * first[g]
             second[g] = value if t == 0 else value + decay_t * second[g]
@@ -336,8 +355,6 @@
         ],
         axis=0,
     ).astype(BF16)
-    half = times // 2
-    depth = half // CHUNKS
     bases = [
         jnp.concatenate(
             [
@@ -348,39 +365,59 @@
         )
         for c in range(CHUNKS)
     ]
-    iterates = list(bases)
-    for step in range(NEWTON):
-        for c in range(CHUNKS):
-            high, low = parts(jnp.tanh(iterates[c]))
-            right = jnp.concatenate([high, high, low], axis=0)
-            iterates[c] = bases[c] - jnp.dot(left, right, preferred_element_type=F32)
-
     length = jnp.zeros((ROWS, LANES), jnp.int32)
     for one_line in range(lines):
         one_length = jnp.broadcast_to(length_ref[:, one_line : one_line + 1], (ROWS, LANES))
         length = jnp.where(line == one_line, one_length, length)
     node = block * LANES + part * times
     top = lax.broadcasted_iota(jnp.int32, (ROWS, LANES), 0) == 0
-    pieces = []
-    for t in range(times):
-        weight = jnp.where(node + t < length, row(2, t), 0.0)
-        chunk, place = t % half // depth, t % half % depth
-        found = iterates[chunk][
-            t // half * species : (t // half + 1) * species, LANES * place : LANES * (place + 1)
-        ]
-        scaled = [found[ROWS * g : ROWS * (g + 1)] * weight for g in range(groups)]
-        scaled.append(jnp.where(top, weight, 0.0))
-        pieces.append(jnp.concatenate(scaled, axis=0))
-    left = split(jnp.concatenate(pieces, axis=1))
-    relative = lane_groups(cap, here + bundle)
-
-    def scatter(k, carry):
-        sums = lax.dot_general(
-            left,
-            hot(k) if kept is None else kept,
+
+    def weighted(found, c):
+        pieces = []
+        for side in range(2):
+            for place in range(depth):
+                t = side * half + c * depth + place
+                weight = jnp.where(node + t < length, row(2, t), 0.0)
+                columns = slice(LANES * place, LANES * (place + 1))
+                scaled = [
+                    found[side * species + ROWS * g : side * species + ROWS * (g + 1), columns]
+                    * weight
+                    for g in range(groups)
+                ]
+                scaled.append(jnp.where(top, weight, 0.0))
+                pieces.append(jnp.concatenate(scaled, axis=0))
+        return split(jnp.concatenate(pieces, axis=1))
+
+    def slot_sums(value, columns, c):
+        return lax.dot_general(
+            value,
+            jnp.concatenate([columns[c], columns[CHUNKS + c]], axis=1),
             (((1,), (1,)), ((), ())),
             preferred_element_type=F32,
         )
+
+    iterates = list(bases)
+    lefts = []
+    kept_sums = None
+    for step in range(NEWTON):
+        for c in range(CHUNKS):
+            high, low = parts(jnp.tanh(iterates[c]))
+            right = jnp.concatenate([high, high, low], axis=0)
+            iterates[c] = bases[c] - jnp.dot(left, right, preferred_element_type=F32)
+            if step == NEWTON - 1:
+                lefts.append(weighted(iterates[c], c))
+                if kept is not None:
+                    found = slot_sums(lefts[c], kept, c)
+                    kept_sums = found if c == 0 else kept_sums + found
+
+    relative = lane_groups(cap, here + bundle)
+
+    def scatter(k, carry):
+        if kept is None:
+            columns = hot(k)
+            sums = sum(slot_sums(lefts[c], columns, c) for c in range(CHUNKS))
+        else:
+            sums = kept_sums
         sums = sums[:rows] + sums[rows:]
         for half in range(2):
             tiles = pack(

time: 29 us -> 29.5 us (1.017)
  Pallas kernels: 4.42 us -> 4.88 us
    pallas_call x5, Pallas kernels: 4.42 us -> 4.88 us  [call(): pl.pallas_call(kernel, out_shape=[jax.ShapeDtypeStruct(shape, kind) for s...]
where the time goes in v16:
time: 29.5 us; the launch traced here: 29.2 us
  blocking collectives  23.4 us (79%)
  Pallas kernels  4.88 us (17%)
  local copies, waits for them, and re-layouts  0.81 us (3%)
    all_to_all x1, blocking collectives, shards(): lax.all_to_all(outgoing, 'grid', split_axis=0, concat_axis=0, tiled=True)  13.9 us
    all_to_all x1, blocking collectives, shards(): lax.all_to_all(sums, ('bundle', 'grid'), split_axis=0, concat_axis=0, til...  9.53 us
    pallas_call x5, Pallas kernels, call(): pl.pallas_call(kernel, out_shape=[jax.ShapeDtypeStruct(shape, kind) for s...  4.88 us
    unnamed x18, local copies, waits for them, and re-layouts  0.81 us

profile of v16, /device:TPU:0, one launch (start us, length us, event | category | flops | bytes accessed | tf_op | source)
XLA Modules:
  0.0 29.2 jit_solution(16594826317810891860)
XLA Ops:
  0.0 0.0 copy-start.1
  0.0 0.0 copy-start.8
  0.0 0.0 copy-start.7
  0.0 0.0 copy-start
  0.0 0.7 %copy-done.1 = s32[4,1,8,32]{3,2,1,0:T(8,128)S(1)} copy-done((s32[4,1,8,32]{3,2,1,0:T(8,128)S(1)}, s32[4,1,8,32]{3,2,1,0:T(8,128)}, u32[]{:S(2)}) %copy-start.1) | copy-done | bytes 4120
  0.7 0.0 copy-done.8
  0.7 0.0 copy-done.7
  0.7 0.2 shard_map.92
  1.0 0.1 copy-done
  1.0 0.4 %shard_map.93 = f32[8,8,128]{2,1,0:T(8,128)S(1)} custom-call(f32[24,4096]{1,0:T(8,128)S(1)} %copy-done, s32[4,1,8,32]{3,2,1,0:T(8,128)S(1)} %copy-done.1, f32[8,128]{1,0:T(8,128)S(1)} %shard_map.91.first_ref, s32[8,256]{1,0:T(8,128)S(1)} %get-tuple-element.9.refs_0_, bf16[256,256]{1,0:T(8,128)(2,1)S(1)} %get-tuple-element.10.refs_1_), custom_call_target="tpu_custom_call" | custom-call | tf_op jit(solution)/shard_map/pallas_call | solution.py:574
  1.4 0.0 copy-start.3
  1.4 0.0 copy-start.4
  1.4 0.0 copy-start.5
  1.4 0.0 copy-start.6
  1.4 13.9 %all_to_all.10.table_ref = f32[8,8,128]{2,1,0:T(8,128)S(1)} all-to-all(f32[8,8,128]{2,1,0:T(8,128)S(1)} %shard_map.93), channel_id=1, replica_groups=mesh['grid'=8,'bundle'=4] {'grid'}, dimensions={0} | all-to-all | bytes 65536 | tf_op jit(solution)/shard_map/all_to_all | solution.py:619
  15.3 0.0 copy-done.3
  15.3 0.0 copy-done.4
  15.3 0.0 copy-done.5
  15.3 0.0 copy-done.6
  15.4 2.9 %shard_map.94 = f32[32,8,128]{2,1,0:T(8,128)S(1)} custom-call(f32[8,8,128]{2,1,0:T(8,128)S(1)} %all_to_all.10.table_ref, s32[32,128]{1,0:T(8,128)S(1)} %bitcast.17, s32[1,2]{1,0:T(1,128)S(1)} %copy-done.7, f32[32,128]{1,0:T(8,128)S(1)} %bitcast.18, f32[32,128]{1,0:T(8,128)S(1)} %bitcast.19, f32[1,24]{1,0:T(1,128)S(1)} %copy-done.8, f32[24,24]{1,0:T(8,128)S(1)} %copy-done.6), custom_call_target="tpu_custom_call" | custom-call | tf_op jit(solution)/shard_map/pallas_call | solution.py:574
  18.2 0.0 copy-start.2
  18.2 9.5 %all_to_all.11.sums_ref = f32[32,8,128]{2,1,0:T(8,128)S(1)} all-to-all(f32[32,8,128]{2,1,0:T(8,128)S(1)} %shard_map.94), channel_id=1, replica_groups=mesh['grid'=8,'bundle'=4] {'bundle','grid'}, dimensions={0} | all-to-all | bytes 262144 | tf_op jit(solution)/shard_map/all_to_all | solution.py:640
  27.8 0.0 copy-done.2
  27.8 1.4 %shard_map.95 = f32[24,4096]{1,0:T(8,128)} custom-call(f32[32,8,128]{2,1,0:T(8,128)S(1)} %all_to_all.11.sums_ref, s32[4,1,8,32]{3,2,1,0:T(8,128)S(1)} %copy-done.1, f32[1,4096]{1,0:T(1,128)S(1)} %bitcast.16, f32[24,4096]{1,0:T(8,128)S(1)} %copy-done, bf16[16,1024]{1,0:T(8,128)(2,1)S(1)} %get-tuple-element.11.refs_0_, ...), custom_call_target="tpu_custom_call" | custom-call | tf_op jit(solution)/shard_map/pallas_call | solution.py:574
  (1 shorter events, 0.0 us)
Async XLA Ops:
  0.0 0.7 %copy-start.1 = (s32[4,1,8,32]{3,2,1,0:T(8,128)S(1)}, s32[4,1,8,32]{3,2,1,0:T(8,128)}, u32[]{:S(2)}) copy-start(s32[4,1,8,32]{3,2,1,0:T(8,128)} %request_ref.5) | copy-start | bytes 12292
  0.0 0.7 %copy-start.8 = (f32[1,24]{1,0:T(1,128)S(1)}, f32[1,24]{1,0:T(1,128)}, u32[]{:S(2)}) copy-start(f32[1,24]{1,0:T(1,128)} %inflow_ref.3) | copy-start | bytes 292
  0.0 0.7 %copy-start.7 = (s32[1,2]{1,0:T(1,128)S(1)}, s32[1,2]{1,0:T(1,128)}, u32[]{:S(2)}) copy-start(s32[1,2]{1,0:T(1,128)} %length_ref.3) | copy-start | bytes 28
  0.0 1.0 %copy-start = (f32[24,4096]{1,0:T(8,128)S(1)}, f32[24,4096]{1,0:T(8,128)}, u32[]{:S(2)}) copy-start(f32[24,4096]{1,0:T(8,128)} %cell_ref.3) | copy-start | bytes 1179652
  1.4 13.9 %copy-start.3 = (s32[1,2,2048]{2,1,0:T(2,128)S(1)}, s32[1,2,2048]{2,1,0:T(2,128)}, u32[]{:S(2)}) copy-start(s32[1,2,2048]{2,1,0:T(2,128)} %param.12) | copy-start | bytes 49156
  1.4 13.9 %copy-start.4 = (f32[1,2,2048]{2,1,0:T(2,128)S(1)}, f32[1,2,2048]{2,1,0:T(2,128)}, u32[]{:S(2)}) copy-start(f32[1,2,2048]{2,1,0:T(2,128)} %param.14) | copy-start | bytes 49156
  1.4 13.9 %copy-start.5 = (f32[1,2,2048]{2,1,0:T(2,128)S(1)}, f32[1,2,2048]{2,1,0:T(2,128)}, u32[]{:S(2)}) copy-start(f32[1,2,2048]{2,1,0:T(2,128)} %param.15) | copy-start | bytes 49156
  1.4 13.9 %copy-start.6 = (f32[24,24]{1,0:T(8,128)S(1)}, f32[24,24]{1,0:T(8,128)}, u32[]{:S(2)}) copy-start(f32[24,24]{1,0:T(8,128)} %interaction_ref.1) | copy-start | bytes 6916
  18.2 9.5 %copy-start.2 = (f32[4096]{0:T(1024)S(1)}, f32[4096]{0:T(1024)}, u32[]{:S(2)}) copy-start(f32[4096]{0:T(1024)} %param.10) | copy-start | bytes 49156

commit v17 on v14

--- a/solution.py
+++ b/solution.py
@@ -14,7 +14,7 @@
 F32 = jnp.float32
 BF16 = jnp.bfloat16
 VMEM_BYTES = 32 * 1024 * 1024
-CHUNKS = 4
+CHUNKS = 1
 
 
 def repeat_steps(count, body, carry):

time: 29 us -> 29 us (level)
  no operation moved by 1% of the time
where the time goes in v17:
time: 29 us; the launch traced here: 28.7 us
  blocking collectives  23.4 us (81%)
  Pallas kernels  4.42 us (15%)
  local copies, waits for them, and re-layouts  0.81 us (3%)
    all_to_all x1, blocking collectives, shards(): lax.all_to_all(outgoing, 'grid', split_axis=0, concat_axis=0, tiled=True)  13.9 us
    all_to_all x1, blocking collectives, shards(): lax.all_to_all(sums, ('bundle', 'grid'), split_axis=0, concat_axis=0, til...  9.54 us
    pallas_call x5, Pallas kernels, call(): pl.pallas_call(kernel, out_shape=[jax.ShapeDtypeStruct(shape, kind) for s...  4.42 us
    unnamed x18, local copies, waits for them, and re-layouts  0.81 us

profile of v17, /device:TPU:0, one launch (start us, length us, event | category | flops | bytes accessed | tf_op | source)
XLA Modules:
  0.0 28.7 jit_solution(18003957276363124767)
XLA Ops:
  0.0 0.0 copy-start.1
  0.0 0.0 copy-start.8
  0.0 0.0 copy-start.7
  0.0 0.0 copy-start
  0.0 0.7 %copy-done.1 = s32[4,1,8,32]{3,2,1,0:T(8,128)S(1)} copy-done((s32[4,1,8,32]{3,2,1,0:T(8,128)S(1)}, s32[4,1,8,32]{3,2,1,0:T(8,128)}, u32[]{:S(2)}) %copy-start.1) | copy-done | bytes 4120
  0.7 0.0 copy-done.8
  0.7 0.0 copy-done.7
  0.7 0.2 shard_map.92
  1.0 0.1 copy-done
  1.0 0.4 %shard_map.93 = f32[8,8,128]{2,1,0:T(8,128)S(1)} custom-call(f32[24,4096]{1,0:T(8,128)S(1)} %copy-done, s32[4,1,8,32]{3,2,1,0:T(8,128)S(1)} %copy-done.1, f32[8,128]{1,0:T(8,128)S(1)} %shard_map.91.first_ref, s32[8,256]{1,0:T(8,128)S(1)} %get-tuple-element.9.refs_0_, bf16[256,256]{1,0:T(8,128)(2,1)S(1)} %get-tuple-element.10.refs_1_), custom_call_target="tpu_custom_call" | custom-call | tf_op jit(solution)/shard_map/pallas_call | solution.py:537
  1.4 0.0 copy-start.3
  1.4 0.0 copy-start.4
  1.4 0.0 copy-start.5
  1.4 0.0 copy-start.6
  1.4 13.9 %all_to_all.10.table_ref = f32[8,8,128]{2,1,0:T(8,128)S(1)} all-to-all(f32[8,8,128]{2,1,0:T(8,128)S(1)} %shard_map.93), channel_id=1, replica_groups=mesh['grid'=8,'bundle'=4] {'grid'}, dimensions={0} | all-to-all | bytes 65536 | tf_op jit(solution)/shard_map/all_to_all | solution.py:582
  15.3 0.0 copy-done.3
  15.3 0.0 copy-done.4
  15.3 0.0 copy-done.5
  15.3 0.0 copy-done.6
  15.4 2.4 %shard_map.94 = f32[32,8,128]{2,1,0:T(8,128)S(1)} custom-call(f32[8,8,128]{2,1,0:T(8,128)S(1)} %all_to_all.10.table_ref, s32[32,128]{1,0:T(8,128)S(1)} %bitcast.17, s32[1,2]{1,0:T(1,128)S(1)} %copy-done.7, f32[32,128]{1,0:T(8,128)S(1)} %bitcast.18, f32[32,128]{1,0:T(8,128)S(1)} %bitcast.19, f32[1,24]{1,0:T(1,128)S(1)} %copy-done.8, f32[24,24]{1,0:T(8,128)S(1)} %copy-done.6), custom_call_target="tpu_custom_call" | custom-call | tf_op jit(solution)/shard_map/pallas_call | solution.py:537
  17.8 0.0 copy-start.2
  17.8 9.5 %all_to_all.11.sums_ref = f32[32,8,128]{2,1,0:T(8,128)S(1)} all-to-all(f32[32,8,128]{2,1,0:T(8,128)S(1)} %shard_map.94), channel_id=1, replica_groups=mesh['grid'=8,'bundle'=4] {'bundle','grid'}, dimensions={0} | all-to-all | bytes 262144 | tf_op jit(solution)/shard_map/all_to_all | solution.py:603
  27.3 0.0 copy-done.2
  27.3 1.4 %shard_map.95 = f32[24,4096]{1,0:T(8,128)} custom-call(f32[32,8,128]{2,1,0:T(8,128)S(1)} %all_to_all.11.sums_ref, s32[4,1,8,32]{3,2,1,0:T(8,128)S(1)} %copy-done.1, f32[1,4096]{1,0:T(1,128)S(1)} %bitcast.16, f32[24,4096]{1,0:T(8,128)S(1)} %copy-done, bf16[16,1024]{1,0:T(8,128)(2,1)S(1)} %get-tuple-element.11.refs_0_, ...), custom_call_target="tpu_custom_call" | custom-call | tf_op jit(solution)/shard_map/pallas_call | solution.py:537
  (1 shorter events, 0.0 us)
Async XLA Ops:
  0.0 0.7 %copy-start.1 = (s32[4,1,8,32]{3,2,1,0:T(8,128)S(1)}, s32[4,1,8,32]{3,2,1,0:T(8,128)}, u32[]{:S(2)}) copy-start(s32[4,1,8,32]{3,2,1,0:T(8,128)} %request_ref.5) | copy-start | bytes 12292
  0.0 0.7 %copy-start.8 = (f32[1,24]{1,0:T(1,128)S(1)}, f32[1,24]{1,0:T(1,128)}, u32[]{:S(2)}) copy-start(f32[1,24]{1,0:T(1,128)} %inflow_ref.3) | copy-start | bytes 292
  0.0 0.7 %copy-start.7 = (s32[1,2]{1,0:T(1,128)S(1)}, s32[1,2]{1,0:T(1,128)}, u32[]{:S(2)}) copy-start(s32[1,2]{1,0:T(1,128)} %length_ref.3) | copy-start | bytes 28
  0.0 1.0 %copy-start = (f32[24,4096]{1,0:T(8,128)S(1)}, f32[24,4096]{1,0:T(8,128)}, u32[]{:S(2)}) copy-start(f32[24,4096]{1,0:T(8,128)} %cell_ref.3) | copy-start | bytes 1179652
  1.4 13.9 %copy-start.3 = (s32[1,2,2048]{2,1,0:T(2,128)S(1)}, s32[1,2,2048]{2,1,0:T(2,128)}, u32[]{:S(2)}) copy-start(s32[1,2,2048]{2,1,0:T(2,128)} %param.12) | copy-start | bytes 49156
  1.4 13.9 %copy-start.4 = (f32[1,2,2048]{2,1,0:T(2,128)S(1)}, f32[1,2,2048]{2,1,0:T(2,128)}, u32[]{:S(2)}) copy-start(f32[1,2,2048]{2,1,0:T(2,128)} %param.14) | copy-start | bytes 49156
  1.4 13.9 %copy-start.5 = (f32[1,2,2048]{2,1,0:T(2,128)S(1)}, f32[1,2,2048]{2,1,0:T(2,128)}, u32[]{:S(2)}) copy-start(f32[1,2,2048]{2,1,0:T(2,128)} %param.15) | copy-start | bytes 49156
  1.4 13.9 %copy-start.6 = (f32[24,24]{1,0:T(8,128)S(1)}, f32[24,24]{1,0:T(8,128)}, u32[]{:S(2)}) copy-start(f32[24,24]{1,0:T(8,128)} %interaction_ref.1) | copy-start | bytes 6916
  17.8 9.6 %copy-start.2 = (f32[4096]{0:T(1024)S(1)}, f32[4096]{0:T(1024)}, u32[]{:S(2)}) copy-start(f32[4096]{0:T(1024)} %param.10) | copy-start | bytes 49156

commit v18 on v17

--- a/solution.py
+++ b/solution.py
@@ -163,7 +163,8 @@
 def to_segments(values, width):
     groups = LANES // width
     stacked = [value.astype(F32) for value in values]
-    stacked.append(jnp.zeros((LANES - width * len(values), LANES), F32))
+    if width * len(values) < LANES:
+        stacked.append(jnp.zeros((LANES - width * len(values), LANES), F32))
     turned = jnp.transpose(jnp.concatenate(stacked, axis=0))
     times = LANES // groups
     return exchange_groups([turned[times * g : times * (g + 1)] for g in range(groups)], width)
@@ -199,30 +200,28 @@
 
     slot = slot_ref[...]
     within = (slot + lax.rem(here, all_groups) * cap) % LANES
-    slot, courant, flux = to_segments(
-        [slot - slot % LANES + within, courant_ref[...], flux_ref[...]], width
-    )[:3]
+    within, half_index, courant, flux = to_segments(
+        [within, slot // LANES, courant_ref[...], flux_ref[...]], width
+    )[:4]
     scale = 1.0 / (1.0 + courant)
     rows_ref[0] = scale
     rows_ref[1] = courant * scale
     rows_ref[2] = flux
-    rows_ref[3] = slot
+    rows_ref[3] = within
+    rows_ref[4] = half_index
 
     def row(kind, t, depth=ROWS):
         return jnp.broadcast_to(rows_ref[kind, t : t + 1], (depth, LANES))
 
-    def hot(k):
-        index = lax.broadcasted_iota(jnp.int32, (2 * LANES, LANES), 0).astype(F32).astype(BF16)
-        one, zero = jnp.ones_like(index), jnp.zeros_like(index)
-        base = lax.convert_element_type(k * 2 * LANES, F32)
-        columns = []
-        for t in range(times):
-            local = (row(3, t, 2 * ROWS) - base).astype(BF16)
-            local = jnp.concatenate([local] * (LANES // ROWS), axis=0)
-            columns.append(jnp.where(local == index, one, zero))
-        return jnp.concatenate(columns, axis=1)
-
-    kept = hot(0) if chunks == 1 else None
+    index = lax.broadcasted_iota(jnp.int32, (LANES, LANES), 0).astype(F32).astype(BF16)
+    one, zero = jnp.ones_like(index), jnp.zeros_like(index)
+    columns = []
+    for t in range(times):
+        lanes = row(3, t, 2 * ROWS).astype(BF16)
+        lanes = jnp.concatenate([lanes] * (LANES // (2 * ROWS)), axis=0)
+        columns.append(jnp.where(lanes == index, one, zero))
+    hot = jnp.concatenate(columns, axis=1)
+    half_rows = jnp.concatenate([row(4, t) for t in range(times)], axis=1)
 
     relative = lane_groups(cap, here)
 
@@ -238,10 +237,15 @@
                     axis=0,
                 )
             )
-        left = split(jnp.concatenate(halves, axis=1))
-        found = jnp.dot(left, hot(k) if kept is None else kept, preferred_element_type=F32)
-        found = found[:species] + found[species:]
-        return found if chunks == 1 else state + found
+        left = jnp.concatenate([split(value) for value in halves], axis=0)
+        found = jnp.dot(left, hot, preferred_element_type=F32)
+        lower = found[:species] + found[species : 2 * species]
+        upper = found[2 * species : 3 * species] + found[3 * species :]
+        number = jnp.concatenate([half_rows] * groups, axis=0)
+        if chunks == 1:
+            return jnp.where(number == 0.0, lower, upper)
+        base = lax.convert_element_type(2 * k, F32)
+        return jnp.where(number == base, lower, jnp.where(number == base + 1.0, upper, state))
 
     start = repeat_steps(
         chunks, gather, jnp.zeros((species, lines * nodes), F32) if chunks > 1 else 0
@@ -374,20 +378,25 @@
     left = split(jnp.concatenate(pieces, axis=1))
     relative = lane_groups(cap, here + bundle)
 
+    half_rows = jnp.concatenate([half_rows] * (2 * rows // ROWS), axis=0).astype(BF16)
+
     def scatter(k, carry):
+        base = lax.convert_element_type(2 * k, F32)
+        masked = [
+            jnp.where(half_rows == (base + half).astype(BF16), left, jnp.zeros_like(left))
+            for half in range(2)
+        ]
         sums = lax.dot_general(
-            left,
-            hot(k) if kept is None else kept,
+            jnp.concatenate(masked, axis=0),
+            hot,
             (((1,), (1,)), ((), ())),
             preferred_element_type=F32,
         )
-        sums = sums[:rows] + sums[rows:]
         for half in range(2):
+            both = sums[2 * rows * half : 2 * rows * (half + 1)]
+            both = both[:rows] + both[rows:]
             tiles = pack(
-                [
-                    sums[ROWS * g : ROWS * (g + 1), LANES * half : LANES * (half + 1)]
-                    for g in range(all_groups)
-                ],
+                [both[ROWS * g : ROWS * (g + 1)] for g in range(all_groups)],
                 cap,
                 bundle,
                 relative,
@@ -598,7 +607,7 @@
             inflow,
             interaction,
         ),
-        scratch=(pltpu.VMEM((4, lines * blocks, LANES), F32),),
+        scratch=(pltpu.VMEM((5, lines * blocks, LANES), F32),),
     )[0]
     back = lax.all_to_all(sums, ("bundle", "grid"), split_axis=0, concat_axis=0, tiled=True)
     return call(

time: 29 us -> 28.7 us (0.990)
  Pallas kernels: 4.42 us -> 4.11 us
    pallas_call x5, Pallas kernels: 4.42 us -> 4.11 us  [call(): pl.pallas_call(kernel, out_shape=[jax.ShapeDtypeStruct(shape, kind) for s...]
where the time goes in v18:
time: 28.7 us; the launch traced here: 28.4 us
  blocking collectives  23.4 us (82%)
  Pallas kernels  4.11 us (14%)
  local copies, waits for them, and re-layouts  0.81 us (3%)
    all_to_all x1, blocking collectives, shards(): lax.all_to_all(outgoing, 'grid', split_axis=0, concat_axis=0, tiled=True)  13.9 us
    all_to_all x1, blocking collectives, shards(): lax.all_to_all(sums, ('bundle', 'grid'), split_axis=0, concat_axis=0, til...  9.54 us
    pallas_call x5, Pallas kernels, call(): pl.pallas_call(kernel, out_shape=[jax.ShapeDtypeStruct(shape, kind) for s...  4.11 us
    unnamed x18, local copies, waits for them, and re-layouts  0.81 us

profile of v18, /device:TPU:0, one launch (start us, length us, event | category | flops | bytes accessed | tf_op | source)
XLA Modules:
  0.0 28.4 jit_solution(12941324859545572178)
XLA Ops:
  0.0 0.0 copy-start.1
  0.0 0.0 copy-start.8
  0.0 0.0 copy-start.7
  0.0 0.0 copy-start
  0.0 0.7 %copy-done.1 = s32[4,1,8,32]{3,2,1,0:T(8,128)S(1)} copy-done((s32[4,1,8,32]{3,2,1,0:T(8,128)S(1)}, s32[4,1,8,32]{3,2,1,0:T(8,128)}, u32[]{:S(2)}) %copy-start.1) | copy-done | bytes 4120
  0.7 0.0 copy-done.8
  0.7 0.0 copy-done.7
  0.7 0.2 shard_map.92
  1.0 0.1 copy-done
  1.0 0.4 %shard_map.93 = f32[8,8,128]{2,1,0:T(8,128)S(1)} custom-call(f32[24,4096]{1,0:T(8,128)S(1)} %copy-done, s32[4,1,8,32]{3,2,1,0:T(8,128)S(1)} %copy-done.1, f32[8,128]{1,0:T(8,128)S(1)} %shard_map.91.first_ref, s32[8,256]{1,0:T(8,128)S(1)} %get-tuple-element.9.refs_0_, bf16[256,256]{1,0:T(8,128)(2,1)S(1)} %get-tuple-element.10.refs_1_), custom_call_target="tpu_custom_call" | custom-call | tf_op jit(solution)/shard_map/pallas_call | solution.py:546
  1.4 0.0 copy-start.3
  1.4 0.0 copy-start.4
  1.4 0.0 copy-start.5
  1.4 0.0 copy-start.6
  1.4 13.9 %all_to_all.10.table_ref = f32[8,8,128]{2,1,0:T(8,128)S(1)} all-to-all(f32[8,8,128]{2,1,0:T(8,128)S(1)} %shard_map.93), channel_id=1, replica_groups=mesh['grid'=8,'bundle'=4] {'grid'}, dimensions={0} | all-to-all | bytes 65536 | tf_op jit(solution)/shard_map/all_to_all | solution.py:591
  15.3 0.0 copy-done.3
  15.3 0.0 copy-done.4
  15.3 0.0 copy-done.5
  15.3 0.0 copy-done.6
  15.4 2.1 %shard_map.94 = f32[32,8,128]{2,1,0:T(8,128)S(1)} custom-call(f32[8,8,128]{2,1,0:T(8,128)S(1)} %all_to_all.10.table_ref, s32[32,128]{1,0:T(8,128)S(1)} %bitcast.17, s32[1,2]{1,0:T(1,128)S(1)} %copy-done.7, f32[32,128]{1,0:T(8,128)S(1)} %bitcast.18, f32[32,128]{1,0:T(8,128)S(1)} %bitcast.19, f32[1,24]{1,0:T(1,128)S(1)} %copy-done.8, f32[24,24]{1,0:T(8,128)S(1)} %copy-done.6), custom_call_target="tpu_custom_call" | custom-call | tf_op jit(solution)/shard_map/pallas_call | solution.py:546
  17.5 0.0 copy-start.2
  17.5 9.5 %all_to_all.11.sums_ref = f32[32,8,128]{2,1,0:T(8,128)S(1)} all-to-all(f32[32,8,128]{2,1,0:T(8,128)S(1)} %shard_map.94), channel_id=1, replica_groups=mesh['grid'=8,'bundle'=4] {'bundle','grid'}, dimensions={0} | all-to-all | bytes 262144 | tf_op jit(solution)/shard_map/all_to_all | solution.py:612
  27.0 0.0 copy-done.2
  27.0 1.4 %shard_map.95 = f32[24,4096]{1,0:T(8,128)} custom-call(f32[32,8,128]{2,1,0:T(8,128)S(1)} %all_to_all.11.sums_ref, s32[4,1,8,32]{3,2,1,0:T(8,128)S(1)} %copy-done.1, f32[1,4096]{1,0:T(1,128)S(1)} %bitcast.16, f32[24,4096]{1,0:T(8,128)S(1)} %copy-done, bf16[16,1024]{1,0:T(8,128)(2,1)S(1)} %get-tuple-element.11.refs_0_, ...), custom_call_target="tpu_custom_call" | custom-call | tf_op jit(solution)/shard_map/pallas_call | solution.py:546
  (1 shorter events, 0.0 us)
Async XLA Ops:
  0.0 0.7 %copy-start.1 = (s32[4,1,8,32]{3,2,1,0:T(8,128)S(1)}, s32[4,1,8,32]{3,2,1,0:T(8,128)}, u32[]{:S(2)}) copy-start(s32[4,1,8,32]{3,2,1,0:T(8,128)} %request_ref.5) | copy-start | bytes 12292
  0.0 0.7 %copy-start.8 = (f32[1,24]{1,0:T(1,128)S(1)}, f32[1,24]{1,0:T(1,128)}, u32[]{:S(2)}) copy-start(f32[1,24]{1,0:T(1,128)} %inflow_ref.3) | copy-start | bytes 292
  0.0 0.7 %copy-start.7 = (s32[1,2]{1,0:T(1,128)S(1)}, s32[1,2]{1,0:T(1,128)}, u32[]{:S(2)}) copy-start(s32[1,2]{1,0:T(1,128)} %length_ref.3) | copy-start | bytes 28
  0.0 1.0 %copy-start = (f32[24,4096]{1,0:T(8,128)S(1)}, f32[24,4096]{1,0:T(8,128)}, u32[]{:S(2)}) copy-start(f32[24,4096]{1,0:T(8,128)} %cell_ref.3) | copy-start | bytes 1179652
  1.4 13.9 %copy-start.3 = (s32[1,2,2048]{2,1,0:T(2,128)S(1)}, s32[1,2,2048]{2,1,0:T(2,128)}, u32[]{:S(2)}) copy-start(s32[1,2,2048]{2,1,0:T(2,128)} %param.12) | copy-start | bytes 49156
  1.4 13.9 %copy-start.4 = (f32[1,2,2048]{2,1,0:T(2,128)S(1)}, f32[1,2,2048]{2,1,0:T(2,128)}, u32[]{:S(2)}) copy-start(f32[1,2,2048]{2,1,0:T(2,128)} %param.14) | copy-start | bytes 49156
  1.4 13.9 %copy-start.5 = (f32[1,2,2048]{2,1,0:T(2,128)S(1)}, f32[1,2,2048]{2,1,0:T(2,128)}, u32[]{:S(2)}) copy-start(f32[1,2,2048]{2,1,0:T(2,128)} %param.15) | copy-start | bytes 49156
  1.4 13.9 %copy-start.6 = (f32[24,24]{1,0:T(8,128)S(1)}, f32[24,24]{1,0:T(8,128)}, u32[]{:S(2)}) copy-start(f32[24,24]{1,0:T(8,128)} %interaction_ref.1) | copy-start | bytes 6916
  17.5 9.6 %copy-start.2 = (f32[4096]{0:T(1024)S(1)}, f32[4096]{0:T(1024)}, u32[]{:S(2)}) copy-start(f32[4096]{0:T(1024)} %param.10) | copy-start | bytes 49156

commit v19 on v18

--- a/solution.py
+++ b/solution.py
@@ -241,11 +241,16 @@
         found = jnp.dot(left, hot, preferred_element_type=F32)
         lower = found[:species] + found[species : 2 * species]
         upper = found[2 * species : 3 * species] + found[3 * species :]
-        number = jnp.concatenate([half_rows] * groups, axis=0)
-        if chunks == 1:
-            return jnp.where(number == 0.0, lower, upper)
         base = lax.convert_element_type(2 * k, F32)
-        return jnp.where(number == base, lower, jnp.where(number == base + 1.0, upper, state))
+        is_lower, is_upper = half_rows == base, half_rows == base + 1.0
+        merged = []
+        for g in range(groups):
+            part_rows = slice(ROWS * g, ROWS * (g + 1))
+            rest = upper[part_rows]
+            if chunks > 1:
+                rest = jnp.where(is_upper, rest, state[part_rows])
+            merged.append(jnp.where(is_lower, lower[part_rows], rest))
+        return jnp.concatenate(merged, axis=0)
 
     start = repeat_steps(
         chunks, gather, jnp.zeros((species, lines * nodes), F32) if chunks > 1 else 0
@@ -378,14 +383,16 @@
     left = split(jnp.concatenate(pieces, axis=1))
     relative = lane_groups(cap, here + bundle)
 
-    half_rows = jnp.concatenate([half_rows] * (2 * rows // ROWS), axis=0).astype(BF16)
+    half_rows = jnp.concatenate([half_rows] * 2, axis=0).astype(BF16)
 
     def scatter(k, carry):
         base = lax.convert_element_type(2 * k, F32)
-        masked = [
-            jnp.where(half_rows == (base + half).astype(BF16), left, jnp.zeros_like(left))
-            for half in range(2)
-        ]
+        masked = []
+        for half in range(2):
+            chosen = half_rows == (base + half).astype(BF16)
+            for r in range(0, 2 * rows, 2 * ROWS):
+                piece = left[r : r + 2 * ROWS]
+                masked.append(jnp.where(chosen, piece, jnp.zeros_like(piece)))
         sums = lax.dot_general(
             jnp.concatenate(masked, axis=0),
             hot,

time: 28.7 us -> 28.7 us (level)
  no operation moved by 1% of the time
where the time goes in v19:
time: 28.7 us; the launch traced here: 28.4 us
  blocking collectives  23.4 us (82%)
  Pallas kernels  4.11 us (14%)
  local copies, waits for them, and re-layouts  0.81 us (3%)
    all_to_all x1, blocking collectives, shards(): lax.all_to_all(outgoing, 'grid', split_axis=0, concat_axis=0, tiled=True)  13.9 us
    all_to_all x1, blocking collectives, shards(): lax.all_to_all(sums, ('bundle', 'grid'), split_axis=0, concat_axis=0, til...  9.54 us
    pallas_call x5, Pallas kernels, call(): pl.pallas_call(kernel, out_shape=[jax.ShapeDtypeStruct(shape, kind) for s...  4.11 us
    unnamed x18, local copies, waits for them, and re-layouts  0.81 us

profile of v19, /device:TPU:0, one launch (start us, length us, event | category | flops | bytes accessed | tf_op | source)
XLA Modules:
  0.0 28.4 jit_solution(12941324859545572178)
XLA Ops:
  0.0 0.0 copy-start.1
  0.0 0.0 copy-start.8
  0.0 0.0 copy-start.7
  0.0 0.0 copy-start
  0.0 0.7 %copy-done.1 = s32[4,1,8,32]{3,2,1,0:T(8,128)S(1)} copy-done((s32[4,1,8,32]{3,2,1,0:T(8,128)S(1)}, s32[4,1,8,32]{3,2,1,0:T(8,128)}, u32[]{:S(2)}) %copy-start.1) | copy-done | bytes 4120
  0.7 0.0 copy-done.8
  0.7 0.0 copy-done.7
  0.7 0.2 shard_map.92
  1.0 0.1 copy-done
  1.0 0.4 %shard_map.93 = f32[8,8,128]{2,1,0:T(8,128)S(1)} custom-call(f32[24,4096]{1,0:T(8,128)S(1)} %copy-done, s32[4,1,8,32]{3,2,1,0:T(8,128)S(1)} %copy-done.1, f32[8,128]{1,0:T(8,128)S(1)} %shard_map.91.first_ref, s32[8,256]{1,0:T(8,128)S(1)} %get-tuple-element.9.refs_0_, bf16[256,256]{1,0:T(8,128)(2,1)S(1)} %get-tuple-element.10.refs_1_), custom_call_target="tpu_custom_call" | custom-call | tf_op jit(solution)/shard_map/pallas_call | solution.py:553
  1.4 0.0 copy-start.3
  1.4 0.0 copy-start.4
  1.4 0.0 copy-start.5
  1.4 0.0 copy-start.6
  1.4 13.9 %all_to_all.10.table_ref = f32[8,8,128]{2,1,0:T(8,128)S(1)} all-to-all(f32[8,8,128]{2,1,0:T(8,128)S(1)} %shard_map.93), channel_id=1, replica_groups=mesh['grid'=8,'bundle'=4] {'grid'}, dimensions={0} | all-to-all | bytes 65536 | tf_op jit(solution)/shard_map/all_to_all | solution.py:598
  15.3 0.0 copy-done.3
  15.3 0.0 copy-done.4
  15.3 0.0 copy-done.5
  15.3 0.0 copy-done.6
  15.4 2.1 %shard_map.94 = f32[32,8,128]{2,1,0:T(8,128)S(1)} custom-call(f32[8,8,128]{2,1,0:T(8,128)S(1)} %all_to_all.10.table_ref, s32[32,128]{1,0:T(8,128)S(1)} %bitcast.17, s32[1,2]{1,0:T(1,128)S(1)} %copy-done.7, f32[32,128]{1,0:T(8,128)S(1)} %bitcast.18, f32[32,128]{1,0:T(8,128)S(1)} %bitcast.19, f32[1,24]{1,0:T(1,128)S(1)} %copy-done.8, f32[24,24]{1,0:T(8,128)S(1)} %copy-done.6), custom_call_target="tpu_custom_call" | custom-call | tf_op jit(solution)/shard_map/pallas_call | solution.py:553
  17.5 0.0 copy-start.2
  17.5 9.5 %all_to_all.11.sums_ref = f32[32,8,128]{2,1,0:T(8,128)S(1)} all-to-all(f32[32,8,128]{2,1,0:T(8,128)S(1)} %shard_map.94), channel_id=1, replica_groups=mesh['grid'=8,'bundle'=4] {'bundle','grid'}, dimensions={0} | all-to-all | bytes 262144 | tf_op jit(solution)/shard_map/all_to_all | solution.py:619
  27.0 0.0 copy-done.2
  27.0 1.4 %shard_map.95 = f32[24,4096]{1,0:T(8,128)} custom-call(f32[32,8,128]{2,1,0:T(8,128)S(1)} %all_to_all.11.sums_ref, s32[4,1,8,32]{3,2,1,0:T(8,128)S(1)} %copy-done.1, f32[1,4096]{1,0:T(1,128)S(1)} %bitcast.16, f32[24,4096]{1,0:T(8,128)S(1)} %copy-done, bf16[16,1024]{1,0:T(8,128)(2,1)S(1)} %get-tuple-element.11.refs_0_, ...), custom_call_target="tpu_custom_call" | custom-call | tf_op jit(solution)/shard_map/pallas_call | solution.py:553
  (1 shorter events, 0.0 us)
Async XLA Ops:
  0.0 0.7 %copy-start.1 = (s32[4,1,8,32]{3,2,1,0:T(8,128)S(1)}, s32[4,1,8,32]{3,2,1,0:T(8,128)}, u32[]{:S(2)}) copy-start(s32[4,1,8,32]{3,2,1,0:T(8,128)} %request_ref.5) | copy-start | bytes 12292
  0.0 0.7 %copy-start.8 = (f32[1,24]{1,0:T(1,128)S(1)}, f32[1,24]{1,0:T(1,128)}, u32[]{:S(2)}) copy-start(f32[1,24]{1,0:T(1,128)} %inflow_ref.3) | copy-start | bytes 292
  0.0 0.7 %copy-start.7 = (s32[1,2]{1,0:T(1,128)S(1)}, s32[1,2]{1,0:T(1,128)}, u32[]{:S(2)}) copy-start(s32[1,2]{1,0:T(1,128)} %length_ref.3) | copy-start | bytes 28
  0.0 1.0 %copy-start = (f32[24,4096]{1,0:T(8,128)S(1)}, f32[24,4096]{1,0:T(8,128)}, u32[]{:S(2)}) copy-start(f32[24,4096]{1,0:T(8,128)} %cell_ref.3) | copy-start | bytes 1179652
  1.4 13.9 %copy-start.3 = (s32[1,2,2048]{2,1,0:T(2,128)S(1)}, s32[1,2,2048]{2,1,0:T(2,128)}, u32[]{:S(2)}) copy-start(s32[1,2,2048]{2,1,0:T(2,128)} %param.12) | copy-start | bytes 49156
  1.4 13.9 %copy-start.4 = (f32[1,2,2048]{2,1,0:T(2,128)S(1)}, f32[1,2,2048]{2,1,0:T(2,128)}, u32[]{:S(2)}) copy-start(f32[1,2,2048]{2,1,0:T(2,128)} %param.14) | copy-start | bytes 49156
  1.4 13.9 %copy-start.5 = (f32[1,2,2048]{2,1,0:T(2,128)S(1)}, f32[1,2,2048]{2,1,0:T(2,128)}, u32[]{:S(2)}) copy-start(f32[1,2,2048]{2,1,0:T(2,128)} %param.15) | copy-start | bytes 49156
  1.4 13.9 %copy-start.6 = (f32[24,24]{1,0:T(8,128)S(1)}, f32[24,24]{1,0:T(8,128)}, u32[]{:S(2)}) copy-start(f32[24,24]{1,0:T(8,128)} %interaction_ref.1) | copy-start | bytes 6916
  17.5 9.6 %copy-start.2 = (f32[4096]{0:T(1024)S(1)}, f32[4096]{0:T(1024)}, u32[]{:S(2)}) copy-start(f32[4096]{0:T(1024)} %param.10) | copy-start | bytes 49156

commit v20 on v19

--- a/solution.py
+++ b/solution.py
@@ -15,6 +15,19 @@
 BF16 = jnp.bfloat16
 VMEM_BYTES = 32 * 1024 * 1024
 CHUNKS = 1
+
+
+def fast_size(owners):
+    return 2 if owners % 2 == 0 else 1
+
+
+def turned_place(owner, owners):
+    fast = fast_size(owners)
+    return owner % fast * (owners // fast) + owner // fast
+
+
+def grid_place():
+    return lax.axis_index("slow") * lax.axis_size("fast") + lax.axis_index("fast")
 
 
 def repeat_steps(count, body, carry):
@@ -122,7 +135,7 @@
     groups = LANES // cap
     chunks = owners // (2 * groups)
     highs = cells // LANES
-    here = lax.axis_index("grid")
+    here = grid_place()
     relative = lane_groups(cap, here)
     cell = cell_ref[...]
     stacked = jnp.concatenate(
@@ -154,7 +167,7 @@
                 relative,
             )
             for j in range(groups):
-                out_ref[first + half * groups + j] = tiles[j]
+                out_ref[turned_place(first + half * groups + j, owners)] = tiles[j]
         return carry
 
     repeat_steps(chunks, chunk, 0)
@@ -196,7 +209,7 @@
     times = LANES // segments
     chunk_owners = 2 * all_groups
     chunks = owners // chunk_owners
-    here, bundle = lax.axis_index("grid"), lax.axis_index("bundle")
+    here, bundle = grid_place(), lax.axis_index("bundle")
 
     slot = slot_ref[...]
     within = (slot + lax.rem(here, all_groups) * cap) % LANES
@@ -232,7 +245,7 @@
             halves.append(
                 jnp.concatenate(
                     unpack(
-                        [table_ref[first + j] for j in range(all_groups)], cap, relative, groups
+                        [table_ref[turned_place(first + j, owners)] for j in range(all_groups)], cap, relative, groups
                     ),
                     axis=0,
                 )
@@ -421,7 +434,7 @@
     bundles, cap = request_ref.shape[0], request_ref.shape[3]
     all_groups = LANES // cap
     width = 2 * LANES
-    here = lax.axis_index("grid")
+    here = grid_place()
     sublane = lax.broadcasted_iota(jnp.int32, (ROWS, LANES), 0)
     indices = []
     for t in range(bundles // all_groups):
@@ -470,7 +483,7 @@
     width = 2 * LANES
     highs = cells // width
     chunks = owners // ROWS
-    here = lax.axis_index("grid")
+    here = grid_place()
 
     def chunk(k, total):
         values, weights = [], []
@@ -595,7 +608,7 @@
         [((owners, ROWS, LANES), F32)],
         (cell_state, request_cell, first, *indices[:2]),
     )[0]
-    table = lax.all_to_all(outgoing, "grid", split_axis=0, concat_axis=0, tiled=True)
+    table = lax.all_to_all(outgoing, ("fast", "slow"), split_axis=0, concat_axis=0, tiled=True)
     lines, nodes = node_slot.shape[1:]
     blocks = nodes // LANES
 
@@ -616,7 +629,7 @@
         ),
         scratch=(pltpu.VMEM((5, lines * blocks, LANES), F32),),
     )[0]
-    back = lax.all_to_all(sums, ("bundle", "grid"), split_axis=0, concat_axis=0, tiled=True)
+    back = lax.all_to_all(sums, ("bundle", "slow", "fast"), split_axis=0, concat_axis=0, tiled=True)
     return call(
         functools.partial(blend_kernel, bundles),
         [(cell_state.shape, F32)],
@@ -627,21 +640,26 @@
 
 
 def solution(mesh):
+    owners, bundles = mesh.shape["grid"], mesh.shape["bundle"]
+    fast = fast_size(owners)
+    devices = mesh.devices.reshape(owners // fast, fast, bundles)
+    finer = jax.sharding.Mesh(devices, ("slow", "fast", "bundle"))
+    grid = ("slow", "fast")
     placed = (
-        P(None, "grid"),
-        P("grid"),
-        P(None, "grid", None, None),
-        P("bundle", "grid", None),
-        P("bundle", "grid"),
-        P("bundle", "grid", None),
-        P("bundle", "grid", None),
+        P(None, grid),
+        P(grid),
+        P(None, grid, None, None),
+        P("bundle", grid, None),
+        P("bundle", grid),
+        P("bundle", grid, None),
+        P("bundle", grid, None),
         P("bundle", None),
         P(),
     )
     return jax.shard_map(
-        functools.partial(shards, mesh.shape["bundle"]),
-        mesh=mesh,
+        functools.partial(shards, bundles),
+        mesh=finer,
         in_specs=placed,
-        out_specs=P(None, "grid"),
+        out_specs=P(None, grid),
         check_vma=False,
     )

time: 28.7 us -> 28.6 us (level)
  no operation moved by 1% of the time
where the time goes in v20:
time: 28.6 us; the launch traced here: 28.4 us
  blocking collectives  23.4 us (82%)
  Pallas kernels  4.13 us (14%)
  local copies, waits for them, and re-layouts  0.81 us (3%)
    all_to_all x1, blocking collectives, shards(): lax.all_to_all(outgoing, ('fast', 'slow'), split_axis=0, concat_axis=0, t...  13.9 us
    all_to_all x1, blocking collectives, shards(): lax.all_to_all(sums, ('bundle', 'slow', 'fast'), split_axis=0, concat_axi...  9.44 us
    pallas_call x5, Pallas kernels, call(): pl.pallas_call(kernel, out_shape=[jax.ShapeDtypeStruct(shape, kind) for s...  4.13 us
    unnamed x18, local copies, waits for them, and re-layouts  0.81 us

profile of v20, /device:TPU:0, one launch (start us, length us, event | category | flops | bytes accessed | tf_op | source)
XLA Modules:
  0.0 28.4 jit_solution(13477087947658584315)
XLA Ops:
  0.0 0.0 copy-start.1
  0.0 0.0 copy-start.8
  0.0 0.0 copy-start.7
  0.0 0.0 copy-start
  0.0 0.7 %copy-done.1 = s32[4,1,8,32]{3,2,1,0:T(8,128)S(1)} copy-done((s32[4,1,8,32]{3,2,1,0:T(8,128)S(1)}, s32[4,1,8,32]{3,2,1,0:T(8,128)}, u32[]{:S(2)}) %copy-start.1) | copy-done | bytes 4120
  0.7 0.0 copy-done.8
  0.7 0.0 copy-done.7
  0.7 0.2 shard_map.92
  1.0 0.1 copy-done
  1.0 0.4 %shard_map.93 = f32[8,8,128]{2,1,0:T(8,128)S(1)} custom-call(f32[24,4096]{1,0:T(8,128)S(1)} %copy-done, s32[4,1,8,32]{3,2,1,0:T(8,128)S(1)} %copy-done.1, f32[8,128]{1,0:T(8,128)S(1)} %shard_map.91.first_ref, s32[8,256]{1,0:T(8,128)S(1)} %get-tuple-element.9.refs_0_, bf16[256,256]{1,0:T(8,128)(2,1)S(1)} %get-tuple-element.10.refs_1_), custom_call_target="tpu_custom_call" | custom-call | tf_op jit(solution)/shard_map/pallas_call | solution.py:566
  1.4 0.0 copy-start.3
  1.4 0.0 copy-start.4
  1.4 0.0 copy-start.5
  1.4 0.0 copy-start.6
  1.4 13.9 %all_to_all.10.table_ref = f32[8,8,128]{2,1,0:T(8,128)S(1)} all-to-all(f32[8,8,128]{2,1,0:T(8,128)S(1)} %shard_map.93), channel_id=1, replica_groups=mesh['slow'=4,'fast'=2,'bundle'=4] {'fast','slow'}, dimensions={0} | all-to-all | bytes 65536 | tf_op jit(solution)/shard_map/all_to_all | solution.py:611
  15.4 0.0 copy-done.3
  15.4 0.0 copy-done.4
  15.4 0.0 copy-done.5
  15.4 0.0 copy-done.6
  15.4 2.1 %shard_map.94 = f32[32,8,128]{2,1,0:T(8,128)S(1)} custom-call(f32[8,8,128]{2,1,0:T(8,128)S(1)} %all_to_all.10.table_ref, s32[32,128]{1,0:T(8,128)S(1)} %bitcast.17, s32[1,2]{1,0:T(1,128)S(1)} %copy-done.7, f32[32,128]{1,0:T(8,128)S(1)} %bitcast.18, f32[32,128]{1,0:T(8,128)S(1)} %bitcast.19, f32[1,24]{1,0:T(1,128)S(1)} %copy-done.8, f32[24,24]{1,0:T(8,128)S(1)} %copy-done.6), custom_call_target="tpu_custom_call" | custom-call | tf_op jit(solution)/shard_map/pallas_call | solution.py:566
  17.5 0.0 copy-start.2
  17.5 9.4 %all_to_all.11.sums_ref = f32[32,8,128]{2,1,0:T(8,128)S(1)} all-to-all(f32[32,8,128]{2,1,0:T(8,128)S(1)} %shard_map.94), channel_id=1, replica_groups=mesh['slow'=4,'fast'=2,'bundle'=4] {'bundle','slow','fast'}, dimensions={0} | all-to-all | bytes 262144 | tf_op jit(solution)/shard_map/all_to_all | solution.py:632
  27.0 0.0 copy-done.2
  27.0 1.4 %shard_map.95 = f32[24,4096]{1,0:T(8,128)} custom-call(f32[32,8,128]{2,1,0:T(8,128)S(1)} %all_to_all.11.sums_ref, s32[4,1,8,32]{3,2,1,0:T(8,128)S(1)} %copy-done.1, f32[1,4096]{1,0:T(1,128)S(1)} %bitcast.16, f32[24,4096]{1,0:T(8,128)S(1)} %copy-done, bf16[16,1024]{1,0:T(8,128)(2,1)S(1)} %get-tuple-element.11.refs_0_, ...), custom_call_target="tpu_custom_call" | custom-call | tf_op jit(solution)/shard_map/pallas_call | solution.py:566
  (1 shorter events, 0.0 us)
Async XLA Ops:
  0.0 0.7 %copy-start.1 = (s32[4,1,8,32]{3,2,1,0:T(8,128)S(1)}, s32[4,1,8,32]{3,2,1,0:T(8,128)}, u32[]{:S(2)}) copy-start(s32[4,1,8,32]{3,2,1,0:T(8,128)} %request_ref.5) | copy-start | bytes 12292
  0.0 0.7 %copy-start.8 = (f32[1,24]{1,0:T(1,128)S(1)}, f32[1,24]{1,0:T(1,128)}, u32[]{:S(2)}) copy-start(f32[1,24]{1,0:T(1,128)} %inflow_ref.3) | copy-start | bytes 292
  0.0 0.7 %copy-start.7 = (s32[1,2]{1,0:T(1,128)S(1)}, s32[1,2]{1,0:T(1,128)}, u32[]{:S(2)}) copy-start(s32[1,2]{1,0:T(1,128)} %length_ref.3) | copy-start | bytes 28
  0.0 1.0 %copy-start = (f32[24,4096]{1,0:T(8,128)S(1)}, f32[24,4096]{1,0:T(8,128)}, u32[]{:S(2)}) copy-start(f32[24,4096]{1,0:T(8,128)} %cell_ref.3) | copy-start | bytes 1179652
  1.4 14.0 %copy-start.3 = (s32[1,2,2048]{2,1,0:T(2,128)S(1)}, s32[1,2,2048]{2,1,0:T(2,128)}, u32[]{:S(2)}) copy-start(s32[1,2,2048]{2,1,0:T(2,128)} %param.12) | copy-start | bytes 49156
  1.4 14.0 %copy-start.4 = (f32[1,2,2048]{2,1,0:T(2,128)S(1)}, f32[1,2,2048]{2,1,0:T(2,128)}, u32[]{:S(2)}) copy-start(f32[1,2,2048]{2,1,0:T(2,128)} %param.14) | copy-start | bytes 49156
  1.4 14.0 %copy-start.5 = (f32[1,2,2048]{2,1,0:T(2,128)S(1)}, f32[1,2,2048]{2,1,0:T(2,128)}, u32[]{:S(2)}) copy-start(f32[1,2,2048]{2,1,0:T(2,128)} %param.15) | copy-start | bytes 49156
  1.4 14.0 %copy-start.6 = (f32[24,24]{1,0:T(8,128)S(1)}, f32[24,24]{1,0:T(8,128)}, u32[]{:S(2)}) copy-start(f32[24,24]{1,0:T(8,128)} %interaction_ref.1) | copy-start | bytes 6916
  17.5 9.5 %copy-start.2 = (f32[4096]{0:T(1024)S(1)}, f32[4096]{0:T(1024)}, u32[]{:S(2)}) copy-start(f32[4096]{0:T(1024)} %param.10) | copy-start | bytes 49156

commit v21 on v20

--- a/solution.py
+++ b/solution.py
@@ -424,7 +424,7 @@
             for j in range(all_groups):
                 owner = k * chunk_owners + half * all_groups + j
                 for copy in range(copies):
-                    out_ref[copy * owners + owner] = tiles[j]
+                    out_ref[copy * owners + turned_place(owner, owners)] = tiles[j]
         return carry
 
     repeat_steps(chunks, scatter, 0)
@@ -491,7 +491,7 @@
             for d in range(ROWS):
                 found = unpack(
                     [
-                        sums_ref[(t * all_groups + j) * owners + k * ROWS + d]
+                        sums_ref[(t * all_groups + j) * owners + turned_place(k * ROWS + d, owners)]
                         for j in range(all_groups)
                     ],
                     cap,
@@ -629,7 +629,7 @@
         ),
         scratch=(pltpu.VMEM((5, lines * blocks, LANES), F32),),
     )[0]
-    back = lax.all_to_all(sums, ("bundle", "slow", "fast"), split_axis=0, concat_axis=0, tiled=True)
+    back = lax.all_to_all(sums, ("bundle", "fast", "slow"), split_axis=0, concat_axis=0, tiled=True)
     return call(
         functools.partial(blend_kernel, bundles),
         [(cell_state.shape, F32)],

time: 28.6 us -> 28.6 us (level)
  no operation moved by 1% of the time
where the time goes in v21:
time: 28.6 us; the launch traced here: 28.4 us
  blocking collectives  23.4 us (82%)
  Pallas kernels  4.12 us (14%)
  local copies, waits for them, and re-layouts  0.81 us (3%)
    all_to_all x1, blocking collectives, shards(): lax.all_to_all(outgoing, ('fast', 'slow'), split_axis=0, concat_axis=0, t...  13.9 us
    all_to_all x1, blocking collectives, shards(): lax.all_to_all(sums, ('bundle', 'fast', 'slow'), split_axis=0, concat_axi...  9.44 us
    pallas_call x5, Pallas kernels, call(): pl.pallas_call(kernel, out_shape=[jax.ShapeDtypeStruct(shape, kind) for s...  4.12 us
    unnamed x18, local copies, waits for them, and re-layouts  0.81 us

profile of v21, /device:TPU:0, one launch (start us, length us, event | category | flops | bytes accessed | tf_op | source)
XLA Modules:
  0.0 28.4 jit_solution(6401392572939719749)
XLA Ops:
  0.0 0.0 copy-start.1
  0.0 0.0 copy-start.8
  0.0 0.0 copy-start.7
  0.0 0.0 copy-start
  0.0 0.7 %copy-done.1 = s32[4,1,8,32]{3,2,1,0:T(8,128)S(1)} copy-done((s32[4,1,8,32]{3,2,1,0:T(8,128)S(1)}, s32[4,1,8,32]{3,2,1,0:T(8,128)}, u32[]{:S(2)}) %copy-start.1) | copy-done | bytes 4120
  0.7 0.0 copy-done.8
  0.7 0.0 copy-done.7
  0.7 0.2 shard_map.92
  1.0 0.1 copy-done
  1.0 0.4 %shard_map.93 = f32[8,8,128]{2,1,0:T(8,128)S(1)} custom-call(f32[24,4096]{1,0:T(8,128)S(1)} %copy-done, s32[4,1,8,32]{3,2,1,0:T(8,128)S(1)} %copy-done.1, f32[8,128]{1,0:T(8,128)S(1)} %shard_map.91.first_ref, s32[8,256]{1,0:T(8,128)S(1)} %get-tuple-element.9.refs_0_, bf16[256,256]{1,0:T(8,128)(2,1)S(1)} %get-tuple-element.10.refs_1_), custom_call_target="tpu_custom_call" | custom-call | tf_op jit(solution)/shard_map/pallas_call | solution.py:566
  1.4 0.0 copy-start.3
  1.4 0.0 copy-start.4
  1.4 0.0 copy-start.5
  1.4 0.0 copy-start.6
  1.4 13.9 %all_to_all.10.table_ref = f32[8,8,128]{2,1,0:T(8,128)S(1)} all-to-all(f32[8,8,128]{2,1,0:T(8,128)S(1)} %shard_map.93), channel_id=1, replica_groups=mesh['slow'=4,'fast'=2,'bundle'=4] {'fast','slow'}, dimensions={0} | all-to-all | bytes 65536 | tf_op jit(solution)/shard_map/all_to_all | solution.py:611
  15.4 0.0 copy-done.3
  15.4 0.0 copy-done.4
  15.4 0.0 copy-done.5
  15.4 0.0 copy-done.6
  15.4 2.1 %shard_map.94 = f32[32,8,128]{2,1,0:T(8,128)S(1)} custom-call(f32[8,8,128]{2,1,0:T(8,128)S(1)} %all_to_all.10.table_ref, s32[32,128]{1,0:T(8,128)S(1)} %bitcast.17, s32[1,2]{1,0:T(1,128)S(1)} %copy-done.7, f32[32,128]{1,0:T(8,128)S(1)} %bitcast.18, f32[32,128]{1,0:T(8,128)S(1)} %bitcast.19, f32[1,24]{1,0:T(1,128)S(1)} %copy-done.8, f32[24,24]{1,0:T(8,128)S(1)} %copy-done.6), custom_call_target="tpu_custom_call" | custom-call | tf_op jit(solution)/shard_map/pallas_call | solution.py:566
  17.5 0.0 copy-start.2
  17.5 9.4 %all_to_all.11.sums_ref = f32[32,8,128]{2,1,0:T(8,128)S(1)} all-to-all(f32[32,8,128]{2,1,0:T(8,128)S(1)} %shard_map.94), channel_id=1, replica_groups=mesh['slow'=4,'fast'=2,'bundle'=4] {'bundle','fast','slow'}, dimensions={0} | all-to-all | bytes 262144 | tf_op jit(solution)/shard_map/all_to_all | solution.py:632
  27.0 0.0 copy-done.2
  27.0 1.4 %shard_map.95 = f32[24,4096]{1,0:T(8,128)} custom-call(f32[32,8,128]{2,1,0:T(8,128)S(1)} %all_to_all.11.sums_ref, s32[4,1,8,32]{3,2,1,0:T(8,128)S(1)} %copy-done.1, f32[1,4096]{1,0:T(1,128)S(1)} %bitcast.16, f32[24,4096]{1,0:T(8,128)S(1)} %copy-done, bf16[16,1024]{1,0:T(8,128)(2,1)S(1)} %get-tuple-element.11.refs_0_, ...), custom_call_target="tpu_custom_call" | custom-call | tf_op jit(solution)/shard_map/pallas_call | solution.py:566
  (1 shorter events, 0.0 us)
Async XLA Ops:
  0.0 0.7 %copy-start.1 = (s32[4,1,8,32]{3,2,1,0:T(8,128)S(1)}, s32[4,1,8,32]{3,2,1,0:T(8,128)}, u32[]{:S(2)}) copy-start(s32[4,1,8,32]{3,2,1,0:T(8,128)} %request_ref.5) | copy-start | bytes 12292
  0.0 0.7 %copy-start.8 = (f32[1,24]{1,0:T(1,128)S(1)}, f32[1,24]{1,0:T(1,128)}, u32[]{:S(2)}) copy-start(f32[1,24]{1,0:T(1,128)} %inflow_ref.3) | copy-start | bytes 292
  0.0 0.7 %copy-start.7 = (s32[1,2]{1,0:T(1,128)S(1)}, s32[1,2]{1,0:T(1,128)}, u32[]{:S(2)}) copy-start(s32[1,2]{1,0:T(1,128)} %length_ref.3) | copy-start | bytes 28
  0.0 1.0 %copy-start = (f32[24,4096]{1,0:T(8,128)S(1)}, f32[24,4096]{1,0:T(8,128)}, u32[]{:S(2)}) copy-start(f32[24,4096]{1,0:T(8,128)} %cell_ref.3) | copy-start | bytes 1179652
  1.4 14.0 %copy-start.3 = (s32[1,2,2048]{2,1,0:T(2,128)S(1)}, s32[1,2,2048]{2,1,0:T(2,128)}, u32[]{:S(2)}) copy-start(s32[1,2,2048]{2,1,0:T(2,128)} %param.12) | copy-start | bytes 49156
  1.4 14.0 %copy-start.4 = (f32[1,2,2048]{2,1,0:T(2,128)S(1)}, f32[1,2,2048]{2,1,0:T(2,128)}, u32[]{:S(2)}) copy-start(f32[1,2,2048]{2,1,0:T(2,128)} %param.14) | copy-start | bytes 49156
  1.4 14.0 %copy-start.5 = (f32[1,2,2048]{2,1,0:T(2,128)S(1)}, f32[1,2,2048]{2,1,0:T(2,128)}, u32[]{:S(2)}) copy-start(f32[1,2,2048]{2,1,0:T(2,128)} %param.15) | copy-start | bytes 49156
  1.4 14.0 %copy-start.6 = (f32[24,24]{1,0:T(8,128)S(1)}, f32[24,24]{1,0:T(8,128)}, u32[]{:S(2)}) copy-start(f32[24,24]{1,0:T(8,128)} %interaction_ref.1) | copy-start | bytes 6916
  17.5 9.5 %copy-start.2 = (f32[4096]{0:T(1024)S(1)}, f32[4096]{0:T(1024)}, u32[]{:S(2)}) copy-start(f32[4096]{0:T(1024)} %param.10) | copy-start | bytes 49156
